TPU v7x, 32 devices: a whole 2x2x4 slice. The times are simulated.
32 devices in a mesh: groups: 2 (over y), tensor: 4 (over z), dp: 2 (over x), pipe: 2 (over core).
Axes of the slice: x: 2, y: 2, z: 4, core: 2. Of those that a mesh axis runs over, the one named last changes fastest.
Arguments:
- layer_input: bfloat16 [8192, 4096], P(('groups', 'dp'), 'tensor'), parts along dimension 0, may hold values from -6 to 6
- out_grads: bfloat16 [2, 8192, 14336], P('pipe', ('groups', 'dp'), 'tensor'), parts along dimension 1, may hold values from -6 to 6
- proj_in: bfloat16 [2, 4096, 64], P('pipe', 'tensor'), may hold values from -0.09375 to 0.09375
- proj_out: bfloat16 [2, 14336, 64], P('pipe', 'tensor'), may hold values from -0.046875 to 0.046875
- queries: float32 [2, 4096, 128], P('pipe', ('tensor', 'dp')), may hold values from -6 to 6
Outputs:
- hessian: float32 [2, 8192, 4096], P('pipe', ('groups', 'tensor', 'dp')), parts along dimension 1
- scores: float32 [8, 128], P('groups'), parts along dimension 0
There are 2 independent parts, one for each index of `groups`. A program takes and returns all parts, laid end to end along the dimension named above; an argument that names none is the same for every part. Nothing has to cross between parts.
All inputs are finite; a program needn't handle non-finite values.
Results may differ from a plain program's by a relative error of at most 0.0084.
Values may be sent and summed in bfloat16 or wider, within the bound.
No kernel may reach another device: no remote copies, remote signals or barrier semaphores. Data moves between devices by JAX's collectives and lax.ppermute only.
A program may use at most 128 MiB of HBM per device.

v0:
```python
import jax
import jax.numpy as jnp
from jax import lax
from jax.sharding import PartitionSpec as P

LEN = 1024
SEQ_DEV = 2
ITERS = 6


damping = 0.1


def shards(layer_input, out_grads, proj_in, proj_out, queries):
    highest = lax.Precision.HIGHEST
    rank = proj_in.shape[2]
    width = rank * rank
    dp_size = lax.axis_size("dp")
    tok_dev = layer_input.shape[0]
    owned = queries.shape[1]
    examples = SEQ_DEV * dp_size
    tensor_pos = lax.axis_index("tensor")
    dp_pos = lax.axis_index("dp")
    owner = tensor_pos * dp_size + dp_pos
    first_row = owner * owned
    x_part = jnp.dot(layer_input, proj_in[0], preferred_element_type=jnp.float32)
    g_part = jnp.dot(out_grads[0], proj_out[0], preferred_element_type=jnp.float32)
    partial_value = jnp.concatenate([x_part, g_part], axis=1)

    def sides(outer, mine):
        return (mine, outer)

    gram_shape = (owned, width)
    initial = (jnp.zeros(gram_shape, jnp.float32), jnp.zeros((examples, owned), jnp.float32))
    summed = lax.psum(partial_value, "tensor").astype(jnp.bfloat16)

    def label_summed(positions):
        return positions // LEN

    carry = initial
    piece = lax.all_gather(summed, "dp", axis=0, tiled=True)
    count = piece.shape[0]
    block = 512

    def one_block(totals, index):
        rows = lax.dynamic_slice_in_dim(piece, index * block, block, 0)
        outer = (rows[:, :rank][:, :, None] * rows[:, rank:][:, None, :]).reshape(block, width)
        mine = lax.dynamic_slice_in_dim(outer, first_row, owned, 1)
        left, right = sides(outer, mine)
        gram = totals[0] + lax.dot_general(
            left, right, (((0,), (0,)), ((), ())), preferred_element_type=jnp.float32
        )
        labels = label_summed(index * block + jnp.arange(block, dtype=jnp.int32))
        onehot = (labels[None, :] == jnp.arange(examples, dtype=jnp.int32)[:, None]).astype(
            jnp.bfloat16
        )
        sums = totals[1] + jnp.dot(onehot, mine, preferred_element_type=jnp.float32)
        return ((gram, sums), None)

    carry, _ = lax.scan(one_block, carry, jnp.arange(count // block, dtype=jnp.int32))
    gram, sums = carry
    tokens_all = tok_dev * dp_size
    identity = (
        jnp.arange(width, dtype=jnp.int32)[None, :]
        == first_row + jnp.arange(owned, dtype=jnp.int32)[:, None]
    ).astype(jnp.float32)
    grads = sums / LEN
    rhs = queries[0]
    hessian = gram / tokens_all + damping * identity

    def squares(field):
        return lax.psum(jnp.sum(field * field, axis=0), ("tensor", "dp"))

    solution = jnp.zeros_like(rhs)
    residual = rhs
    direction = rhs
    norm_now = squares(residual)
    for step in range(ITERS):
        image = jnp.dot(
            hessian,
            lax.all_gather(direction, ("tensor", "dp"), axis=0, tiled=True),
            precision=highest,
            preferred_element_type=jnp.float32,
        )
        alpha = norm_now / lax.psum(jnp.sum(direction * image, axis=0), ("tensor", "dp"))
        solution = solution + alpha * direction
        residual = residual - alpha * image
        norm_next = squares(residual)
        direction = residual + norm_next / norm_now * direction
        norm_now = norm_next
    local = jnp.dot(grads, solution, precision=highest, preferred_element_type=jnp.float32)
    scores = lax.psum(local, ("tensor", "dp", "pipe"))
    return (hessian[None], scores)


def solution(mesh):
    in_specs = (
        P(("groups", "dp"), "tensor"),
        P("pipe", ("groups", "dp"), "tensor"),
        P("pipe", "tensor", None),
        P("pipe", "tensor", None),
        P("pipe", ("tensor", "dp"), None),
    )
    out_specs = (P("pipe", ("groups", "tensor", "dp"), None), P("groups", None))
    return jax.shard_map(shards, mesh=mesh, in_specs=in_specs, out_specs=out_specs, check_vma=False)
```

profile of v0, /device:TPU:0, one launch (start us, length us, event | category | flops | bytes accessed | tf_op | source)
XLA Modules:
  0.0 763.5 jit_solution(18437454425302811004)
XLA Ops:
  7.2 3.6 fusion.29
  10.9 9.7 %fusion.8 = f32[2048,64]{0,1:T(8,128)S(1)} fusion(bf16[1,2048,3584]{2,1,0:T(8,128)(2,1)} %param.8, bf16[1,3584,64]{1,2,0:T(8,128)(2,1)S(1)} %copy-done), kind=kOutput, calls=%fused_computation.19 | convolution fusion | flops 939524096 | bytes 15663104 | tf_op jit(solution)/shard_map/dot_general | solution.py:27
  20.6 45.5 %all-reduce.2 = bf16[2048,128]{0,1:T(8,128)(2,1)} all-reduce(f32[2048,128]{0,1:T(8,128)S(1)} %pad_maximum_fusion), channel_id=1, replica_groups=mesh['groups'=2,'tensor'=4,'dp'=2,'pipe'=2] {'tensor'}, use_global_device_ids=true, to_apply=%region_0.0 | all-reduce | flops 262144 | bytes 1572864 | tf_op jit(solution)/shard_map/psum | solution.py:35
  67.0 19.8 %all-gather.9.cloned.1.call-done = bf16[4096,128]{0,1:T(8,128)(2,1)} async-done(((bf16[2048,128]{0,1:T(8,128)(2,1)}), bf16[4096,128]{0,1:T(8,128)(2,1)}) %all-gather.9.cloned.1.call-update) | async-done | bytes 1048592 | tf_op jit(solution)/shard_map/all_gather | solution.py:41
  86.9 127.0 %while.15 = (s32[]{:T(128)}, f32[512,4096]{1,0:T(8,128)}, f32[4,512]{1,0:T(4,128)S(1)}, s32[8]{0:T(128)S(1)}, bf16[4096,128]{0,1:T(8,128)(2,1)}, /*index=5*/s32[...) while((s32[]{:T(128)}, f32[512,4096]{1,0:T(8,128)}, ...), condition=%wide.region_2.3_spmd.clone, body=%wide.region_1.2_spmd.clone.sunk | while | flops 2155886592 | bytes 26629320 | solution.py:60
  88.1 0.9 constant_dynamic-slice_fusion.2
  89.0 2.3 broadcast_multiply_fusion.2
  91.3 8.0 %select_add_fusion.9 = f32[512,4096]{1,0:T(8,128)} fusion(f32[512,4096]{1,0:T(8,128)} %get-tuple-element.200, bf16[512,4096]{0,1:T(8,128)(2,1)} %bitcast.61, pred[]{:T(512)S(6)} %compare.14, s32[]{:T(128)} %get-tuple-element.215), kind=kOutput, calls=%fused_computation.clone.1 | convolution fusion | flops 2151677952 | bytes 21496320 | tf_op jit(solution)/shard_map/while/body/eval_jaxpr/dot_general | solution.py:50
  99.3 1.3 convolution_add_fusion.2
  101.8 0.9 constant_dynamic-slice_fusion.2
  102.7 2.3 broadcast_multiply_fusion.2
  105.0 10.5 %select_add_fusion.9 = f32[512,4096]{1,0:T(8,128)} fusion(f32[512,4096]{1,0:T(8,128)} %get-tuple-element.200, bf16[512,4096]{0,1:T(8,128)(2,1)} %bitcast.61, pred[]{:T(512)S(6)} %compare.14, s32[]{:T(128)} %get-tuple-element.215), kind=kOutput, calls=%fused_computation.clone.1 | convolution fusion | flops 2151677952 | bytes 21496320 | tf_op jit(solution)/shard_map/while/body/eval_jaxpr/dot_general | solution.py:50
  115.5 1.3 convolution_add_fusion.2
  118.1 0.9 constant_dynamic-slice_fusion.2
  119.0 2.3 broadcast_multiply_fusion.2
  121.3 10.5 %select_add_fusion.9 = f32[512,4096]{1,0:T(8,128)} fusion(f32[512,4096]{1,0:T(8,128)} %get-tuple-element.200, bf16[512,4096]{0,1:T(8,128)(2,1)} %bitcast.61, pred[]{:T(512)S(6)} %compare.14, s32[]{:T(128)} %get-tuple-element.215), kind=kOutput, calls=%fused_computation.clone.1 | convolution fusion | flops 2151677952 | bytes 21496320 | tf_op jit(solution)/shard_map/while/body/eval_jaxpr/dot_general | solution.py:50
  131.7 1.3 convolution_add_fusion.2
  134.3 0.9 constant_dynamic-slice_fusion.2
  135.2 2.3 broadcast_multiply_fusion.2
  137.5 10.4 %select_add_fusion.9 = f32[512,4096]{1,0:T(8,128)} fusion(f32[512,4096]{1,0:T(8,128)} %get-tuple-element.200, bf16[512,4096]{0,1:T(8,128)(2,1)} %bitcast.61, pred[]{:T(512)S(6)} %compare.14, s32[]{:T(128)} %get-tuple-element.215), kind=kOutput, calls=%fused_computation.clone.1 | convolution fusion | flops 2151677952 | bytes 21496320 | tf_op jit(solution)/shard_map/while/body/eval_jaxpr/dot_general | solution.py:50
  147.9 1.3 convolution_add_fusion.2
  150.4 0.9 constant_dynamic-slice_fusion.2
  151.3 2.3 broadcast_multiply_fusion.2
  153.6 10.4 %select_add_fusion.9 = f32[512,4096]{1,0:T(8,128)} fusion(f32[512,4096]{1,0:T(8,128)} %get-tuple-element.200, bf16[512,4096]{0,1:T(8,128)(2,1)} %bitcast.61, pred[]{:T(512)S(6)} %compare.14, s32[]{:T(128)} %get-tuple-element.215), kind=kOutput, calls=%fused_computation.clone.1 | convolution fusion | flops 2151677952 | bytes 21496320 | tf_op jit(solution)/shard_map/while/body/eval_jaxpr/dot_general | solution.py:50
  164.1 1.3 convolution_add_fusion.2
  166.6 0.9 constant_dynamic-slice_fusion.2
  167.5 2.3 broadcast_multiply_fusion.2
  169.8 10.4 %select_add_fusion.9 = f32[512,4096]{1,0:T(8,128)} fusion(f32[512,4096]{1,0:T(8,128)} %get-tuple-element.200, bf16[512,4096]{0,1:T(8,128)(2,1)} %bitcast.61, pred[]{:T(512)S(6)} %compare.14, s32[]{:T(128)} %get-tuple-element.215), kind=kOutput, calls=%fused_computation.clone.1 | convolution fusion | flops 2151677952 | bytes 21496320 | tf_op jit(solution)/shard_map/while/body/eval_jaxpr/dot_general | solution.py:50
  180.2 1.3 convolution_add_fusion.2
  182.8 0.9 constant_dynamic-slice_fusion.2
  183.7 2.3 broadcast_multiply_fusion.2
  186.0 10.4 %select_add_fusion.9 = f32[512,4096]{1,0:T(8,128)} fusion(f32[512,4096]{1,0:T(8,128)} %get-tuple-element.200, bf16[512,4096]{0,1:T(8,128)(2,1)} %bitcast.61, pred[]{:T(512)S(6)} %compare.14, s32[]{:T(128)} %get-tuple-element.215), kind=kOutput, calls=%fused_computation.clone.1 | convolution fusion | flops 2151677952 | bytes 21496320 | tf_op jit(solution)/shard_map/while/body/eval_jaxpr/dot_general | solution.py:50
  196.4 1.3 convolution_add_fusion.2
  199.0 0.9 constant_dynamic-slice_fusion.2
  199.8 2.3 broadcast_multiply_fusion.2
  202.1 10.4 %select_add_fusion.9 = f32[512,4096]{1,0:T(8,128)} fusion(f32[512,4096]{1,0:T(8,128)} %get-tuple-element.200, bf16[512,4096]{0,1:T(8,128)(2,1)} %bitcast.61, pred[]{:T(512)S(6)} %compare.14, s32[]{:T(128)} %get-tuple-element.215), kind=kOutput, calls=%fused_computation.clone.1 | convolution fusion | flops 2151677952 | bytes 21496320 | tf_op jit(solution)/shard_map/while/body/eval_jaxpr/dot_general | solution.py:50
  212.6 1.3 convolution_add_fusion.2
  213.9 11.1 %fusion.16 = (f32[128]{0:T(128)S(1)}, f32[128]{0:T(128)S(1)}, f32[512,128]{1,0:T(8,128)S(1)}) fusion(f32[1,512,128]{2,1,0:T(8,128)S(1)} %copy-done.1, f32[1,4096,128]{2,1,0:T(8,128)} %all-gather.21.cloned.1.call-done, f32[512,4096]{1,0:T(8,128)} %get-tuple-element.85, s32[512]{0:T(512)S(1)} %iota_add_fusion.1), kind=kOutput, calls=%fused_computation.36 | convolution fusion | flops 3229875968 | bytes 11013120 | tf_op jit(solution)/shard_map/dot_general | solution.py:79
  225.0 20.4 %all-reduce = (f32[128]{0:T(128)S(1)}, f32[128]{0:T(128)S(1)}) all-reduce(f32[128]{0:T(128)S(1)} %get-tuple-element.115, f32[128]{0:T(128)S(1)} %get-tuple-element.114), channel_id=1, replica_groups=mesh['groups'=2,'tensor'=4,'dp'=2,'pipe'=2] {'tensor','dp'}, use_global_device_ids=true, to_apply=%region_4.5 | all-reduce | flops 256 | bytes 2048 | tf_op jit(solution)/shard_map/psum | solution.py:72
  245.5 17.1 %psum.101 = f32[128]{0:T(128)S(1)} all-reduce(f32[128]{0:T(128)S(1)} %multiply_reduce_fusion.8), channel_id=1, replica_groups=mesh['groups'=2,'tensor'=4,'dp'=2,'pipe'=2] {'tensor','dp'}, use_global_device_ids=true, to_apply=%region_8.9 | all-reduce | flops 128 | bytes 1024 | tf_op jit(solution)/shard_map/psum | solution.py:72
  262.6 0.7 fusion.15
  263.6 47.9 %all-gather.11.cloned.1.call-done = f32[4096,128]{1,0:T(8,128)} async-done(((f32[512,128]{1,0:T(8,128)}), f32[4096,128]{1,0:T(8,128)}) %all-gather.11.cloned.1.call-update) | async-done | bytes 2097168 | tf_op jit(solution)/shard_map/all_gather | solution.py:81
  311.5 11.1 %multiply_reduce_fusion.7 = (f32[128]{0:T(128)S(1)}, f32[512,128]{1,0:T(8,128)S(1)}) fusion(f32[512,128]{1,0:T(8,128)} %fusion.15, f32[4096,128]{1,0:T(8,128)} %all-gather.11.cloned.1.call-done, f32[512,4096]{1,0:T(8,128)} %get-tuple-element.85, s32[512]{0:T(512)S(1)} %iota_add_fusion.1), kind=kOutput, calls=%fused_computation.63 | convolution fusion | flops 3229745152 | bytes 11012608 | tf_op jit(solution)/shard_map/dot_general | solution.py:79
  322.6 18.9 %psum.102 = f32[128]{0:T(128)S(1)} all-reduce(f32[128]{0:T(128)S(1)} %get-tuple-element.139), channel_id=1, replica_groups=mesh['groups'=2,'tensor'=4,'dp'=2,'pipe'=2] {'tensor','dp'}, use_global_device_ids=true, to_apply=%region_10.11 | all-reduce | flops 128 | bytes 1024 | tf_op jit(solution)/shard_map/psum | solution.py:85
  341.6 17.3 %psum.103 = f32[128]{0:T(128)S(1)} all-reduce(f32[128]{0:T(128)S(1)} %get-tuple-element.134), channel_id=1, replica_groups=mesh['groups'=2,'tensor'=4,'dp'=2,'pipe'=2] {'tensor','dp'}, use_global_device_ids=true, to_apply=%region_12.13 | all-reduce | flops 128 | bytes 1024 | tf_op jit(solution)/shard_map/psum | solution.py:72
  359.8 47.9 %all-gather.13.cloned.1.call-done = f32[4096,128]{1,0:T(8,128)} async-done(((f32[512,128]{1,0:T(8,128)}), f32[4096,128]{1,0:T(8,128)}) %all-gather.13.cloned.1.call-update) | async-done | bytes 2097168 | tf_op jit(solution)/shard_map/all_gather | solution.py:81
  407.7 11.1 %multiply_reduce_fusion.5 = (f32[128]{0:T(128)S(1)}, f32[512,128]{1,0:T(8,128)S(1)}) fusion(f32[512,128]{1,0:T(8,128)} %multiply_add_fusion.3, f32[4096,128]{1,0:T(8,128)} %all-gather.13.cloned.1.call-done, f32[512,4096]{1,0:T(8,128)} %get-tuple-element.85, s32[512]{0:T(512)S(1)} %iota_add_fusion.1), kind=kOutput, calls=%fused_computation.58 | convolution fusion | flops 3229745152 | bytes 11012608 | tf_op jit(solution)/shard_map/dot_general | solution.py:79
  418.8 18.9 %psum.104 = f32[128]{0:T(128)S(1)} all-reduce(f32[128]{0:T(128)S(1)} %get-tuple-element.141), channel_id=1, replica_groups=mesh['groups'=2,'tensor'=4,'dp'=2,'pipe'=2] {'tensor','dp'}, use_global_device_ids=true, to_apply=%region_14.15 | all-reduce | flops 128 | bytes 1024 | tf_op jit(solution)/shard_map/psum | solution.py:85
  437.8 17.3 %psum.105 = f32[128]{0:T(128)S(1)} all-reduce(f32[128]{0:T(128)S(1)} %get-tuple-element.132), channel_id=1, replica_groups=mesh['groups'=2,'tensor'=4,'dp'=2,'pipe'=2] {'tensor','dp'}, use_global_device_ids=true, to_apply=%region_16.17 | all-reduce | flops 128 | bytes 1024 | tf_op jit(solution)/shard_map/psum | solution.py:72
  455.2 0.7 multiply_add_fusion.2
  456.2 47.7 %all-gather.15.cloned.1.call-done = f32[4096,128]{1,0:T(8,128)} async-done(((f32[512,128]{1,0:T(8,128)}), f32[4096,128]{1,0:T(8,128)}) %all-gather.15.cloned.1.call-update) | async-done | bytes 2097168 | tf_op jit(solution)/shard_map/all_gather | solution.py:81
  503.9 11.1 %multiply_reduce_fusion.3 = (f32[128]{0:T(128)S(1)}, f32[512,128]{1,0:T(8,128)S(1)}) fusion(f32[512,128]{1,0:T(8,128)} %multiply_add_fusion.2, f32[4096,128]{1,0:T(8,128)} %all-gather.15.cloned.1.call-done, f32[512,4096]{1,0:T(8,128)} %get-tuple-element.85, s32[512]{0:T(512)S(1)} %iota_add_fusion.1), kind=kOutput, calls=%fused_computation.53 | convolution fusion | flops 3229745152 | bytes 11012608 | tf_op jit(solution)/shard_map/dot_general | solution.py:79
  515.0 18.9 %psum.106 = f32[128]{0:T(128)S(1)} all-reduce(f32[128]{0:T(128)S(1)} %get-tuple-element.143), channel_id=1, replica_groups=mesh['groups'=2,'tensor'=4,'dp'=2,'pipe'=2] {'tensor','dp'}, use_global_device_ids=true, to_apply=%region_18.19 | all-reduce | flops 128 | bytes 1024 | tf_op jit(solution)/shard_map/psum | solution.py:85
  534.0 17.3 %psum.107 = f32[128]{0:T(128)S(1)} all-reduce(f32[128]{0:T(128)S(1)} %get-tuple-element.130), channel_id=1, replica_groups=mesh['groups'=2,'tensor'=4,'dp'=2,'pipe'=2] {'tensor','dp'}, use_global_device_ids=true, to_apply=%region_20.21 | all-reduce | flops 128 | bytes 1024 | tf_op jit(solution)/shard_map/psum | solution.py:72
  552.2 47.9 %all-gather.17.cloned.1.call-done = f32[4096,128]{1,0:T(8,128)} async-done(((f32[512,128]{1,0:T(8,128)}), f32[4096,128]{1,0:T(8,128)}) %all-gather.17.cloned.1.call-update) | async-done | bytes 2097168 | tf_op jit(solution)/shard_map/all_gather | solution.py:81
  600.0 11.1 %multiply_reduce_fusion.1 = (f32[128]{0:T(128)S(1)}, f32[512,128]{1,0:T(8,128)S(1)}) fusion(f32[512,128]{1,0:T(8,128)} %multiply_add_fusion.1, f32[4096,128]{1,0:T(8,128)} %all-gather.17.cloned.1.call-done, f32[512,4096]{1,0:T(8,128)} %get-tuple-element.85, s32[512]{0:T(512)S(1)} %iota_add_fusion.1), kind=kOutput, calls=%fused_computation.48 | convolution fusion | flops 3229745152 | bytes 11012608 | tf_op jit(solution)/shard_map/dot_general | solution.py:79
  611.2 18.9 %psum.108 = f32[128]{0:T(128)S(1)} all-reduce(f32[128]{0:T(128)S(1)} %get-tuple-element.145), channel_id=1, replica_groups=mesh['groups'=2,'tensor'=4,'dp'=2,'pipe'=2] {'tensor','dp'}, use_global_device_ids=true, to_apply=%region_22.23 | all-reduce | flops 128 | bytes 1024 | tf_op jit(solution)/shard_map/psum | solution.py:85
  630.2 17.6 %psum.109 = f32[128]{0:T(128)S(1)} all-reduce(f32[128]{0:T(128)S(1)} %multiply_reduce_fusion), channel_id=1, replica_groups=mesh['groups'=2,'tensor'=4,'dp'=2,'pipe'=2] {'tensor','dp'}, use_global_device_ids=true, to_apply=%region_24.25 | all-reduce | flops 128 | bytes 1024 | tf_op jit(solution)/shard_map/psum | solution.py:72
  647.8 0.8 multiply_add_fusion
  648.6 8.9 %fusion.44 = f32[1,512,4096]{2,1,0:T(8,128)} fusion(s32[512]{0:T(512)S(1)} %iota_add_fusion.1, f32[512,4096]{1,0:T(8,128)} %get-tuple-element.85), kind=kLoop, calls=%fused_computation.81 | loop fusion | flops 8388608 | bytes 16779264 | tf_op jit(solution)/shard_map/broadcast_in_dim | solution.py:93
  657.5 39.1 %all-gather.19.cloned.1.call-done = f32[4096,128]{1,0:T(8,128)} async-done(((f32[512,128]{1,0:T(8,128)}), f32[4096,128]{1,0:T(8,128)}) %all-gather.19.cloned.1.call-update) | async-done | bytes 2097168 | tf_op jit(solution)/shard_map/all_gather | solution.py:81
  696.5 10.8 %fusion.12 = f32[128]{0:T(128)S(1)} fusion(f32[512,128]{1,0:T(8,128)S(1)} %copy-done.6, f32[4096,128]{1,0:T(8,128)} %all-gather.19.cloned.1.call-done, f32[512,4096]{1,0:T(8,128)} %get-tuple-element.85, s32[512]{0:T(512)S(1)} %iota_add_fusion.1), kind=kOutput, calls=%fused_computation.26 | convolution fusion | flops 3229745152 | bytes 10750464 | tf_op jit(solution)/shard_map/dot_general | solution.py:79
  707.3 18.9 %psum.110 = f32[128]{0:T(128)S(1)} all-reduce(f32[128]{0:T(128)S(1)} %fusion.12), channel_id=1, replica_groups=mesh['groups'=2,'tensor'=4,'dp'=2,'pipe'=2] {'tensor','dp'}, use_global_device_ids=true, to_apply=%region_26.27 | all-reduce | flops 128 | bytes 1024 | tf_op jit(solution)/shard_map/psum | solution.py:85
  726.6 30.1 %psum.111 = f32[4,128]{1,0:T(4,128)} all-reduce(f32[4,128]{1,0:T(4,128)S(1)} %fusion.22), channel_id=1, replica_groups=mesh['groups'=2,'tensor'=4,'dp'=2,'pipe'=2] {'tensor','dp','pipe'}, use_global_device_ids=true, to_apply=%region_27.28 | all-reduce | flops 512 | bytes 4096 | tf_op jit(solution)/shard_map/psum | solution.py:92
  (69 shorter events, 8.9 us)
Async XLA Ops:
  7.2 3.7 copy-start
  7.2 79.7 %all-gather.9.cloned.1.call-start = ((), (), s32[]{:S(2)}) async-start(), calls=%async_computation | async-start | bytes 1572864 | tf_op jit(solution)/shard_map/all_gather | solution.py:41
  66.2 147.7 %all-gather.21.cloned.1.call-start = ((), (), s32[]{:S(2)}) async-start(), calls=%async_computation.6 | async-start | bytes 2359296 | tf_op jit(solution)/shard_map/all_gather | solution.py:81
  66.9 244.6 %all-gather.11.cloned.1.call-start = ((), (), s32[]{:S(2)}) async-start(), calls=%async_computation.1 | async-start | bytes 2359296 | tf_op jit(solution)/shard_map/all_gather | solution.py:81
  86.9 127.0 %copy-start.1 = (f32[1,512,128]{2,1,0:T(8,128)S(1)}, f32[1,512,128]{2,1,0:T(8,128)}, u32[]{:S(2)}) copy-start(f32[1,512,128]{2,1,0:T(8,128)} %param.11) | copy-start | bytes 786436
  263.4 95.6 %copy-start.3 = (f32[512,128]{1,0:T(8,128)S(1)}, f32[512,128]{1,0:T(8,128)}, u32[]{:S(2)}) copy-start(f32[512,128]{1,0:T(8,128)} %fusion.15) | copy-start | bytes 786436
  263.4 144.3 %all-gather.13.cloned.1.call-start = ((), (), s32[]{:S(2)}) async-start(), calls=%async_computation.2 | async-start | bytes 2359296 | tf_op jit(solution)/shard_map/all_gather | solution.py:81
  359.7 95.4 %copy-start.4 = (f32[512,128]{1,0:T(8,128)S(1)}, f32[512,128]{1,0:T(8,128)}, u32[]{:S(2)}) copy-start(f32[512,128]{1,0:T(8,128)} %multiply_add_fusion.3) | copy-start | bytes 786436
  359.8 144.1 %all-gather.15.cloned.1.call-start = ((), (), s32[]{:S(2)}) async-start(), calls=%async_computation.3 | async-start | bytes 2359296 | tf_op jit(solution)/shard_map/all_gather | solution.py:81
  455.9 95.4 %copy-start.5 = (f32[512,128]{1,0:T(8,128)S(1)}, f32[512,128]{1,0:T(8,128)}, u32[]{:S(2)}) copy-start(f32[512,128]{1,0:T(8,128)} %multiply_add_fusion.2) | copy-start | bytes 786436
  455.9 144.1 %all-gather.17.cloned.1.call-start = ((), (), s32[]{:S(2)}) async-start(), calls=%async_computation.4 | async-start | bytes 2359296 | tf_op jit(solution)/shard_map/all_gather | solution.py:81
  552.1 95.7 %copy-start.2 = (f32[512,128]{1,0:T(8,128)S(1)}, f32[512,128]{1,0:T(8,128)}, u32[]{:S(2)}) copy-start(f32[512,128]{1,0:T(8,128)} %multiply_add_fusion.1) | copy-start | bytes 786436
  552.1 144.4 %all-gather.19.cloned.1.call-start = ((), (), s32[]{:S(2)}) async-start(), calls=%async_computation.5 | async-start | bytes 2359296 | tf_op jit(solution)/shard_map/all_gather | solution.py:81
  648.6 47.9 %copy-start.6 = (f32[512,128]{1,0:T(8,128)S(1)}, f32[512,128]{1,0:T(8,128)}, u32[]{:S(2)}) copy-start(f32[512,128]{1,0:T(8,128)} %multiply_add_fusion) | copy-start | bytes 786436
Sparse Core Ops, SparseCore 0:
  66.3 20.5 all-gather.8
  89.0 49.6 all-gather.20
  263.5 47.9 all-gather.10
  359.9 47.7 all-gather.12
  456.0 47.7 all-gather.14
  552.2 47.7 all-gather.16
  648.7 47.7 all-gather.18
where the time goes:
time: 765 us; the launch traced here: 763 us
  blocking collectives  277 us (36%)
  waiting for transfers between devices  251 us (33%)
  matrix products  171 us (22%)
  other arithmetic  31.6 us (4%)
  between operations  14.3 us (2%)
  local copies, waits for them, and re-layouts  12 us (2%)
    all_gather x6, waiting for transfers between devices, shards(): lax.all_gather(direction, ('tensor', 'dp'), axis=0, tiled=True)  230 us
    psum x6, blocking collectives, squares(): return lax.psum(jnp.sum(field * field, axis=0), ('tensor', 'dp'))  107 us
    psum x5, blocking collectives, shards(): lax.psum(jnp.sum(direction * image, axis=0), ('tensor', 'dp'))  94.6 us
    dot_general x8, matrix products, one_block(): lax.dot_general(left, right, (((0,), (0,)), ((), ())), preferred_element_...  81.1 us
    dot_general x6, matrix products, shards(): jnp.dot(hessian, lax.all_gather(direction, ('tensor', 'dp'), axis=0, tile...  66.3 us
    psum x1, blocking collectives, shards(): summed = lax.psum(partial_value, 'tensor').astype(jnp.bfloat16)  45.5 us
    psum x1, blocking collectives, shards(): scores = lax.psum(local, ('tensor', 'dp', 'pipe'))  30.1 us
    all_gather x1, waiting for transfers between devices, shards(): piece = lax.all_gather(summed, 'dp', axis=0, tiled=True)  19.8 us
  transfers between devices with their start and end apart: 7, of which 6 were waited for; matrix products, arithmetic and copies ran while one was open for 17% of the time, Pallas kernels for 0%

commit v1 on v0

v1 whole, which is shorter than its diff:
```python
import functools

import jax
import jax.numpy as jnp
from jax import lax
from jax.experimental import pallas as pl
from jax.experimental.pallas import tpu as pltpu
from jax.sharding import PartitionSpec as P

LEN = 1024
ITERS = 6
DAMPING = 0.1
NT = (((1,), (1,)), ((), ()))
VMEM_BYTES = 56 * 1024 * 1024


def whole_spec(shape):
    zeros = (0,) * len(shape)
    return pl.BlockSpec(shape, lambda *_: zeros)


def swap(value, axes, size, offset):
    return lax.ppermute(value, axes, [(i, i ^ offset) for i in range(size)])


def project_kernel(place, inputs, grads, proj_in, proj_out, *outs):
    step = pl.program_id(0)
    x = jnp.dot(inputs[...], proj_in[...], preferred_element_type=jnp.float32)
    g = jnp.dot(grads[...], proj_out[...], preferred_element_type=jnp.float32)
    both = jnp.concatenate([x, g], axis=1).T
    for k, out in enumerate(outs):

        @pl.when(step == k)
        def _():
            out[...] = both


def project(place, inputs, grads, proj_in, proj_out, chunk, block):
    parts = lax.axis_size("tensor")
    features, rank = proj_in.shape
    hidden = proj_out.shape[0]

    def rows(step, place):
        return (chunk * parts + lax.bitwise_xor(step, place[0]), 0)

    shape = (2 * rank, block)
    return pl.pallas_call(
        project_kernel,
        grid_spec=pltpu.PrefetchScalarGridSpec(
            num_scalar_prefetch=1,
            grid=(parts,),
            in_specs=[
                pl.BlockSpec((block, features), rows),
                pl.BlockSpec((block, hidden), rows),
                whole_spec(proj_in.shape),
                whole_spec(proj_out.shape),
            ],
            out_specs=[whole_spec(shape)] * parts,
        ),
        out_shape=[jax.ShapeDtypeStruct(shape, jnp.float32)] * parts,
        compiler_params=pltpu.CompilerParams(vmem_limit_bytes=VMEM_BYTES),
        cost_estimate=pl.CostEstimate(
            flops=2 * parts * block * (features + hidden) * rank,
            bytes_accessed=2 * parts * block * (features + hidden),
            transcendentals=0,
        ),
        name="project",
    )(place, inputs, grads, proj_in, proj_out)


def split_queries_kernel(place, queries, *rest):
    outs, turned = rest[:-1], rest[-1]
    cols, mine, rank = outs[0].shape
    for i in range(mine):
        turned[:, i, :] = queries[i * rank : (i + 1) * rank, :].T
    for k, out in enumerate(outs):
        out[...] = turned[pl.ds(lax.bitwise_xor(place[0], k) * cols, cols)]


def split_queries(place, queries, owners, rank):
    rows, total = queries.shape
    shape = (total // owners, rows // rank, rank)
    return pl.pallas_call(
        split_queries_kernel,
        in_specs=[pl.BlockSpec(memory_space=pltpu.SMEM), pl.BlockSpec(memory_space=pltpu.VMEM)],
        out_specs=[pl.BlockSpec(memory_space=pltpu.VMEM)] * owners,
        out_shape=[jax.ShapeDtypeStruct(shape, jnp.float32)] * owners,
        scratch_shapes=[pltpu.VMEM((total, rows // rank, rank), jnp.float32)],
        compiler_params=pltpu.CompilerParams(vmem_limit_bytes=VMEM_BYTES),
        name="split_queries",
    )(place, queries)


def solve_kernel(tokens, groups, nblocks, place, *refs):
    blocks = refs[:nblocks]
    rest = refs[nblocks:]
    x_s, g_s, pair, direction, residual, image, sums = rest[-7:]
    out = rest[-8]
    queries = rest[:-8]
    cols, side, rank = direction.shape
    mine = side // len(queries)
    block = x_s.shape[2]
    per_group = nblocks // groups
    for n in range(nblocks):
        x_s[n] = blocks[n][:rank, :].astype(jnp.float32)
        g = blocks[n][rank:, :]
        g_s[n] = jnp.concatenate([g, g], axis=0)
    for k, part in enumerate(queries):
        first = pl.multiple_of(lax.bitwise_xor(place[0], k) * mine, mine)
        direction[:, pl.ds(first, mine), :] = part[...]
    residual[...] = direction[...]

    def total(value):
        return jnp.sum(jnp.sum(value, axis=1, keepdims=True), axis=2, keepdims=True)

    def forward(n):
        w = jnp.dot(pair[...], g_s[n], preferred_element_type=jnp.float32)
        x = x_s[n][None]
        u = jnp.sum(w.reshape(cols, side, block) * x, axis=1, keepdims=True)
        sums[n // per_group] += jnp.sum(u, axis=2, keepdims=True)
        return u, x

    def prepare():
        d = direction[...]
        high = d.astype(jnp.bfloat16)
        low = (d - high.astype(jnp.float32)).astype(jnp.bfloat16)
        pair[...] = jnp.concatenate([high, low], axis=2).reshape(cols * side, 2 * rank)
        sums[...] = jnp.zeros_like(sums)
        return total(d * d)

    def step_size(norm, length, energy):
        return norm / (energy * (1.0 / tokens) + DAMPING * length)

    out[...] = jnp.zeros_like(out)

    def one_step(_, norm):
        length = prepare()
        image[...] = jnp.zeros_like(image)

        def one_block(n, energy):
            u, x = forward(n)
            spread = (u * x).astype(jnp.bfloat16).reshape(cols * side, block)
            image[...] += lax.dot_general(
                spread, g_s[n, :rank, :], NT, preferred_element_type=jnp.float32
            ).reshape(cols, side, rank)
            return energy + jnp.sum(u * u, axis=2, keepdims=True)

        energy = lax.fori_loop(0, nblocks, one_block, jnp.zeros_like(norm))
        alpha = step_size(norm, length, energy)
        out[...] += alpha[None] * sums[...]
        d = direction[...]
        r = residual[...] - alpha * (image[...] * (1.0 / tokens) + DAMPING * d)
        residual[...] = r
        later = total(r * r)
        direction[...] = r + later / norm * d
        return later

    norm = lax.fori_loop(0, ITERS - 1, one_step, total(residual[...] * residual[...]))
    length = prepare()

    def last_block(n, energy):
        u, _ = forward(n)
        return energy + jnp.sum(u * u, axis=2, keepdims=True)

    energy = lax.fori_loop(0, nblocks, last_block, jnp.zeros_like(norm))
    out[...] += step_size(norm, length, energy)[None] * sums[...]


def solve(place, blocks, queries, tokens, groups):
    cols, mine, rank = queries[0].shape
    side = mine * len(queries)
    block = blocks[0].shape[1]
    count = len(blocks)
    vectors = pltpu.VMEM((cols, side, rank), jnp.float32)
    return pl.pallas_call(
        functools.partial(solve_kernel, tokens, groups, count),
        in_specs=[pl.BlockSpec(memory_space=pltpu.SMEM)]
        + [pl.BlockSpec(memory_space=pltpu.VMEM)] * (count + len(queries)),
        out_specs=pl.BlockSpec(memory_space=pltpu.VMEM),
        out_shape=jax.ShapeDtypeStruct((groups, cols, 1, 128), jnp.float32),
        scratch_shapes=[
            pltpu.VMEM((count, rank, block), jnp.float32),
            pltpu.VMEM((count, 2 * rank, block), jnp.bfloat16),
            pltpu.VMEM((cols * side, 2 * rank), jnp.bfloat16),
            vectors,
            vectors,
            vectors,
            pltpu.VMEM((groups, cols, 1, 128), jnp.float32),
        ],
        compiler_params=pltpu.CompilerParams(vmem_limit_bytes=VMEM_BYTES),
        cost_estimate=pl.CostEstimate(
            flops=2 * 2 * ITERS * 4 * tokens * cols * side * rank,
            bytes_accessed=4 * tokens * rank,
            transcendentals=0,
        ),
        name="solve",
    )(place, *blocks, *queries)


def hessian_kernel(tokens, count, place, *refs):
    blocks = refs[:count]
    out, x_s, g_s, own, other = refs[count:]
    step = pl.program_id(0)
    rank = x_s.shape[0]
    block = blocks[0].shape[1]
    rows, columns = out.shape

    def vectors(i):
        return (x_s[pl.ds(i, 1), :] * g_s[...]).astype(jnp.bfloat16)

    @pl.when(step == 0)
    def _():
        for n in range(count):
            x_s[:, n * block : (n + 1) * block] = blocks[n][:rank, :].astype(jnp.float32)
            g_s[:, n * block : (n + 1) * block] = blocks[n][rank:, :].astype(jnp.float32)
        for i in range(rows // rank):
            own[i * rank : (i + 1) * rank, :] = vectors(place[0] * (rows // rank) + i)

    for j in range(columns // rank):
        other[j * rank : (j + 1) * rank, :] = vectors(step * (columns // rank) + j)
    gram = lax.dot_general(own[...], other[...], NT, preferred_element_type=jnp.float32)
    row = lax.broadcasted_iota(jnp.int32, (rows, columns), 0) + place[0] * rows
    column = lax.broadcasted_iota(jnp.int32, (rows, columns), 1) + step * columns
    out[...] = gram * (1.0 / tokens) + jnp.where(row == column, DAMPING, 0.0)


def hessian_rows(place, blocks, tokens, rows):
    rank, block = blocks[0].shape[0] // 2, blocks[0].shape[1]
    count = len(blocks)
    width = rank * rank
    columns = 256
    return pl.pallas_call(
        functools.partial(hessian_kernel, tokens, count),
        grid=(width // columns,),
        in_specs=[pl.BlockSpec(memory_space=pltpu.SMEM)]
        + [whole_spec(blocks[0].shape)] * count,
        out_specs=pl.BlockSpec((rows, columns), lambda step: (0, step)),
        out_shape=jax.ShapeDtypeStruct((rows, width), jnp.float32),
        scratch_shapes=[
            pltpu.VMEM((rank, count * block), jnp.float32),
            pltpu.VMEM((rank, count * block), jnp.float32),
            pltpu.VMEM((rows, count * block), jnp.bfloat16),
            pltpu.VMEM((columns, count * block), jnp.bfloat16),
        ],
        compiler_params=pltpu.CompilerParams(vmem_limit_bytes=VMEM_BYTES),
        cost_estimate=pl.CostEstimate(
            flops=2 * rows * width * tokens,
            bytes_accessed=4 * rows * width,
            transcendentals=0,
        ),
        name="hessian_rows",
    )(place, *blocks)


def shards(layer_input, out_grads, proj_in, proj_out, queries):
    rank = proj_in.shape[2]
    parts, dp_size, pipe_size = (lax.axis_size(a) for a in ("tensor", "dp", "pipe"))
    owners = parts * dp_size
    tok_dev = layer_input.shape[0]
    owned, nq = queries.shape[1:]
    tensor_pos = lax.axis_index("tensor").astype(jnp.int32)
    dp_pos = lax.axis_index("dp").astype(jnp.int32)
    owner = tensor_pos * dp_size + dp_pos
    tensor_place = tensor_pos.reshape(1)
    owner_place = owner.reshape(1)
    chunks = 2 if tok_dev // (2 * parts) >= 128 else 1
    block = tok_dev // (chunks * parts)
    tokens = tok_dev * dp_size

    mine = split_queries(owner_place, queries[0], owners, rank)
    columns = [mine[0]] + [swap(mine[k], ("tensor", "dp"), owners, k) for k in range(1, owners)]

    gathered = []
    for chunk in range(chunks):
        partial = project(
            tensor_place, layer_input, out_grads[0], proj_in[0], proj_out[0], chunk, block
        )
        summed = partial[0]
        for k in range(1, parts):
            summed = summed + swap(partial[k], "tensor", parts, k)
        summed = summed.astype(jnp.bfloat16)
        near = [summed] + [swap(summed, "tensor", parts, k) for k in range(1, parts)]
        gathered.append(near)
        for k in range(1, dp_size):
            gathered.append([swap(piece, "dp", dp_size, k) for piece in near])

    blocks = [piece for near in gathered for piece in near]
    groups = len(gathered) if tok_dev // chunks <= LEN else len(blocks)
    each = len(blocks) // groups
    sums = solve(owner_place, blocks, columns, tokens, groups)[:, :, 0, 0]

    example = []
    for g in range(groups):
        chunk, rest = divmod(g * each, dp_size * parts)
        apart, k = divmod(rest, parts)
        first = chunk * parts * block
        if each == 1:
            first = first + (tensor_pos ^ k) * block
        example.append((dp_pos ^ apart) * (tok_dev // LEN) + first // LEN)
    examples = dp_size * tok_dev // LEN
    onehot = jnp.stack(example)[None, :] == jnp.arange(examples, dtype=jnp.int32)[:, None]
    local = jnp.sum(jnp.where(onehot[:, :, None], sums[None], 0.0), axis=1) / LEN
    cols = nq // owners
    placed = lax.dynamic_update_slice(
        jnp.zeros((examples, nq), jnp.float32), local, (jnp.int32(0), owner * cols)
    )
    axes = ("tensor", "dp", "pipe")
    devices = owners * pipe_size
    if devices <= 16:
        scores = placed
        for k in range(1, devices):
            scores = scores + swap(placed, axes, devices, k)
    else:
        scores = lax.psum(placed, axes)
    hessian = hessian_rows(owner_place, blocks, tokens, owned)
    return (hessian[None], scores)


def solution(mesh):
    in_specs = (
        P(("groups", "dp"), "tensor"),
        P("pipe", ("groups", "dp"), "tensor"),
        P("pipe", "tensor", None),
        P("pipe", "tensor", None),
        P("pipe", ("tensor", "dp"), None),
    )
    out_specs = (P("pipe", ("groups", "tensor", "dp"), None), P("groups", None))
    return jax.shard_map(shards, mesh=mesh, in_specs=in_specs, out_specs=out_specs, check_vma=False)
```

time: 765 us -> 184 us (0.24)
  blocking collectives: 277 us -> 0 us
  waiting for transfers between devices: 251 us -> 18.1 us
  matrix products: 171 us -> 0 us
  Pallas kernels: 0 us -> 96.4 us
  starting transfers between devices: 0.69 us -> 60.2 us
  other arithmetic: 31.6 us -> 1.82 us
  between operations: 14.3 us -> 1.01 us
    psum x13 -> x0, blocking collectives: 277 us -> none  [the longest x6 107 us: squares(): return lax.psum(jnp.sum(field * field, axis=0), ('tensor', 'dp'))]
    all_gather x7 -> x0, waiting for transfers between devices: 250 us -> none  [the longest x6 230 us: shards(): lax.all_gather(direction, ('tensor', 'dp'), axis=0, tiled=True)]
    dot_general x25 -> x0, matrix products: 171 us -> none  [the longest x8 81.1 us: one_block(): lax.dot_general(left, right, (((0,), (0,)), ((), ())), preferred_element_...]
    pallas_call x0 -> x5, Pallas kernels: none -> 96.4 us  [the longest x1 54.7 us: solve(): pl.pallas_call(functools.partial(solve_kernel, tokens, groups, count), in...]
    ppermute x0 -> x42, starting transfers between devices: none -> 60.2 us  [swap(): return lax.ppermute(value, axes, [(i, i ^ offset) for i in range(size)])]
    mul x8 -> x0, other arithmetic: 18.3 us -> none  [one_block(): rows[:, :rank][:, :, None] * rows[:, rank:][:, None, :]]
    ppermute x0 -> x42, waiting for transfers between devices: none -> 18.1 us  [swap(): return lax.ppermute(value, axes, [(i, i ^ offset) for i in range(size)])]
    broadcast_in_dim x1 -> x0, other arithmetic: 8.87 us -> none  [shards(): return (hessian[None], scores)]
  transfers between devices with their start and end apart: 7 -> 42, of which waited for: 6 -> 11; matrix products, arithmetic and copies ran while one was open for 17% -> 1% of each run, Pallas kernels for 0% -> 19%
where the time goes in v1:
time: 184 us; the launch traced here: 183 us
  Pallas kernels  96.4 us (52%)
  starting transfers between devices  60.2 us (33%)
  waiting for transfers between devices  18.1 us (10%)
  local copies, waits for them, and re-layouts  5.73 us (3%)
    ppermute x42, starting transfers between devices, swap(): return lax.ppermute(value, axes, [(i, i ^ offset) for i in range(size)])  60.2 us
    pallas_call x1, Pallas kernels, solve(): pl.pallas_call(functools.partial(solve_kernel, tokens, groups, count), in...  54.7 us
    pallas_call x1, Pallas kernels, hessian_rows(): pl.pallas_call(functools.partial(hessian_kernel, tokens, count), grid=(wi...  24.8 us
    ppermute x42, waiting for transfers between devices, swap(): return lax.ppermute(value, axes, [(i, i ^ offset) for i in range(size)])  18.1 us
    pallas_call x2, Pallas kernels, project(): pl.pallas_call(project_kernel, grid_spec=pltpu.PrefetchScalarGridSpec(num...  14.8 us
    unnamed x56, local copies, waits for them, and re-layouts  4.55 us
  transfers between devices with their start and end apart: 42, of which 11 were waited for; matrix products, arithmetic and copies ran while one was open for 1% of the time, Pallas kernels for 19%

profile of v1, /device:TPU:0, one launch (start us, length us, event | category | flops | bytes accessed | tf_op | source)
XLA Modules:
  0.0 183.4 jit_solution(5309156320811200161)
XLA Ops:
  0.6 1.7 copy.11
  2.4 2.3 %copy.12 = bf16[1,3584,64]{2,1,0:T(8,128)(2,1)} copy(bf16[1,3584,64]{1,2,0:T(8,128)(2,1)} %param.8) | data formatting | bytes 917504 | tf_op args[3]
  4.6 7.4 %project.3 = (f32[128,256]{1,0:T(8,128)}, f32[128,256]{1,0:T(8,128)}, f32[128,256]{1,0:T(8,128)}, f32[128,256]{1,0:T(8,128)}) custom-call(s32[1]{0:T(128)} %bitcast.1.place, bf16[2048,1024]{1,0:T(8,128)(2,1)} %inputs.3, bf16[2048,3584]{1,0:T(8,128)(2,1)} %bitcast.11, bf16[1024,64]{1,0:T(8,128)(2,1)} %bitcast.15, bf16[3584,64]{1,0:T(8,128)(2,1)} %bitcast.13), custom_call_target="tpu_custom_call" | custom-call | flops 603979776 | bytes 9437184 | tf_op jit(solution)/shard_map/project/pallas_call | solution.py:47
  12.0 3.0 %collective-permute-start.10 = (f32[128,256]{1,0:T(8,128)}, f32[128,256]{1,0:T(8,128)S(1)}, u32[]{:S(2)}, u32[]{:S(2)}) collective-permute-start(f32[128,256]{1,0:T(8,128)} %get-tuple-element.23), channel_id=1, source_target_pairs={{0,4},{4,0},{8,12},{12,8},{1,5},{5,1},{9,13},{13,9},{2,6},{6,2},{1... | collective-permute-start | bytes 393224 | tf_op jit(solution)/shard_map/ppermute | solution.py:23
  15.1 2.6 %collective-permute-start.11 = (f32[128,256]{1,0:T(8,128)}, f32[128,256]{1,0:T(8,128)S(1)}, u32[]{:S(2)}, u32[]{:S(2)}) collective-permute-start(f32[128,256]{1,0:T(8,128)} %get-tuple-element.24), channel_id=1, source_target_pairs={{0,8},{4,12},{8,0},{12,4},{1,9},{5,13},{9,1},{13,5},{2,10},{6,14},... | collective-permute-start | bytes 393224 | tf_op jit(solution)/shard_map/ppermute | solution.py:23
  17.7 2.1 %split_queries.1 = (f32[16,8,64]{2,1,0:T(8,128)}, f32[16,8,64]{2,1,0:T(8,128)}, f32[16,8,64]{2,1,0:T(8,128)}, f32[16,8,64]{2,1,0:T(8,128)}, f32[16,8,64]{2,1,0:T...) custom-call(s32[1]{0:T(128)} %bitcast.place, f32[512,128]{1,0:T(8,128)} %bitcast.17), custom_call_target="tpu_custom_call" | custom-call | tf_op jit(solution)/shard_map/split_queries/pallas_call | solution.py:83
  19.8 1.7 collective-permute-start.20
  21.5 0.7 collective-permute-start.21
  22.2 2.1 %collective-permute-done.20.refs_17_ = f32[16,8,64]{2,1,0:T(8,128)S(1)} collective-permute-done((f32[16,8,64]{2,1,0:T(8,128)}, f32[16,8,64]{2,1,0:T(8,128)S(1)}, u32[]{:S(2)}, u32[]{:S(2)}) %collective-permute-start.20) | collective-permute-done | bytes 32800 | tf_op jit(solution)/shard_map/ppermute | solution.py:23
  24.3 1.8 collective-permute-start.22
  26.1 2.6 %collective-permute-done.21.refs_18_ = f32[16,8,64]{2,1,0:T(8,128)S(1)} collective-permute-done((f32[16,8,64]{2,1,0:T(8,128)}, f32[16,8,64]{2,1,0:T(8,128)S(1)}, u32[]{:S(2)}, u32[]{:S(2)}) %collective-permute-start.21) | collective-permute-done | bytes 32800 | tf_op jit(solution)/shard_map/ppermute | solution.py:23
  28.7 1.0 collective-permute-start.23
  29.7 7.4 %project.2 = (f32[128,256]{1,0:T(8,128)}, f32[128,256]{1,0:T(8,128)}, f32[128,256]{1,0:T(8,128)}, f32[128,256]{1,0:T(8,128)}) custom-call(s32[1]{0:T(128)} %bitcast.1.place, bf16[2048,1024]{1,0:T(8,128)(2,1)} %inputs.3, bf16[2048,3584]{1,0:T(8,128)(2,1)} %bitcast.12, bf16[1024,64]{1,0:T(8,128)(2,1)} %bitcast.16, bf16[3584,64]{1,0:T(8,128)(2,1)} %bitcast.14), custom_call_target="tpu_custom_call" | custom-call | flops 603979776 | bytes 9437184 | tf_op jit(solution)/shard_map/project/pallas_call | solution.py:47
  37.1 0.0 copy-start.5
  37.1 1.2 collective-permute-start.24
  38.3 4.2 %collective-permute-start.25 = (f32[16,8,64]{2,1,0:T(8,128)S(1)}, f32[16,8,64]{2,1,0:T(8,128)S(1)}, u32[]{:S(2)}, u32[]{:S(2)}) collective-permute-start(f32[16,8,64]{2,1,0:T(8,128)S(1)} %copy-done.25), channel_id=1, source_target_pairs={{0,12},{2,14},{4,8},{6,10},{8,4},{10,6},{12,0},{14,2},{1,13},{3,15... | collective-permute-start | bytes 98312 | tf_op jit(solution)/shard_map/ppermute | solution.py:23
  42.5 0.6 collective-permute-start.1
  43.1 3.7 %collective-permute-start.2 = (f32[128,256]{1,0:T(8,128)}, f32[128,256]{1,0:T(8,128)S(1)}, u32[]{:S(2)}, u32[]{:S(2)}) collective-permute-start(f32[128,256]{1,0:T(8,128)} %get-tuple-element.21), channel_id=1, source_target_pairs={{0,12},{4,8},{8,4},{12,0},{1,13},{5,9},{9,5},{13,1},{2,14},{6,10},... | collective-permute-start | bytes 393224 | tf_op jit(solution)/shard_map/ppermute | solution.py:23
  46.9 1.6 collective-permute-start.26
  48.5 0.1 collective-permute-start.16
  48.6 1.4 collective-permute-done
  50.0 2.3 %collective-permute-start.15 = (bf16[128,256]{1,0:T(8,128)(2,1)S(1)}, bf16[128,256]{1,0:T(8,128)(2,1)S(1)}, u32[]{:S(2)}, u32[]{:S(2)}) collective-permute-start(bf16[128,256]{1,0:T(8,128)(2,1)S(1)} %add_convert_fusion.refs_8_), channel_id=1, source_target_pairs={{0,12},{4,8},{8,4},{12,0},{1,13},{5,9},{9,5},{13,1},{2,14},{6,10},... | collective-permute-start | bytes 196616 | tf_op jit(solution)/shard_map/ppermute | solution.py:23
  52.3 5.8 %collective-permute-done.1 = f32[128,256]{1,0:T(8,128)S(1)} collective-permute-done((f32[128,256]{1,0:T(8,128)}, f32[128,256]{1,0:T(8,128)S(1)}, u32[]{:S(2)}, u32[]{:S(2)}) %collective-permute-start.1) | collective-permute-done | bytes 131104 | tf_op jit(solution)/shard_map/ppermute | solution.py:23
  58.1 3.4 %collective-permute-start.13 = (bf16[128,256]{1,0:T(8,128)(2,1)S(1)}, bf16[128,256]{1,0:T(8,128)(2,1)S(1)}, u32[]{:S(2)}, u32[]{:S(2)}) collective-permute-start(bf16[128,256]{1,0:T(8,128)(2,1)S(1)} %add_convert_fusion.refs_8_), channel_id=1, source_target_pairs={{0,4},{4,0},{8,12},{12,8},{1,5},{5,1},{9,13},{13,9},{2,6},{6,2},{1... | collective-permute-start | bytes 196616 | tf_op jit(solution)/shard_map/ppermute | solution.py:23
  61.5 0.9 add_convert_fusion.1.refs_0_
  62.4 1.0 collective-permute-start.6
  63.5 2.4 %collective-permute-start.5 = (bf16[128,256]{1,0:T(8,128)(2,1)S(1)}, bf16[128,256]{1,0:T(8,128)(2,1)S(1)}, u32[]{:S(2)}, u32[]{:S(2)}) collective-permute-start(bf16[128,256]{1,0:T(8,128)(2,1)S(1)} %add_convert_fusion.1.refs_0_), channel_id=1, source_target_pairs={{0,12},{4,8},{8,4},{12,0},{1,13},{5,9},{9,5},{13,1},{2,14},{6,10},... | collective-permute-start | bytes 196616 | tf_op jit(solution)/shard_map/ppermute | solution.py:23
  65.9 0.6 collective-permute-start.4
  66.5 1.4 collective-permute-start.3
  67.9 1.1 collective-permute-start.19
  68.9 0.1 pad_add_fusion
  69.0 1.0 collective-permute-start.18
  70.1 1.0 collective-permute-start.17
  71.1 0.5 collective-permute-done.4.refs_2_
  71.6 0.9 collective-permute-start.9
  72.6 1.1 collective-permute-start.8
  73.7 1.0 collective-permute-start.7
  74.6 0.6 collective-permute-done.17.refs_13_
  75.2 0.7 collective-permute-done.9.refs_7_
  75.9 0.9 collective-permute-done.8.refs_6_
  76.8 1.1 collective-permute-done.7.refs_5_
  78.1 0.4 copy-done.24
  78.6 54.7 %solve.1 = f32[4,16,1,128]{3,2,1,0:T(1,128)} custom-call(s32[1]{0:T(128)} %bitcast.place, bf16[128,256]{1,0:T(8,128)(2,1)} %copy-done.2, bf16[128,256]{1,0:T(8,128)(2,1)} %copy-done.16, bf16[128,256]{1,0:T(8,128)(2,1)} %copy-done.15, bf16[128,256]{1,0:T(8,128)(2,1)} %copy-done.14, bf16[128,256]{1,0:T(8,128)(2,1)} %copy-done.13, bf16[128,256]{1,0:T(8,128)(2,1)} %copy-done.24, ...), custom_call_target="tpu_custom_call" | custom-call | flops 25769803776 | bytes 1048576 | tf_op jit(solution)/shard_map/solve/pallas_call | solution.py:175
  133.3 1.0 slice_reduce_fusion
  134.2 0.1 select_reduce_fusion
  134.3 0.1 dynamic_update_slice.5
  134.5 0.1 collective-permute-start.41
  134.6 2.4 %collective-permute-start.40 = (f32[4,128]{1,0:T(4,128)S(1)}, f32[4,128]{1,0:T(4,128)S(1)}, u32[]{:S(2)}, u32[]{:S(2)}) collective-permute-start(f32[4,128]{1,0:T(4,128)S(1)} %dynamic_update_slice.5), channel_id=1, source_target_pairs={{0,14},{1,15},{2,12},{3,13},{4,10},{5,11},{6,8},{7,9},{8,6},{9,7},... | collective-permute-start | bytes 6152 | tf_op jit(solution)/shard_map/ppermute | solution.py:23
  137.0 3.6 %collective-permute-start.39 = (f32[4,128]{1,0:T(4,128)S(1)}, f32[4,128]{1,0:T(4,128)S(1)}, u32[]{:S(2)}, u32[]{:S(2)}) collective-permute-start(f32[4,128]{1,0:T(4,128)S(1)} %dynamic_update_slice.5), channel_id=1, source_target_pairs={{0,13},{1,12},{2,15},{3,14},{4,9},{5,8},{6,11},{7,10},{8,5},{9,4},... | collective-permute-start | bytes 6152 | tf_op jit(solution)/shard_map/ppermute | solution.py:23
  140.6 1.9 %collective-permute-start.38 = (f32[4,128]{1,0:T(4,128)S(1)}, f32[4,128]{1,0:T(4,128)S(1)}, u32[]{:S(2)}, u32[]{:S(2)}) collective-permute-start(f32[4,128]{1,0:T(4,128)S(1)} %dynamic_update_slice.5), channel_id=1, source_target_pairs={{0,12},{1,13},{2,14},{3,15},{4,8},{5,9},{6,10},{7,11},{8,4},{9,5},... | collective-permute-start | bytes 6152 | tf_op jit(solution)/shard_map/ppermute | solution.py:23
  142.5 1.7 collective-permute-start.36
  144.2 1.5 collective-permute-start.35
  145.7 3.0 %collective-permute-start.34 = (f32[4,128]{1,0:T(4,128)S(1)}, f32[4,128]{1,0:T(4,128)S(1)}, u32[]{:S(2)}, u32[]{:S(2)}) collective-permute-start(f32[4,128]{1,0:T(4,128)S(1)} %dynamic_update_slice.5), channel_id=1, source_target_pairs={{0,8},{1,9},{2,10},{3,11},{4,12},{5,13},{6,14},{7,15},{8,0},{9,1},... | collective-permute-start | bytes 6152 | tf_op jit(solution)/shard_map/ppermute | solution.py:23
  148.8 0.2 collective-permute-start.27
  149.0 24.8 %hessian_rows.1 = f32[512,4096]{1,0:T(8,128)} custom-call(s32[1]{0:T(128)} %bitcast.place, bf16[128,256]{1,0:T(8,128)(2,1)} %copy-done.2, bf16[128,256]{1,0:T(8,128)(2,1)} %copy-done.16, bf16[128,256]{1,0:T(8,128)(2,1)} %copy-done.15, bf16[128,256]{1,0:T(8,128)(2,1)} %copy-done.14, bf16[128,256]{1,0:T(8,128)(2,1)} %copy-done.13, ...), custom_call_target="tpu_custom_call" | custom-call | flops 17179869184 | bytes 8388608 | tf_op jit(solution)/shard_map/hessian_rows/pallas_call | solution.py:232
  173.8 2.9 %collective-permute-start.32 = (f32[4,128]{1,0:T(4,128)S(1)}, f32[4,128]{1,0:T(4,128)S(1)}, u32[]{:S(2)}, u32[]{:S(2)}) collective-permute-start(f32[4,128]{1,0:T(4,128)S(1)} %dynamic_update_slice.5), channel_id=1, source_target_pairs={{0,6},{1,7},{2,4},{3,5},{4,2},{5,3},{6,0},{7,1},{8,14},{9,15},{10,... | collective-permute-start | bytes 6152 | tf_op jit(solution)/shard_map/ppermute | solution.py:23
  176.7 1.4 collective-permute-start.30
  178.1 1.1 collective-permute-start.29
  179.2 1.0 collective-permute-start.28
  180.2 0.1 dynamic-slice_add_fusion
  180.3 0.1 add.86
  180.4 0.7 collective-permute-done.29
  181.1 1.7 collective-permute-done.28
  182.8 0.6 add_add_fusion
  (93 shorter events, 0.2 us)
Async XLA Ops:
  12.0 30.4 %collective-permute-start.10 = (f32[128,256]{1,0:T(8,128)}, f32[128,256]{1,0:T(8,128)S(1)}, u32[]{:S(2)}, u32[]{:S(2)}) collective-permute-start(f32[128,256]{1,0:T(8,128)} %get-tuple-element.23), channel_id=1, source_target_pairs={{0,4},{4,0},{8,12},{12,8},{1,5},{5,1},{9,13},{13,9},{2,6},{6,2},{1... | collective-permute-start | bytes 393224 | tf_op jit(solution)/shard_map/ppermute | solution.py:23
  15.1 27.4 %collective-permute-start.11 = (f32[128,256]{1,0:T(8,128)}, f32[128,256]{1,0:T(8,128)S(1)}, u32[]{:S(2)}, u32[]{:S(2)}) collective-permute-start(f32[128,256]{1,0:T(8,128)} %get-tuple-element.24), channel_id=1, source_target_pairs={{0,8},{4,12},{8,0},{12,4},{1,9},{5,13},{9,1},{13,5},{2,10},{6,14},... | collective-permute-start | bytes 393224 | tf_op jit(solution)/shard_map/ppermute | solution.py:23
  17.7 25.5 %collective-permute-start.12 = (f32[128,256]{1,0:T(8,128)}, f32[128,256]{1,0:T(8,128)S(1)}, u32[]{:S(2)}, u32[]{:S(2)}) collective-permute-start(f32[128,256]{1,0:T(8,128)} %get-tuple-element.25), channel_id=1, source_target_pairs={{0,12},{4,8},{8,4},{12,0},{1,13},{5,9},{9,5},{13,1},{2,14},{6,10},... | collective-permute-start | bytes 393224 | tf_op jit(solution)/shard_map/ppermute | solution.py:23
  19.8 4.5 %collective-permute-start.20 = (f32[16,8,64]{2,1,0:T(8,128)}, f32[16,8,64]{2,1,0:T(8,128)S(1)}, u32[]{:S(2)}, u32[]{:S(2)}) collective-permute-start(f32[16,8,64]{2,1,0:T(8,128)} %get-tuple-element.27), channel_id=1, source_target_pairs={{0,2},{2,0},{4,6},{6,4},{8,10},{10,8},{12,14},{14,12},{1,3},{3,1},... | collective-permute-start | bytes 98312 | tf_op jit(solution)/shard_map/ppermute | solution.py:23
  21.5 7.2 %collective-permute-start.21 = (f32[16,8,64]{2,1,0:T(8,128)}, f32[16,8,64]{2,1,0:T(8,128)S(1)}, u32[]{:S(2)}, u32[]{:S(2)}) collective-permute-start(f32[16,8,64]{2,1,0:T(8,128)} %get-tuple-element.28), channel_id=1, source_target_pairs={{0,4},{2,6},{4,0},{6,2},{8,12},{10,14},{12,8},{14,10},{1,5},{3,7},... | collective-permute-start | bytes 98312 | tf_op jit(solution)/shard_map/ppermute | solution.py:23
  24.3 12.8 %copy-start.3 = (f32[16,8,64]{2,1,0:T(8,128)}, f32[16,8,64]{2,1,0:T(8,128)S(1)}, u32[]{:S(2)}) copy-start(f32[16,8,64]{2,1,0:T(8,128)S(1)} %collective-permute-done.20.refs_17_) | copy-start | bytes 98308
  24.3 12.8 %collective-permute-start.22 = (f32[16,8,64]{2,1,0:T(8,128)}, f32[16,8,64]{2,1,0:T(8,128)S(1)}, u32[]{:S(2)}, u32[]{:S(2)}) collective-permute-start(f32[16,8,64]{2,1,0:T(8,128)} %get-tuple-element.29), channel_id=1, source_target_pairs={{0,6},{2,4},{4,2},{6,0},{8,14},{10,12},{12,10},{14,8},{1,7},{3,5},... | collective-permute-start | bytes 98312 | tf_op jit(solution)/shard_map/ppermute | solution.py:23
  28.6 8.4 %copy-start.4 = (f32[16,8,64]{2,1,0:T(8,128)}, f32[16,8,64]{2,1,0:T(8,128)S(1)}, u32[]{:S(2)}) copy-start(f32[16,8,64]{2,1,0:T(8,128)S(1)} %collective-permute-done.21.refs_18_) | copy-start | bytes 98308
  28.6 8.4 %copy-start.26 = (f32[16,8,64]{2,1,0:T(8,128)S(1)}, f32[16,8,64]{2,1,0:T(8,128)}, u32[]{:S(2)}) copy-start(f32[16,8,64]{2,1,0:T(8,128)} %get-tuple-element.31) | copy-start | bytes 98308
  28.7 9.6 %copy-start.25 = (f32[16,8,64]{2,1,0:T(8,128)S(1)}, f32[16,8,64]{2,1,0:T(8,128)}, u32[]{:S(2)}) copy-start(f32[16,8,64]{2,1,0:T(8,128)} %get-tuple-element.32) | copy-start | bytes 98308
  28.7 18.2 %copy-start = (f32[128,256]{1,0:T(8,128)S(1)}, f32[128,256]{1,0:T(8,128)}, u32[]{:S(2)}) copy-start(f32[128,256]{1,0:T(8,128)} %get-tuple-element.22) | copy-start | bytes 393220
  28.7 18.3 %copy-start.21 = (f32[16,8,64]{2,1,0:T(8,128)S(1)}, f32[16,8,64]{2,1,0:T(8,128)}, u32[]{:S(2)}) copy-start(f32[16,8,64]{2,1,0:T(8,128)} %get-tuple-element.33) | copy-start | bytes 98308
  28.7 9.6 %collective-permute-start.23 = (f32[16,8,64]{2,1,0:T(8,128)}, f32[16,8,64]{2,1,0:T(8,128)S(1)}, u32[]{:S(2)}, u32[]{:S(2)}) collective-permute-start(f32[16,8,64]{2,1,0:T(8,128)} %get-tuple-element.30), channel_id=1, source_target_pairs={{0,8},{2,10},{4,12},{6,14},{8,0},{10,2},{12,4},{14,6},{1,9},{3,11}... | collective-permute-start | bytes 98312 | tf_op jit(solution)/shard_map/ppermute | solution.py:23
  37.1 40.8 %copy-start.5 = (f32[16,8,64]{2,1,0:T(8,128)}, f32[16,8,64]{2,1,0:T(8,128)S(1)}, u32[]{:S(2)}) copy-start(f32[16,8,64]{2,1,0:T(8,128)S(1)} %collective-permute-done.22.refs_19_) | copy-start | bytes 98308
  37.1 9.8 %collective-permute-start.24 = (f32[16,8,64]{2,1,0:T(8,128)S(1)}, f32[16,8,64]{2,1,0:T(8,128)S(1)}, u32[]{:S(2)}, u32[]{:S(2)}) collective-permute-start(f32[16,8,64]{2,1,0:T(8,128)S(1)} %copy-done.26), channel_id=1, source_target_pairs={{0,10},{2,8},{4,14},{6,12},{8,2},{10,0},{12,6},{14,4},{1,11},{3,9}... | collective-permute-start | bytes 98312 | tf_op jit(solution)/shard_map/ppermute | solution.py:23
  38.3 39.6 %copy-start.7 = (f32[16,8,64]{2,1,0:T(8,128)}, f32[16,8,64]{2,1,0:T(8,128)S(1)}, u32[]{:S(2)}) copy-start(f32[16,8,64]{2,1,0:T(8,128)S(1)} %collective-permute-done.23.refs_20_) | copy-start | bytes 98308
  38.3 10.2 %collective-permute-start.25 = (f32[16,8,64]{2,1,0:T(8,128)S(1)}, f32[16,8,64]{2,1,0:T(8,128)S(1)}, u32[]{:S(2)}, u32[]{:S(2)}) collective-permute-start(f32[16,8,64]{2,1,0:T(8,128)S(1)} %copy-done.25), channel_id=1, source_target_pairs={{0,12},{2,14},{4,8},{6,10},{8,4},{10,6},{12,0},{14,2},{1,13},{3,15... | collective-permute-start | bytes 98312 | tf_op jit(solution)/shard_map/ppermute | solution.py:23
  42.5 7.5 %collective-permute-start = (f32[128,256]{1,0:T(8,128)}, f32[128,256]{1,0:T(8,128)S(1)}, u32[]{:S(2)}, u32[]{:S(2)}) collective-permute-start(f32[128,256]{1,0:T(8,128)} %get-tuple-element.19), channel_id=1, source_target_pairs={{0,4},{4,0},{8,12},{12,8},{1,5},{5,1},{9,13},{13,9},{2,6},{6,2},{1... | collective-permute-start | bytes 393224 | tf_op jit(solution)/shard_map/ppermute | solution.py:23
  42.5 15.6 %collective-permute-start.1 = (f32[128,256]{1,0:T(8,128)}, f32[128,256]{1,0:T(8,128)S(1)}, u32[]{:S(2)}, u32[]{:S(2)}) collective-permute-start(f32[128,256]{1,0:T(8,128)} %get-tuple-element.20), channel_id=1, source_target_pairs={{0,8},{4,12},{8,0},{12,4},{1,9},{5,13},{9,1},{13,5},{2,10},{6,14},... | collective-permute-start | bytes 393224 | tf_op jit(solution)/shard_map/ppermute | solution.py:23
  43.1 15.0 %collective-permute-start.2 = (f32[128,256]{1,0:T(8,128)}, f32[128,256]{1,0:T(8,128)S(1)}, u32[]{:S(2)}, u32[]{:S(2)}) collective-permute-start(f32[128,256]{1,0:T(8,128)} %get-tuple-element.21), channel_id=1, source_target_pairs={{0,12},{4,8},{8,4},{12,0},{1,13},{5,9},{9,5},{13,1},{2,14},{6,10},... | collective-permute-start | bytes 393224 | tf_op jit(solution)/shard_map/ppermute | solution.py:23
  46.9 31.0 %copy-start.1 = (bf16[128,256]{1,0:T(8,128)(2,1)}, bf16[128,256]{1,0:T(8,128)(2,1)S(1)}, u32[]{:S(2)}) copy-start(bf16[128,256]{1,0:T(8,128)(2,1)S(1)} %add_convert_fusion.refs_8_) | copy-start | bytes 196612
  46.9 31.0 %copy-start.10 = (f32[16,8,64]{2,1,0:T(8,128)}, f32[16,8,64]{2,1,0:T(8,128)S(1)}, u32[]{:S(2)}) copy-start(f32[16,8,64]{2,1,0:T(8,128)S(1)} %collective-permute-done.24.refs_21_) | copy-start | bytes 98308
  46.9 15.5 %collective-permute-start.26 = (f32[16,8,64]{2,1,0:T(8,128)S(1)}, f32[16,8,64]{2,1,0:T(8,128)S(1)}, u32[]{:S(2)}, u32[]{:S(2)}) collective-permute-start(f32[16,8,64]{2,1,0:T(8,128)S(1)} %copy-done.21), channel_id=1, source_target_pairs={{0,14},{2,12},{4,10},{6,8},{8,6},{10,4},{12,2},{14,0},{1,15},{3,13... | collective-permute-start | bytes 98312 | tf_op jit(solution)/shard_map/ppermute | solution.py:23
  48.5 29.4 %copy-start.12 = (f32[16,8,64]{2,1,0:T(8,128)}, f32[16,8,64]{2,1,0:T(8,128)S(1)}, u32[]{:S(2)}) copy-start(f32[16,8,64]{2,1,0:T(8,128)S(1)} %collective-permute-done.25.refs_22_) | copy-start | bytes 98308
  48.5 15.0 %collective-permute-start.16 = (bf16[128,256]{1,0:T(8,128)(2,1)S(1)}, bf16[128,256]{1,0:T(8,128)(2,1)S(1)}, u32[]{:S(2)}, u32[]{:S(2)}) collective-permute-start(bf16[128,256]{1,0:T(8,128)(2,1)S(1)} %add_convert_fusion.refs_8_), channel_id=1, source_target_pairs={{0,2},{2,0},{1,3},{3,1},{4,6},{6,4},{5,7},{7,5},{8,10},{10,8},{9,1... | collective-permute-start | bytes 196616 | tf_op jit(solution)/shard_map/ppermute | solution.py:23
  50.0 15.9 %collective-permute-start.15 = (bf16[128,256]{1,0:T(8,128)(2,1)S(1)}, bf16[128,256]{1,0:T(8,128)(2,1)S(1)}, u32[]{:S(2)}, u32[]{:S(2)}) collective-permute-start(bf16[128,256]{1,0:T(8,128)(2,1)S(1)} %add_convert_fusion.refs_8_), channel_id=1, source_target_pairs={{0,12},{4,8},{8,4},{12,0},{1,13},{5,9},{9,5},{13,1},{2,14},{6,10},... | collective-permute-start | bytes 196616 | tf_op jit(solution)/shard_map/ppermute | solution.py:23
  58.1 8.4 %collective-permute-start.14 = (bf16[128,256]{1,0:T(8,128)(2,1)S(1)}, bf16[128,256]{1,0:T(8,128)(2,1)S(1)}, u32[]{:S(2)}, u32[]{:S(2)}) collective-permute-start(bf16[128,256]{1,0:T(8,128)(2,1)S(1)} %add_convert_fusion.refs_8_), channel_id=1, source_target_pairs={{0,8},{4,12},{8,0},{12,4},{1,9},{5,13},{9,1},{13,5},{2,10},{6,14},... | collective-permute-start | bytes 196616 | tf_op jit(solution)/shard_map/ppermute | solution.py:23
  58.1 9.8 %collective-permute-start.13 = (bf16[128,256]{1,0:T(8,128)(2,1)S(1)}, bf16[128,256]{1,0:T(8,128)(2,1)S(1)}, u32[]{:S(2)}, u32[]{:S(2)}) collective-permute-start(bf16[128,256]{1,0:T(8,128)(2,1)S(1)} %add_convert_fusion.refs_8_), channel_id=1, source_target_pairs={{0,4},{4,0},{8,12},{12,8},{1,5},{5,1},{9,13},{13,9},{2,6},{6,2},{1... | collective-permute-start | bytes 196616 | tf_op jit(solution)/shard_map/ppermute | solution.py:23
  62.4 15.6 %copy-start.2 = (bf16[128,256]{1,0:T(8,128)(2,1)}, bf16[128,256]{1,0:T(8,128)(2,1)S(1)}, u32[]{:S(2)}) copy-start(bf16[128,256]{1,0:T(8,128)(2,1)S(1)} %add_convert_fusion.1.refs_0_) | copy-start | bytes 196612
  62.4 15.5 %copy-start.18 = (f32[16,8,64]{2,1,0:T(8,128)}, f32[16,8,64]{2,1,0:T(8,128)S(1)}, u32[]{:S(2)}) copy-start(f32[16,8,64]{2,1,0:T(8,128)S(1)} %collective-permute-done.26.refs_23_) | copy-start | bytes 98308
  62.4 6.6 %collective-permute-start.6 = (bf16[128,256]{1,0:T(8,128)(2,1)S(1)}, bf16[128,256]{1,0:T(8,128)(2,1)S(1)}, u32[]{:S(2)}, u32[]{:S(2)}) collective-permute-start(bf16[128,256]{1,0:T(8,128)(2,1)S(1)} %add_convert_fusion.1.refs_0_), channel_id=1, source_target_pairs={{0,2},{2,0},{1,3},{3,1},{4,6},{6,4},{5,7},{7,5},{8,10},{10,8},{9,1... | collective-permute-start | bytes 196616 | tf_op jit(solution)/shard_map/ppermute | solution.py:23
  63.5 14.5 %copy-start.6 = (bf16[128,256]{1,0:T(8,128)(2,1)}, bf16[128,256]{1,0:T(8,128)(2,1)S(1)}, u32[]{:S(2)}) copy-start(bf16[128,256]{1,0:T(8,128)(2,1)S(1)} %collective-permute-done.16.refs_12_) | copy-start | bytes 196612
  63.5 6.6 %collective-permute-start.5 = (bf16[128,256]{1,0:T(8,128)(2,1)S(1)}, bf16[128,256]{1,0:T(8,128)(2,1)S(1)}, u32[]{:S(2)}, u32[]{:S(2)}) collective-permute-start(bf16[128,256]{1,0:T(8,128)(2,1)S(1)} %add_convert_fusion.1.refs_0_), channel_id=1, source_target_pairs={{0,12},{4,8},{8,4},{12,0},{1,13},{5,9},{9,5},{13,1},{2,14},{6,10},... | collective-permute-start | bytes 196616 | tf_op jit(solution)/shard_map/ppermute | solution.py:23
  65.9 12.1 %copy-start.8 = (bf16[128,256]{1,0:T(8,128)(2,1)}, bf16[128,256]{1,0:T(8,128)(2,1)S(1)}, u32[]{:S(2)}) copy-start(bf16[128,256]{1,0:T(8,128)(2,1)S(1)} %collective-permute-done.15.refs_11_) | copy-start | bytes 196612
  65.9 5.7 %collective-permute-start.4 = (bf16[128,256]{1,0:T(8,128)(2,1)S(1)}, bf16[128,256]{1,0:T(8,128)(2,1)S(1)}, u32[]{:S(2)}, u32[]{:S(2)}) collective-permute-start(bf16[128,256]{1,0:T(8,128)(2,1)S(1)} %add_convert_fusion.1.refs_0_), channel_id=1, source_target_pairs={{0,8},{4,12},{8,0},{12,4},{1,9},{5,13},{9,1},{13,5},{2,10},{6,14},... | collective-permute-start | bytes 196616 | tf_op jit(solution)/shard_map/ppermute | solution.py:23
  66.5 11.5 %copy-start.9 = (bf16[128,256]{1,0:T(8,128)(2,1)}, bf16[128,256]{1,0:T(8,128)(2,1)S(1)}, u32[]{:S(2)}) copy-start(bf16[128,256]{1,0:T(8,128)(2,1)S(1)} %collective-permute-done.14.refs_10_) | copy-start | bytes 196612
  66.5 6.1 %collective-permute-start.3 = (bf16[128,256]{1,0:T(8,128)(2,1)S(1)}, bf16[128,256]{1,0:T(8,128)(2,1)S(1)}, u32[]{:S(2)}, u32[]{:S(2)}) collective-permute-start(bf16[128,256]{1,0:T(8,128)(2,1)S(1)} %add_convert_fusion.1.refs_0_), channel_id=1, source_target_pairs={{0,4},{4,0},{8,12},{12,8},{1,5},{5,1},{9,13},{13,9},{2,6},{6,2},{1... | collective-permute-start | bytes 196616 | tf_op jit(solution)/shard_map/ppermute | solution.py:23
  67.9 10.1 %copy-start.11 = (bf16[128,256]{1,0:T(8,128)(2,1)}, bf16[128,256]{1,0:T(8,128)(2,1)S(1)}, u32[]{:S(2)}) copy-start(bf16[128,256]{1,0:T(8,128)(2,1)S(1)} %collective-permute-done.13.refs_9_) | copy-start | bytes 196612
  67.9 5.8 %collective-permute-start.19 = (bf16[128,256]{1,0:T(8,128)(2,1)S(1)}, bf16[128,256]{1,0:T(8,128)(2,1)S(1)}, u32[]{:S(2)}, u32[]{:S(2)}) collective-permute-start(bf16[128,256]{1,0:T(8,128)(2,1)S(1)} %collective-permute-done.15.refs_11_), channel_id=1, source_target_pairs={{0,2},{2,0},{1,3},{3,1},{4,6},{6,4},{5,7},{7,5},{8,10},{10,8},{9,1... | collective-permute-start | bytes 196616 | tf_op jit(solution)/shard_map/ppermute | solution.py:23
  69.0 9.0 %copy-start.13 = (bf16[128,256]{1,0:T(8,128)(2,1)}, bf16[128,256]{1,0:T(8,128)(2,1)S(1)}, u32[]{:S(2)}) copy-start(bf16[128,256]{1,0:T(8,128)(2,1)S(1)} %collective-permute-done.6.refs_4_) | copy-start | bytes 196612
  69.0 5.6 %collective-permute-start.18 = (bf16[128,256]{1,0:T(8,128)(2,1)S(1)}, bf16[128,256]{1,0:T(8,128)(2,1)S(1)}, u32[]{:S(2)}, u32[]{:S(2)}) collective-permute-start(bf16[128,256]{1,0:T(8,128)(2,1)S(1)} %collective-permute-done.14.refs_10_), channel_id=1, source_target_pairs={{0,2},{2,0},{1,3},{3,1},{4,6},{6,4},{5,7},{7,5},{8,10},{10,8},{9,1... | collective-permute-start | bytes 196616 | tf_op jit(solution)/shard_map/ppermute | solution.py:23
  70.1 8.0 %copy-start.14 = (bf16[128,256]{1,0:T(8,128)(2,1)}, bf16[128,256]{1,0:T(8,128)(2,1)S(1)}, u32[]{:S(2)}) copy-start(bf16[128,256]{1,0:T(8,128)(2,1)S(1)} %collective-permute-done.5.refs_3_) | copy-start | bytes 196612
  70.1 5.2 %collective-permute-start.17 = (bf16[128,256]{1,0:T(8,128)(2,1)S(1)}, bf16[128,256]{1,0:T(8,128)(2,1)S(1)}, u32[]{:S(2)}, u32[]{:S(2)}) collective-permute-start(bf16[128,256]{1,0:T(8,128)(2,1)S(1)} %collective-permute-done.13.refs_9_), channel_id=1, source_target_pairs={{0,2},{2,0},{1,3},{3,1},{4,6},{6,4},{5,7},{7,5},{8,10},{10,8},{9,1... | collective-permute-start | bytes 196616 | tf_op jit(solution)/shard_map/ppermute | solution.py:23
  71.6 6.4 %copy-start.15 = (bf16[128,256]{1,0:T(8,128)(2,1)}, bf16[128,256]{1,0:T(8,128)(2,1)S(1)}, u32[]{:S(2)}) copy-start(bf16[128,256]{1,0:T(8,128)(2,1)S(1)} %collective-permute-done.4.refs_2_) | copy-start | bytes 196612
  71.6 4.3 %collective-permute-start.9 = (bf16[128,256]{1,0:T(8,128)(2,1)S(1)}, bf16[128,256]{1,0:T(8,128)(2,1)S(1)}, u32[]{:S(2)}, u32[]{:S(2)}) collective-permute-start(bf16[128,256]{1,0:T(8,128)(2,1)S(1)} %collective-permute-done.5.refs_3_), channel_id=1, source_target_pairs={{0,2},{2,0},{1,3},{3,1},{4,6},{6,4},{5,7},{7,5},{8,10},{10,8},{9,1... | collective-permute-start | bytes 196616 | tf_op jit(solution)/shard_map/ppermute | solution.py:23
  72.6 5.5 %copy-start.16 = (bf16[128,256]{1,0:T(8,128)(2,1)}, bf16[128,256]{1,0:T(8,128)(2,1)S(1)}, u32[]{:S(2)}) copy-start(bf16[128,256]{1,0:T(8,128)(2,1)S(1)} %collective-permute-done.3.refs_1_) | copy-start | bytes 196612
  72.6 4.3 %collective-permute-start.8 = (bf16[128,256]{1,0:T(8,128)(2,1)S(1)}, bf16[128,256]{1,0:T(8,128)(2,1)S(1)}, u32[]{:S(2)}, u32[]{:S(2)}) collective-permute-start(bf16[128,256]{1,0:T(8,128)(2,1)S(1)} %collective-permute-done.4.refs_2_), channel_id=1, source_target_pairs={{0,2},{2,0},{1,3},{3,1},{4,6},{6,4},{5,7},{7,5},{8,10},{10,8},{9,1... | collective-permute-start | bytes 196616 | tf_op jit(solution)/shard_map/ppermute | solution.py:23
  73.7 4.4 %copy-start.17 = (bf16[128,256]{1,0:T(8,128)(2,1)}, bf16[128,256]{1,0:T(8,128)(2,1)S(1)}, u32[]{:S(2)}) copy-start(bf16[128,256]{1,0:T(8,128)(2,1)S(1)} %collective-permute-done.19.refs_15_) | copy-start | bytes 196612
  73.7 4.3 %collective-permute-start.7 = (bf16[128,256]{1,0:T(8,128)(2,1)S(1)}, bf16[128,256]{1,0:T(8,128)(2,1)S(1)}, u32[]{:S(2)}, u32[]{:S(2)}) collective-permute-start(bf16[128,256]{1,0:T(8,128)(2,1)S(1)} %collective-permute-done.3.refs_1_), channel_id=1, source_target_pairs={{0,2},{2,0},{1,3},{3,1},{4,6},{6,4},{5,7},{7,5},{8,10},{10,8},{9,1... | collective-permute-start | bytes 196616 | tf_op jit(solution)/shard_map/ppermute | solution.py:23
  134.5 8.1 %collective-permute-start.41 = (f32[4,128]{1,0:T(4,128)S(1)}, f32[4,128]{1,0:T(4,128)S(1)}, u32[]{:S(2)}, u32[]{:S(2)}) collective-permute-start(f32[4,128]{1,0:T(4,128)S(1)} %dynamic_update_slice.5), channel_id=1, source_target_pairs={{0,15},{1,14},{2,13},{3,12},{4,11},{5,10},{6,9},{7,8},{8,7},{9,6},... | collective-permute-start | bytes 6152 | tf_op jit(solution)/shard_map/ppermute | solution.py:23
  134.6 9.7 %collective-permute-start.40 = (f32[4,128]{1,0:T(4,128)S(1)}, f32[4,128]{1,0:T(4,128)S(1)}, u32[]{:S(2)}, u32[]{:S(2)}) collective-permute-start(f32[4,128]{1,0:T(4,128)S(1)} %dynamic_update_slice.5), channel_id=1, source_target_pairs={{0,14},{1,15},{2,12},{3,13},{4,10},{5,11},{6,8},{7,9},{8,6},{9,7},... | collective-permute-start | bytes 6152 | tf_op jit(solution)/shard_map/ppermute | solution.py:23
  137.0 8.7 %collective-permute-start.39 = (f32[4,128]{1,0:T(4,128)S(1)}, f32[4,128]{1,0:T(4,128)S(1)}, u32[]{:S(2)}, u32[]{:S(2)}) collective-permute-start(f32[4,128]{1,0:T(4,128)S(1)} %dynamic_update_slice.5), channel_id=1, source_target_pairs={{0,13},{1,12},{2,15},{3,14},{4,9},{5,8},{6,11},{7,10},{8,5},{9,4},... | collective-permute-start | bytes 6152 | tf_op jit(solution)/shard_map/ppermute | solution.py:23
  140.6 8.1 %collective-permute-start.38 = (f32[4,128]{1,0:T(4,128)S(1)}, f32[4,128]{1,0:T(4,128)S(1)}, u32[]{:S(2)}, u32[]{:S(2)}) collective-permute-start(f32[4,128]{1,0:T(4,128)S(1)} %dynamic_update_slice.5), channel_id=1, source_target_pairs={{0,12},{1,13},{2,14},{3,15},{4,8},{5,9},{6,10},{7,11},{8,4},{9,5},... | collective-permute-start | bytes 6152 | tf_op jit(solution)/shard_map/ppermute | solution.py:23
  142.5 6.2 %collective-permute-start.37 = (f32[4,128]{1,0:T(4,128)S(1)}, f32[4,128]{1,0:T(4,128)S(1)}, u32[]{:S(2)}, u32[]{:S(2)}) collective-permute-start(f32[4,128]{1,0:T(4,128)S(1)} %dynamic_update_slice.5), channel_id=1, source_target_pairs={{0,11},{1,10},{2,9},{3,8},{4,15},{5,14},{6,13},{7,12},{8,3},{9,2},... | collective-permute-start | bytes 6152 | tf_op jit(solution)/shard_map/ppermute | solution.py:23
  142.5 31.2 %collective-permute-start.36 = (f32[4,128]{1,0:T(4,128)S(1)}, f32[4,128]{1,0:T(4,128)S(1)}, u32[]{:S(2)}, u32[]{:S(2)}) collective-permute-start(f32[4,128]{1,0:T(4,128)S(1)} %dynamic_update_slice.5), channel_id=1, source_target_pairs={{0,10},{1,11},{2,8},{3,9},{4,14},{5,15},{6,12},{7,13},{8,2},{9,3},... | collective-permute-start | bytes 6152 | tf_op jit(solution)/shard_map/ppermute | solution.py:23
  144.2 32.5 %collective-permute-start.35 = (f32[4,128]{1,0:T(4,128)S(1)}, f32[4,128]{1,0:T(4,128)S(1)}, u32[]{:S(2)}, u32[]{:S(2)}) collective-permute-start(f32[4,128]{1,0:T(4,128)S(1)} %dynamic_update_slice.5), channel_id=1, source_target_pairs={{0,9},{1,8},{2,11},{3,10},{4,13},{5,12},{6,15},{7,14},{8,1},{9,0},... | collective-permute-start | bytes 6152 | tf_op jit(solution)/shard_map/ppermute | solution.py:23
  145.7 31.0 %collective-permute-start.34 = (f32[4,128]{1,0:T(4,128)S(1)}, f32[4,128]{1,0:T(4,128)S(1)}, u32[]{:S(2)}, u32[]{:S(2)}) collective-permute-start(f32[4,128]{1,0:T(4,128)S(1)} %dynamic_update_slice.5), channel_id=1, source_target_pairs={{0,8},{1,9},{2,10},{3,11},{4,12},{5,13},{6,14},{7,15},{8,0},{9,1},... | collective-permute-start | bytes 6152 | tf_op jit(solution)/shard_map/ppermute | solution.py:23
  148.7 29.3 %collective-permute-start.33 = (f32[4,128]{1,0:T(4,128)S(1)}, f32[4,128]{1,0:T(4,128)S(1)}, u32[]{:S(2)}, u32[]{:S(2)}) collective-permute-start(f32[4,128]{1,0:T(4,128)S(1)} %dynamic_update_slice.5), channel_id=1, source_target_pairs={{0,7},{1,6},{2,5},{3,4},{4,3},{5,2},{6,1},{7,0},{8,15},{9,14},{10,... | collective-permute-start | bytes 6152 | tf_op jit(solution)/shard_map/ppermute | solution.py:23
  148.8 30.4 %collective-permute-start.27 = (f32[4,128]{1,0:T(4,128)S(1)}, f32[4,128]{1,0:T(4,128)S(1)}, u32[]{:S(2)}, u32[]{:S(2)}) collective-permute-start(f32[4,128]{1,0:T(4,128)S(1)} %dynamic_update_slice.5), channel_id=1, source_target_pairs={{0,1},{1,0},{2,3},{3,2},{4,5},{5,4},{6,7},{7,6},{8,9},{9,8},{10,11... | collective-permute-start | bytes 6152 | tf_op jit(solution)/shard_map/ppermute | solution.py:23
  173.8 6.6 %collective-permute-start.32 = (f32[4,128]{1,0:T(4,128)S(1)}, f32[4,128]{1,0:T(4,128)S(1)}, u32[]{:S(2)}, u32[]{:S(2)}) collective-permute-start(f32[4,128]{1,0:T(4,128)S(1)} %dynamic_update_slice.5), channel_id=1, source_target_pairs={{0,6},{1,7},{2,4},{3,5},{4,2},{5,3},{6,0},{7,1},{8,14},{9,15},{10,... | collective-permute-start | bytes 6152 | tf_op jit(solution)/shard_map/ppermute | solution.py:23
  176.7 3.7 %collective-permute-start.31 = (f32[4,128]{1,0:T(4,128)S(1)}, f32[4,128]{1,0:T(4,128)S(1)}, u32[]{:S(2)}, u32[]{:S(2)}) collective-permute-start(f32[4,128]{1,0:T(4,128)S(1)} %dynamic_update_slice.5), channel_id=1, source_target_pairs={{0,5},{1,4},{2,7},{3,6},{4,1},{5,0},{6,3},{7,2},{8,13},{9,12},{10,... | collective-permute-start | bytes 6152 | tf_op jit(solution)/shard_map/ppermute | solution.py:23
  176.7 3.7 %collective-permute-start.30 = (f32[4,128]{1,0:T(4,128)S(1)}, f32[4,128]{1,0:T(4,128)S(1)}, u32[]{:S(2)}, u32[]{:S(2)}) collective-permute-start(f32[4,128]{1,0:T(4,128)S(1)} %dynamic_update_slice.5), channel_id=1, source_target_pairs={{0,4},{1,5},{2,6},{3,7},{4,0},{5,1},{6,2},{7,3},{8,12},{9,13},{10,... | collective-permute-start | bytes 6152 | tf_op jit(solution)/shard_map/ppermute | solution.py:23
  178.1 3.0 %collective-permute-start.29 = (f32[4,128]{1,0:T(4,128)S(1)}, f32[4,128]{1,0:T(4,128)S(1)}, u32[]{:S(2)}, u32[]{:S(2)}) collective-permute-start(f32[4,128]{1,0:T(4,128)S(1)} %dynamic_update_slice.5), channel_id=1, source_target_pairs={{0,3},{1,2},{2,1},{3,0},{4,7},{5,6},{6,5},{7,4},{8,11},{9,10},{10,... | collective-permute-start | bytes 6152 | tf_op jit(solution)/shard_map/ppermute | solution.py:23
  179.2 3.6 %collective-permute-start.28 = (f32[4,128]{1,0:T(4,128)S(1)}, f32[4,128]{1,0:T(4,128)S(1)}, u32[]{:S(2)}, u32[]{:S(2)}) collective-permute-start(f32[4,128]{1,0:T(4,128)S(1)} %dynamic_update_slice.5), channel_id=1, source_target_pairs={{0,2},{1,3},{2,0},{3,1},{4,6},{5,7},{6,4},{7,5},{8,10},{9,11},{10,... | collective-permute-start | bytes 6152 | tf_op jit(solution)/shard_map/ppermute | solution.py:23
  (5 other events, 10.4 us)

commit v2 on v1

v2 whole, which is shorter than its diff:
```python
import functools

import jax
import jax.numpy as jnp
from jax import lax
from jax.experimental import pallas as pl
from jax.experimental.pallas import tpu as pltpu
from jax.sharding import PartitionSpec as P

LEN = 1024
ITERS = 6
DAMPING = 0.1
NT = (((1,), (1,)), ((), ()))
VMEM_BYTES = 56 * 1024 * 1024


def whole_spec(shape):
    zeros = (0,) * len(shape)
    return pl.BlockSpec(shape, lambda *_: zeros)


def swap(value, axes, size, offset):
    return lax.ppermute(value, axes, [(i, i ^ offset) for i in range(size)])


def encode(value):
    return (value * jnp.abs(value)).astype(jnp.bfloat16)


def decode(code):
    wide = code.astype(jnp.float32)
    root = jnp.sqrt(jnp.abs(wide))
    return jnp.where(wide < 0, -root, root)


def project_kernel(inputs, grads, proj_in, proj_out, out):
    x = lax.dot_general(inputs[...], proj_in[...], NT, preferred_element_type=jnp.float32)
    g = lax.dot_general(grads[...], proj_out[...], NT, preferred_element_type=jnp.float32)
    out[0] = encode(jnp.concatenate([x, g], axis=1).T)


def project(inputs, grads, proj_in, proj_out, chunk, block):
    parts = lax.axis_size("tensor")
    rank, features = proj_in.shape
    hidden = proj_out.shape[1]

    def rows(step):
        return (chunk * parts + step, 0)

    return pl.pallas_call(
        project_kernel,
        grid=(parts,),
        in_specs=[
            pl.BlockSpec((block, features), rows),
            pl.BlockSpec((block, hidden), rows),
            whole_spec(proj_in.shape),
            whole_spec(proj_out.shape),
        ],
        out_specs=pl.BlockSpec((1, 2 * rank, block), lambda step: (step, 0, 0)),
        out_shape=jax.ShapeDtypeStruct((parts, 2 * rank, block), jnp.bfloat16),
        compiler_params=pltpu.CompilerParams(vmem_limit_bytes=VMEM_BYTES),
        cost_estimate=pl.CostEstimate(
            flops=2 * parts * block * (features + hidden) * rank,
            bytes_accessed=2 * parts * block * (features + hidden),
            transcendentals=0,
        ),
        name="project",
    )(inputs, grads, proj_in, proj_out)


def split_queries_kernel(queries, out):
    owners, cols, mine, rank = out.shape
    for i in range(mine):
        turned = queries[i * rank : (i + 1) * rank, :].T
        out[:, :, i, :] = turned.reshape(owners, cols, rank)


def split_queries(queries, owners, rank):
    rows, total = queries.shape
    shape = (owners, total // owners, rows // rank, rank)
    return pl.pallas_call(
        split_queries_kernel,
        out_shape=jax.ShapeDtypeStruct(shape, jnp.float32),
        compiler_params=pltpu.CompilerParams(vmem_limit_bytes=VMEM_BYTES),
        name="split_queries",
    )(queries)


def solve_kernel(tokens, span, count, *refs):
    pieces = refs[:count]
    queries, out, x_s, g_s, pair, direction, residual, image, sums = refs[count:]
    cols, side, rank = direction.shape
    chunks, _, wide = x_s.shape
    parts, _, block = pieces[0].shape
    for n in range(count * parts):
        piece = pieces[n // parts]
        c, at = divmod(n * block, wide)
        x_s[c, :, at : at + block] = piece[n % parts, :rank, :].astype(jnp.float32)
        g = piece[n % parts, rank:, :]
        g_s[c, :rank, at : at + block] = g
        g_s[c, rank:, at : at + block] = g
    mine = queries.shape[2]
    for k in range(side // mine):
        direction[:, k * mine : (k + 1) * mine, :] = queries[k]
    residual[...] = direction[...]

    def total(value):
        return jnp.sum(jnp.sum(value, axis=1, keepdims=True), axis=2, keepdims=True)

    def forward(c):
        w = jnp.dot(pair[...], g_s[c], preferred_element_type=jnp.float32)
        x = x_s[c][None]
        return jnp.sum(w.reshape(cols, side, wide) * x, axis=1, keepdims=True), x

    def prepare():
        d = direction[...]
        high = d.astype(jnp.bfloat16)
        low = (d - high.astype(jnp.float32)).astype(jnp.bfloat16)
        pair[...] = jnp.concatenate([high, low], axis=2).reshape(cols * side, 2 * rank)
        sums[...] = jnp.zeros_like(sums)
        return total(d * d)

    def step_size(norm, length, energy):
        energy = jnp.sum(energy, axis=2, keepdims=True)
        return norm / (energy * (1.0 / tokens) + DAMPING * length)

    def fold(c, u):
        sums[c * wide // span] += jnp.sum(u, axis=2, keepdims=True)

    out[...] = jnp.zeros_like(out)

    def one_step(_, norm):
        length = prepare()
        energy = jnp.zeros((cols, 1, wide), jnp.float32)
        for c in range(chunks):
            u, x = forward(c)
            spread = (u * x).astype(jnp.bfloat16).reshape(cols * side, wide)
            part = lax.dot_general(
                spread, g_s[c, :rank, :], NT, preferred_element_type=jnp.float32
            ).reshape(cols, side, rank)
            image[...] = part if c == 0 else image[...] + part
            fold(c, u)
            energy = energy + u * u
        alpha = step_size(norm, length, energy)
        out[...] += alpha[None] * sums[...]
        d = direction[...]
        r = residual[...] - alpha * (image[...] * (1.0 / tokens) + DAMPING * d)
        residual[...] = r
        later = total(r * r)
        direction[...] = r + later / norm * d
        return later

    norm = lax.fori_loop(0, ITERS - 1, one_step, total(residual[...] * residual[...]))
    length = prepare()
    energy = jnp.zeros((cols, 1, wide), jnp.float32)
    for c in range(chunks):
        u, _ = forward(c)
        fold(c, u)
        energy = energy + u * u
    out[...] += step_size(norm, length, energy)[None] * sums[...]


def solve(pieces, queries, tokens, span):
    owners, cols, mine, rank = queries.shape
    side = mine * owners
    wide = min(512, span)
    count = len(pieces)
    vectors = pltpu.VMEM((cols, side, rank), jnp.float32)
    sums = (tokens // span, cols, 1, 128)
    return pl.pallas_call(
        functools.partial(solve_kernel, tokens, span, count),
        out_shape=jax.ShapeDtypeStruct(sums, jnp.float32),
        scratch_shapes=[
            pltpu.VMEM((tokens // wide, rank, wide), jnp.float32),
            pltpu.VMEM((tokens // wide, 2 * rank, wide), jnp.bfloat16),
            pltpu.VMEM((cols * side, 2 * rank), jnp.bfloat16),
            vectors,
            vectors,
            vectors,
            pltpu.VMEM(sums, jnp.float32),
        ],
        compiler_params=pltpu.CompilerParams(vmem_limit_bytes=VMEM_BYTES),
        cost_estimate=pl.CostEstimate(
            flops=2 * 2 * ITERS * 4 * tokens * cols * side * rank,
            bytes_accessed=4 * tokens * rank,
            transcendentals=0,
        ),
        name="solve",
    )(*pieces, queries)


def hessian_kernel(tokens, count, place, *refs):
    pieces = refs[:count]
    out, x_s, g_s, own, even, odd = refs[count:]
    step = pl.program_id(0)
    steps = pl.num_programs(0)
    rank = x_s.shape[0]
    parts, _, block = pieces[0].shape
    rows = out.shape[0]
    columns = even.shape[0]

    def vectors(i):
        return x_s[pl.ds(i, 1), :].astype(jnp.bfloat16) * g_s[...]

    def form(target, tile):
        for j in range(columns // rank):
            target[j * rank : (j + 1) * rank, :] = vectors(tile * (columns // rank) + j)

    def product(source, half):
        gram = lax.dot_general(own[...], source[...], NT, preferred_element_type=jnp.float32)
        shape = (rows, columns)
        row = lax.broadcasted_iota(jnp.int32, shape, 0) + place[0] * rows
        column = lax.broadcasted_iota(jnp.int32, shape, 1) + (2 * step + half) * columns
        value = gram * (1.0 / tokens) + jnp.where(row == column, DAMPING, 0.0)
        out[:, half * columns : (half + 1) * columns] = value

    @pl.when(step == 0)
    def _():
        for n in range(count * parts):
            piece = pieces[n // parts]
            at = slice(n * block, (n + 1) * block)
            x_s[:, at] = piece[n % parts, :rank, :].astype(jnp.float32)
            g_s[:, at] = piece[n % parts, rank:, :]
        for i in range(rows // rank):
            own[i * rank : (i + 1) * rank, :] = vectors(place[0] * (rows // rank) + i)
        form(even, 0)

    form(odd, 2 * step + 1)
    product(even, 0)
    form(even, lax.rem(2 * step + 2, 2 * steps))
    product(odd, 1)


def hessian_rows(place, pieces, tokens, rows):
    rank = pieces[0].shape[1] // 2
    count = len(pieces)
    width = rank * rank
    columns = 256
    return pl.pallas_call(
        functools.partial(hessian_kernel, tokens, count),
        grid=(width // (2 * columns),),
        in_specs=[pl.BlockSpec(memory_space=pltpu.SMEM)]
        + [whole_spec(pieces[0].shape)] * count,
        out_specs=pl.BlockSpec((rows, 2 * columns), lambda step: (0, step)),
        out_shape=jax.ShapeDtypeStruct((rows, width), jnp.float32),
        scratch_shapes=[
            pltpu.VMEM((rank, tokens), jnp.float32),
            pltpu.VMEM((rank, tokens), jnp.bfloat16),
            pltpu.VMEM((rows, tokens), jnp.bfloat16),
            pltpu.VMEM((columns, tokens), jnp.bfloat16),
            pltpu.VMEM((columns, tokens), jnp.bfloat16),
        ],
        compiler_params=pltpu.CompilerParams(vmem_limit_bytes=VMEM_BYTES),
        cost_estimate=pl.CostEstimate(
            flops=2 * rows * width * tokens,
            bytes_accessed=4 * rows * width,
            transcendentals=0,
        ),
        name="hessian_rows",
    )(place, *pieces)


def shards(layer_input, out_grads, proj_in, proj_out, queries):
    rank = proj_in.shape[2]
    parts, dp_size = lax.axis_size("tensor"), lax.axis_size("dp")
    owners = parts * dp_size
    tok_dev = layer_input.shape[0]
    owned, nq = queries.shape[1:]
    dp_pos = lax.axis_index("dp").astype(jnp.int32)
    owner = lax.axis_index("tensor").astype(jnp.int32) * dp_size + dp_pos
    chunks = 2 if tok_dev // (2 * parts) >= 128 else 1
    block = tok_dev // (chunks * parts)
    tokens = tok_dev * dp_size

    def exchange(value, axes):
        return lax.all_to_all(value, axes, 0, 0, tiled=True)

    split = split_queries(queries[0], owners, rank)
    flat = split.reshape(owners, split.shape[1] * split.shape[2], rank)
    columns = exchange(flat, ("tensor", "dp")).reshape(split.shape)

    pieces, first = [], []
    for chunk in range(chunks):
        partial = project(
            layer_input, out_grads[0], proj_in[0].T, proj_out[0].T, chunk, block
        )
        summed = jnp.sum(decode(exchange(partial, "tensor")), axis=0).astype(jnp.bfloat16)
        near = exchange(jnp.broadcast_to(summed, (parts,) + summed.shape), "tensor")
        for k in range(dp_size):
            pieces.append(near if k == 0 else swap(near, "dp", dp_size, k))
            first.append(((dp_pos ^ k) * tok_dev, chunk * (tok_dev // chunks)))

    span = min(tok_dev // chunks, LEN)
    sums = solve(pieces, columns, tokens, span)[:, :, 0, 0]
    example = []
    for g in range(tokens // span):
        piece, inside = divmod(g * span, tok_dev // chunks)
        away, start = first[piece]
        example.append(away // LEN + (start + inside) // LEN)
    examples = tokens // LEN
    onehot = jnp.stack(example)[None, :] == jnp.arange(examples, dtype=jnp.int32)[:, None]
    local = jnp.sum(jnp.where(onehot[:, :, None], sums[None], 0.0), axis=1) / LEN
    cols = nq // owners
    placed = lax.dynamic_update_slice(
        jnp.zeros((examples, nq), jnp.float32), local, (jnp.int32(0), owner * cols)
    )
    scores = jnp.sum(lax.all_gather(placed, ("tensor", "dp", "pipe"), axis=0), axis=0)
    hessian = hessian_rows(owner.reshape(1), pieces, tokens, owned)
    return (hessian[None], scores)


def solution(mesh):
    in_specs = (
        P(("groups", "dp"), "tensor"),
        P("pipe", ("groups", "dp"), "tensor"),
        P("pipe", "tensor", None),
        P("pipe", "tensor", None),
        P("pipe", ("tensor", "dp"), None),
    )
    out_specs = (P("pipe", ("groups", "tensor", "dp"), None), P("groups", None))
    return jax.shard_map(shards, mesh=mesh, in_specs=in_specs, out_specs=out_specs, check_vma=False)
```

time: 184 us -> 149 us (0.81)
  starting transfers between devices: 60.2 us -> 23 us
  Pallas kernels: 96.4 us -> 68.2 us
  blocking collectives: 0 us -> 20.6 us
  waiting for transfers between devices: 18.1 us -> 28.1 us
    ppermute x42 -> x2, starting transfers between devices: 60.2 us -> 2.07 us  [swap(): return lax.ppermute(value, axes, [(i, i ^ offset) for i in range(size)])]
    pallas_call x4, Pallas kernels: 71.6 us -> 45.4 us  [the longest x1 29.2 us: solve(): pl.pallas_call(functools.partial(solve_kernel, tokens, span, count), out_...]
    all_to_all x0 -> x5, waiting for transfers between devices: none -> 25.3 us  [exchange(): return lax.all_to_all(value, axes, 0, 0, tiled=True)]
    all_to_all x0 -> x5, starting transfers between devices: none -> 20.9 us  [exchange(): return lax.all_to_all(value, axes, 0, 0, tiled=True)]
    all_gather x0 -> x1, blocking collectives: none -> 20.6 us  [shards(): lax.all_gather(placed, ('tensor', 'dp', 'pipe'), axis=0)]
    ppermute x42 -> x2, waiting for transfers between devices: 18.1 us -> 2.82 us  [swap(): return lax.ppermute(value, axes, [(i, i ^ offset) for i in range(size)])]
    unnamed x56 -> x8, local copies, waits for them, and re-layouts: 4.55 us -> 0.7 us
    pallas_call x1, Pallas kernels: 24.8 us -> 22.8 us  [hessian_rows(): pl.pallas_call(functools.partial(hessian_kernel, tokens, count), grid=(wi...]
  transfers between devices with their start and end apart: 42 -> 7, of which waited for: 11 -> 6; matrix products, arithmetic and copies ran while one was open for 1% -> 2% of each run, Pallas kernels for 19% -> 6%
where the time goes in v2:
time: 149 us; the launch traced here: 148 us
  Pallas kernels  68.2 us (46%)
  waiting for transfers between devices  28.1 us (19%)
  starting transfers between devices  23 us (15%)
  blocking collectives  20.6 us (14%)
  local copies, waits for them, and re-layouts  6.19 us (4%)
    pallas_call x1, Pallas kernels, solve(): pl.pallas_call(functools.partial(solve_kernel, tokens, span, count), out_...  29.2 us
    all_to_all x5, waiting for transfers between devices, exchange(): return lax.all_to_all(value, axes, 0, 0, tiled=True)  25.3 us
    pallas_call x1, Pallas kernels, hessian_rows(): pl.pallas_call(functools.partial(hessian_kernel, tokens, count), grid=(wi...  22.8 us
    all_to_all x5, starting transfers between devices, exchange(): return lax.all_to_all(value, axes, 0, 0, tiled=True)  20.9 us
    all_gather x1, blocking collectives, shards(): lax.all_gather(placed, ('tensor', 'dp', 'pipe'), axis=0)  20.6 us
    pallas_call x2, Pallas kernels, project(): pl.pallas_call(project_kernel, grid=(parts,), in_specs=[pl.BlockSpec((blo...  14 us
  transfers between devices with their start and end apart: 7, of which 6 were waited for; matrix products, arithmetic and copies ran while one was open for 2% of the time, Pallas kernels for 6%

profile of v2, /device:TPU:0, one launch (start us, length us, event | category | flops | bytes accessed | tf_op | source)
XLA Modules:
  0.0 148.0 jit_solution(11712431290053173533)
XLA Ops:
  0.6 7.0 %project.3 = bf16[4,128,256]{2,1,0:T(8,128)(2,1)} custom-call(bf16[2048,1024]{1,0:T(8,128)(2,1)} %inputs.3, bf16[2048,3584]{1,0:T(8,128)(2,1)} %bitcast.18, bf16[64,1024]{1,0:T(8,128)(2,1)} %bitcast.23, bf16[64,3584]{1,0:T(8,128)(2,1)} %bitcast.21), custom_call_target="tpu_custom_call" | custom-call | flops 603979776 | bytes 9437184 | tf_op jit(solution)/shard_map/project/pallas_call | solution.py:50
  7.7 6.3 %all-to-all-start.2 = ((bf16[4,128,256]{2,1,0:T(8,128)(2,1)}), bf16[4,128,256]{2,1,0:T(8,128)(2,1)S(1)}, u32[]{:S(2)}, u32[]{:S(2)}) async-start(bf16[4,128,256]{2,1,0:T(8,128)(2,1)} %project.3), calls=%async_computation.2 | async-start | bytes 524288 | tf_op jit(solution)/shard_map/all_to_all | solution.py:276
  14.0 7.0 %project.2 = bf16[4,128,256]{2,1,0:T(8,128)(2,1)} custom-call(bf16[2048,1024]{1,0:T(8,128)(2,1)} %inputs.3, bf16[2048,3584]{1,0:T(8,128)(2,1)} %bitcast.19, bf16[64,1024]{1,0:T(8,128)(2,1)} %bitcast.24, bf16[64,3584]{1,0:T(8,128)(2,1)} %bitcast.22), custom_call_target="tpu_custom_call" | custom-call | flops 603979776 | bytes 9437184 | tf_op jit(solution)/shard_map/project/pallas_call | solution.py:50
  20.9 1.9 %all-to-all-done.2 = bf16[4,128,256]{2,1,0:T(8,128)(2,1)S(1)} async-done(((bf16[4,128,256]{2,1,0:T(8,128)(2,1)}), bf16[4,128,256]{2,1,0:T(8,128)(2,1)S(1)}, u32[]{:S(2)}, u32[]{:S(2)}) %all-to-all-start.2) | async-done | bytes 262176 | tf_op jit(solution)/shard_map/all_to_all | solution.py:276
  22.9 3.4 %all-to-all-start = ((bf16[4,128,256]{2,1,0:T(8,128)(2,1)}), bf16[4,128,256]{2,1,0:T(8,128)(2,1)S(1)}, u32[]{:S(2)}, u32[]{:S(2)}) async-start(bf16[4,128,256]{2,1,0:T(8,128)(2,1)} %project.2), calls=%async_computation | async-start | bytes 524288 | tf_op jit(solution)/shard_map/all_to_all | solution.py:276
  26.3 0.2 fusion.3
  26.5 7.9 %all-to-all-done = bf16[4,128,256]{2,1,0:T(8,128)(2,1)S(1)} async-done(((bf16[4,128,256]{2,1,0:T(8,128)(2,1)}), bf16[4,128,256]{2,1,0:T(8,128)(2,1)S(1)}, u32[]{:S(2)}, u32[]{:S(2)}) %all-to-all-start) | async-done | bytes 262176 | tf_op jit(solution)/shard_map/all_to_all | solution.py:276
  34.4 0.7 broadcast_in_dim.38
  35.2 3.4 %all-to-all-start.3 = ((bf16[4,128,256]{2,1,0:T(8,128)(2,1)}), bf16[4,128,256]{2,1,0:T(8,128)(2,1)S(1)}, u32[]{:S(2)}, u32[]{:S(2)}) async-start(bf16[4,128,256]{2,1,0:T(8,128)(2,1)} %broadcast_in_dim.38), calls=%async_computation.3 | async-start | bytes 524288 | tf_op jit(solution)/shard_map/all_to_all | solution.py:276
  38.6 0.2 fusion.2
  38.8 6.5 %all-to-all-done.3.refs_2_ = bf16[4,128,256]{2,1,0:T(8,128)(2,1)S(1)} async-done(((bf16[4,128,256]{2,1,0:T(8,128)(2,1)}), bf16[4,128,256]{2,1,0:T(8,128)(2,1)S(1)}, u32[]{:S(2)}, u32[]{:S(2)}) %all-to-all-start.3) | async-done | bytes 262176 | tf_op jit(solution)/shard_map/all_to_all | solution.py:276
  45.3 0.0 copy-start
  45.3 0.7 broadcast_in_dim.37
  46.1 3.4 %all-to-all-start.1 = ((bf16[4,128,256]{2,1,0:T(8,128)(2,1)}), bf16[4,128,256]{2,1,0:T(8,128)(2,1)S(1)}, u32[]{:S(2)}, u32[]{:S(2)}) async-start(bf16[4,128,256]{2,1,0:T(8,128)(2,1)} %broadcast_in_dim.37), calls=%async_computation.1 | async-start | bytes 524288 | tf_op jit(solution)/shard_map/all_to_all | solution.py:276
  49.5 2.1 %split_queries.1 = f32[8,16,8,64]{3,2,1,0:T(8,128)} custom-call(f32[512,128]{1,0:T(8,128)} %bitcast.26), custom_call_target="tpu_custom_call" | custom-call | tf_op jit(solution)/shard_map/split_queries/pallas_call | solution.py:81
  51.6 1.9 %copy.9 = f32[8,128,64]{1,2,0:T(8,128)} copy(f32[8,128,64]{2,1,0:T(8,128)} %bitcast.20) | data formatting | bytes 524288 | tf_op jit(solution)/shard_map/reshape | solution.py:279
  53.5 2.8 %all-to-all-done.1.refs_0_ = bf16[4,128,256]{2,1,0:T(8,128)(2,1)S(1)} async-done(((bf16[4,128,256]{2,1,0:T(8,128)(2,1)}), bf16[4,128,256]{2,1,0:T(8,128)(2,1)S(1)}, u32[]{:S(2)}, u32[]{:S(2)}) %all-to-all-start.1) | async-done | bytes 262176 | tf_op jit(solution)/shard_map/all_to_all | solution.py:276
  56.3 0.0 copy-start.1
  56.3 4.4 %all-to-all-start.4 = ((f32[8,128,64]{1,2,0:T(8,128)}), f32[8,128,64]{1,2,0:T(8,128)S(1)}, u32[]{:S(2)}, u32[]{:S(2)}) async-start(f32[8,128,64]{1,2,0:T(8,128)} %copy.9), calls=%async_computation.4 | async-start | bytes 524288 | tf_op jit(solution)/shard_map/all_to_all | solution.py:276
  60.6 2.0 %collective-permute-start = (bf16[4,128,256]{2,1,0:T(8,128)(2,1)S(1)}, bf16[4,128,256]{2,1,0:T(8,128)(2,1)S(1)}, u32[]{:S(2)}, u32[]{:S(2)}) collective-permute-start(bf16[4,128,256]{2,1,0:T(8,128)(2,1)S(1)} %all-to-all-done.1.refs_0_), channel_id=1, source_target_pairs={{0,2},{2,0},{1,3},{3,1},{4,6},{6,4},{5,7},{7,5},{8,10},{10,8},{9,1... | collective-permute-start | bytes 786440 | tf_op jit(solution)/shard_map/ppermute | solution.py:23
  62.7 0.0 collective-permute-start.1
  62.7 0.1 pad_add_fusion
  62.8 6.2 %all-to-all-done.4 = f32[8,128,64]{1,2,0:T(8,128)S(1)} async-done(((f32[8,128,64]{1,2,0:T(8,128)}), f32[8,128,64]{1,2,0:T(8,128)S(1)}, u32[]{:S(2)}, u32[]{:S(2)}) %all-to-all-start.4) | async-done | bytes 262176 | tf_op jit(solution)/shard_map/all_to_all | solution.py:276
  69.0 1.0 copy.10
  70.0 0.0 collective-permute-done.refs_1_
  70.0 0.0 copy-start.2
  70.0 2.8 %collective-permute-done.1.refs_3_ = bf16[4,128,256]{2,1,0:T(8,128)(2,1)S(1)} collective-permute-done((bf16[4,128,256]{2,1,0:T(8,128)(2,1)S(1)}, bf16[4,128,256]{2,1,0:T(8,128)(2,1)S(1)}, u32[]{:S(2)}, u32[]{:S(2)}) %collective-permute-start.1) | collective-permute-done | bytes 262176 | tf_op jit(solution)/shard_map/ppermute | solution.py:23
  72.8 0.0 copy-start.3
  72.8 0.0 copy-done
  72.8 0.0 copy-done.1
  72.8 0.0 copy-done.2
  72.8 0.7 copy-done.3
  73.5 29.2 %solve.1 = f32[4,16,1,128]{3,2,1,0:T(1,128)} custom-call(bf16[4,128,256]{2,1,0:T(8,128)(2,1)} %copy-done.1, bf16[4,128,256]{2,1,0:T(8,128)(2,1)} %copy-done.2, bf16[4,128,256]{2,1,0:T(8,128)(2,1)} %copy-done, bf16[4,128,256]{2,1,0:T(8,128)(2,1)} %copy-done.3, f32[8,16,8,64]{3,2,1,0:T(8,128)} %bitcast.25), custom_call_target="tpu_custom_call" | custom-call | flops 25769803776 | bytes 1048576 | tf_op jit(solution)/shard_map/solve/pallas_call | solution.py:170
  102.7 1.0 slice_reduce_fusion
  103.7 0.1 select_reduce_fusion
  103.8 0.1 dynamic_update_slice.4
  104.0 20.6 %all_gather.4 = f32[16,4,128]{2,1,0:T(4,128)S(1)} all-gather(f32[1,4,128]{2,1,0:T(4,128)S(1)} %dynamic_update_slice.4), channel_id=1, replica_groups=mesh['groups'=2,'tensor'=4,'dp'=2,'pipe'=2] {'tensor','dp','pipe'}, dimensions={0}, use_global_device_ids=true | all-gather | bytes 34816 | tf_op jit(solution)/shard_map/all_gather | solution.py:307
  124.6 0.6 reduce_sum.39
  125.2 22.8 %hessian_rows.1 = f32[512,4096]{1,0:T(8,128)} custom-call(s32[1]{0:T(128)} %bitcast.place, bf16[4,128,256]{2,1,0:T(8,128)(2,1)} %copy-done.1, bf16[4,128,256]{2,1,0:T(8,128)(2,1)} %copy-done.2, bf16[4,128,256]{2,1,0:T(8,128)(2,1)} %copy-done, bf16[4,128,256]{2,1,0:T(8,128)(2,1)} %copy-done.3), custom_call_target="tpu_custom_call" | custom-call | flops 17179869184 | bytes 8388608 | tf_op jit(solution)/shard_map/hessian_rows/pallas_call | solution.py:239
  (3 shorter events, 0.0 us)
Async XLA Ops:
  7.7 15.2 %all-to-all-start.2 = ((bf16[4,128,256]{2,1,0:T(8,128)(2,1)}), bf16[4,128,256]{2,1,0:T(8,128)(2,1)S(1)}, u32[]{:S(2)}, u32[]{:S(2)}) async-start(bf16[4,128,256]{2,1,0:T(8,128)(2,1)} %project.3), calls=%async_computation.2 | async-start | bytes 524288 | tf_op jit(solution)/shard_map/all_to_all | solution.py:276
  22.9 11.6 %all-to-all-start = ((bf16[4,128,256]{2,1,0:T(8,128)(2,1)}), bf16[4,128,256]{2,1,0:T(8,128)(2,1)S(1)}, u32[]{:S(2)}, u32[]{:S(2)}) async-start(bf16[4,128,256]{2,1,0:T(8,128)(2,1)} %project.2), calls=%async_computation | async-start | bytes 524288 | tf_op jit(solution)/shard_map/all_to_all | solution.py:276
  35.2 10.2 %all-to-all-start.3 = ((bf16[4,128,256]{2,1,0:T(8,128)(2,1)}), bf16[4,128,256]{2,1,0:T(8,128)(2,1)S(1)}, u32[]{:S(2)}, u32[]{:S(2)}) async-start(bf16[4,128,256]{2,1,0:T(8,128)(2,1)} %broadcast_in_dim.38), calls=%async_computation.3 | async-start | bytes 524288 | tf_op jit(solution)/shard_map/all_to_all | solution.py:276
  45.3 27.5 %copy-start = (bf16[4,128,256]{2,1,0:T(8,128)(2,1)}, bf16[4,128,256]{2,1,0:T(8,128)(2,1)S(1)}, u32[]{:S(2)}) copy-start(bf16[4,128,256]{2,1,0:T(8,128)(2,1)S(1)} %all-to-all-done.3.refs_2_) | copy-start | bytes 786436
  46.1 10.2 %all-to-all-start.1 = ((bf16[4,128,256]{2,1,0:T(8,128)(2,1)}), bf16[4,128,256]{2,1,0:T(8,128)(2,1)S(1)}, u32[]{:S(2)}, u32[]{:S(2)}) async-start(bf16[4,128,256]{2,1,0:T(8,128)(2,1)} %broadcast_in_dim.37), calls=%async_computation.1 | async-start | bytes 524288 | tf_op jit(solution)/shard_map/all_to_all | solution.py:276
  56.3 16.5 %copy-start.1 = (bf16[4,128,256]{2,1,0:T(8,128)(2,1)}, bf16[4,128,256]{2,1,0:T(8,128)(2,1)S(1)}, u32[]{:S(2)}) copy-start(bf16[4,128,256]{2,1,0:T(8,128)(2,1)S(1)} %all-to-all-done.1.refs_0_) | copy-start | bytes 786436
  56.3 12.7 %all-to-all-start.4 = ((f32[8,128,64]{1,2,0:T(8,128)}), f32[8,128,64]{1,2,0:T(8,128)S(1)}, u32[]{:S(2)}, u32[]{:S(2)}) async-start(f32[8,128,64]{1,2,0:T(8,128)} %copy.9), calls=%async_computation.4 | async-start | bytes 524288 | tf_op jit(solution)/shard_map/all_to_all | solution.py:276
  60.6 9.3 %collective-permute-start = (bf16[4,128,256]{2,1,0:T(8,128)(2,1)S(1)}, bf16[4,128,256]{2,1,0:T(8,128)(2,1)S(1)}, u32[]{:S(2)}, u32[]{:S(2)}) collective-permute-start(bf16[4,128,256]{2,1,0:T(8,128)(2,1)S(1)} %all-to-all-done.1.refs_0_), channel_id=1, source_target_pairs={{0,2},{2,0},{1,3},{3,1},{4,6},{6,4},{5,7},{7,5},{8,10},{10,8},{9,1... | collective-permute-start | bytes 786440 | tf_op jit(solution)/shard_map/ppermute | solution.py:23
  62.7 10.1 %collective-permute-start.1 = (bf16[4,128,256]{2,1,0:T(8,128)(2,1)S(1)}, bf16[4,128,256]{2,1,0:T(8,128)(2,1)S(1)}, u32[]{:S(2)}, u32[]{:S(2)}) collective-permute-start(bf16[4,128,256]{2,1,0:T(8,128)(2,1)S(1)} %all-to-all-done.3.refs_2_), channel_id=1, source_target_pairs={{0,2},{2,0},{1,3},{3,1},{4,6},{6,4},{5,7},{7,5},{8,10},{10,8},{9,1... | collective-permute-start | bytes 786440 | tf_op jit(solution)/shard_map/ppermute | solution.py:23
  70.0 2.8 %copy-start.2 = (bf16[4,128,256]{2,1,0:T(8,128)(2,1)}, bf16[4,128,256]{2,1,0:T(8,128)(2,1)S(1)}, u32[]{:S(2)}) copy-start(bf16[4,128,256]{2,1,0:T(8,128)(2,1)S(1)} %collective-permute-done.refs_1_) | copy-start | bytes 786436
  72.8 0.7 copy-start.3

commit v3 on v2

v3 whole, which is shorter than its diff:
```python
import functools

import jax
import jax.numpy as jnp
from jax import lax
from jax.experimental import pallas as pl
from jax.experimental.pallas import tpu as pltpu
from jax.sharding import PartitionSpec as P

LEN = 1024
ITERS = 6
DAMPING = 0.1
NT = (((1,), (1,)), ((), ()))
VMEM_BYTES = 56 * 1024 * 1024


def whole_spec(shape):
    zeros = (0,) * len(shape)
    return pl.BlockSpec(shape, lambda *_: zeros)


def swap(value, axes, size, offset):
    return lax.ppermute(value, axes, [(i, i ^ offset) for i in range(size)])


def encode(value):
    return (value * jnp.abs(value)).astype(jnp.bfloat16)


def decode(code):
    wide = code.astype(jnp.float32)
    root = jnp.sqrt(jnp.abs(wide))
    return jnp.where(wide < 0, -root, root)


def project_kernel(ways, *refs):
    inputs, grads = refs[:ways], refs[ways : 2 * ways]
    proj_in, proj_out, out = refs[2 * ways :]
    rows = inputs[0].shape[0]
    for w in range(ways):
        x = lax.dot_general(inputs[w][...], proj_in[...], NT, preferred_element_type=jnp.float32)
        g = lax.dot_general(grads[w][...], proj_out[...], NT, preferred_element_type=jnp.float32)
        both = jnp.concatenate([x, g], axis=1).T
        out[0, :, w * rows : (w + 1) * rows] = encode(both)


def project(inputs, grads, proj_in, proj_out, parts):
    rank, features = proj_in.shape
    hidden = proj_out.shape[1]
    tokens = inputs.shape[0]
    block = tokens // parts
    tile = min(block, 256)
    split = block // tile
    ways = tile // 128

    def rows(way):
        return lambda step: (step * ways + way, 0)

    return pl.pallas_call(
        functools.partial(project_kernel, ways),
        grid=(parts * split,),
        in_specs=[pl.BlockSpec((128, features), rows(w)) for w in range(ways)]
        + [pl.BlockSpec((128, hidden), rows(w)) for w in range(ways)]
        + [whole_spec(proj_in.shape), whole_spec(proj_out.shape)],
        out_specs=pl.BlockSpec(
            (1, 2 * rank, tile), lambda step: (step // split, 0, lax.rem(step, split))
        ),
        out_shape=jax.ShapeDtypeStruct((parts, 2 * rank, block), jnp.bfloat16),
        compiler_params=pltpu.CompilerParams(vmem_limit_bytes=VMEM_BYTES),
        cost_estimate=pl.CostEstimate(
            flops=2 * tokens * (features + hidden) * rank,
            bytes_accessed=2 * tokens * (features + hidden),
            transcendentals=0,
        ),
        name="project",
    )(*[inputs] * ways, *[grads] * ways, proj_in, proj_out)


def split_queries_kernel(queries, out):
    owners, rank, width = out.shape
    cols = queries.shape[1] // owners
    for i in range(width // cols):
        rows = queries[i * rank : (i + 1) * rank, :]
        for k in range(owners):
            out[k, :, i * cols : (i + 1) * cols] = rows[:, k * cols : (k + 1) * cols]


def split_queries(queries, owners, rank):
    rows, total = queries.shape
    shape = (owners, rank, (rows // rank) * (total // owners))
    return pl.pallas_call(
        split_queries_kernel,
        out_shape=jax.ShapeDtypeStruct(shape, jnp.float32),
        compiler_params=pltpu.CompilerParams(vmem_limit_bytes=VMEM_BYTES),
        name="split_queries",
    )(queries)


def solve_kernel(tokens, span, count, place, *refs):
    pieces = refs[:count]
    queries, scores, out, x_s, g_s, pair, direction, residual, image, sums = refs[count:]
    cols, side, rank = direction.shape
    chunks, _, wide = x_s.shape
    parts, _, block = pieces[0].shape
    for n in range(count * parts):
        piece = pieces[n // parts]
        c, at = divmod(n * block, wide)
        x_s[c, :, at : at + block] = piece[n % parts, :rank, :].astype(jnp.float32)
        g = piece[n % parts, rank:, :]
        g_s[c, :rank, at : at + block] = g
        g_s[c, rank:, at : at + block] = g
    mine = queries.shape[2] // cols
    for k in range(queries.shape[0]):
        turned = queries[k].T
        for i in range(mine):
            direction[:, k * mine + i, :] = turned[i * cols : (i + 1) * cols, :]
    residual[...] = direction[...]

    def total(value):
        return jnp.sum(jnp.sum(value, axis=1, keepdims=True), axis=2, keepdims=True)

    def forward(c):
        w = jnp.dot(pair[...], g_s[c], preferred_element_type=jnp.float32)
        x = x_s[c][None]
        return jnp.sum(w.reshape(cols, side, wide) * x, axis=1, keepdims=True), x

    def prepare():
        d = direction[...]
        high = d.astype(jnp.bfloat16)
        low = (d - high.astype(jnp.float32)).astype(jnp.bfloat16)
        pair[...] = jnp.concatenate([high, low], axis=2).reshape(cols * side, 2 * rank)
        sums[...] = jnp.zeros_like(sums)
        return total(d * d)

    def step_size(norm, length, energy):
        energy = jnp.sum(energy, axis=2, keepdims=True)
        return norm / (energy * (1.0 / tokens) + DAMPING * length)

    def fold(c, u):
        sums[c * wide // span] += jnp.sum(u, axis=2, keepdims=True)

    out[...] = jnp.zeros_like(out)

    def one_step(_, norm):
        length = prepare()
        energy = jnp.zeros((cols, 1, wide), jnp.float32)
        for c in range(chunks):
            u, x = forward(c)
            spread = (u * x).astype(jnp.bfloat16).reshape(cols * side, wide)
            part = lax.dot_general(
                spread, g_s[c, :rank, :], NT, preferred_element_type=jnp.float32
            ).reshape(cols, side, rank)
            image[...] = part if c == 0 else image[...] + part
            fold(c, u)
            energy = energy + u * u
        alpha = step_size(norm, length, energy)
        out[...] += alpha[None] * sums[...]
        d = direction[...]
        r = residual[...] - alpha * (image[...] * (1.0 / tokens) + DAMPING * d)
        residual[...] = r
        later = total(r * r)
        direction[...] = r + later / norm * d
        return later

    norm = lax.fori_loop(0, ITERS - 1, one_step, total(residual[...] * residual[...]))
    length = prepare()
    energy = jnp.zeros((cols, 1, wide), jnp.float32)
    for c in range(chunks):
        u, _ = forward(c)
        fold(c, u)
        energy = energy + u * u
    out[...] += step_size(norm, length, energy)[None] * sums[...]

    scores[...] = jnp.zeros_like(scores)
    lane = lax.broadcasted_iota(jnp.int32, (cols, 1, 128), 2)
    column = lax.broadcasted_iota(jnp.int32, (cols, 1, 128), 0) + place[0] * cols
    for n in range(tokens // span):
        row = jnp.sum(jnp.where(lane == column, out[n], 0.0), axis=0) * (1.0 / LEN)
        at = pl.ds(place[1 + n], 1)
        scores[0, at, :] += row
    for k in range(1, scores.shape[0]):
        scores[k] = scores[0]


def solve(place, pieces, queries, tokens, span, devices):
    owners, rank, width = queries.shape
    side = rank
    cols = owners * width // side
    wide = min(512, span)
    count = len(pieces)
    vectors = pltpu.VMEM((cols, side, rank), jnp.float32)
    sums = (tokens // span, cols, 1, 128)
    return pl.pallas_call(
        functools.partial(solve_kernel, tokens, span, count),
        in_specs=[pl.BlockSpec(memory_space=pltpu.SMEM)]
        + [pl.BlockSpec(memory_space=pltpu.VMEM)] * (count + 1),
        out_specs=pl.BlockSpec(memory_space=pltpu.VMEM),
        out_shape=jax.ShapeDtypeStruct((devices, tokens // LEN, 128), jnp.float32),
        scratch_shapes=[
            pltpu.VMEM(sums, jnp.float32),
            pltpu.VMEM((tokens // wide, rank, wide), jnp.float32),
            pltpu.VMEM((tokens // wide, 2 * rank, wide), jnp.bfloat16),
            pltpu.VMEM((cols * side, 2 * rank), jnp.bfloat16),
            vectors,
            vectors,
            vectors,
            pltpu.VMEM(sums, jnp.float32),
        ],
        compiler_params=pltpu.CompilerParams(vmem_limit_bytes=VMEM_BYTES),
        cost_estimate=pl.CostEstimate(
            flops=2 * 2 * ITERS * 4 * tokens * cols * side * rank,
            bytes_accessed=4 * tokens * rank,
            transcendentals=0,
        ),
        name="solve",
    )(place, *pieces, queries)


def hessian_kernel(tokens, count, first, last, place, *refs):
    pieces = refs[:count]
    before = None if first else refs[count]
    out, x_s, g_s, own, even, odd = refs[-6:]
    step = pl.program_id(0)
    steps = pl.num_programs(0)
    rank = x_s.shape[0]
    parts, _, block = pieces[0].shape
    rows = out.shape[0]
    columns = even.shape[0]

    def vectors(i):
        return x_s[pl.ds(i, 1), :].astype(jnp.bfloat16) * g_s[...]

    def form(target, tile):
        for j in range(columns // rank):
            target[j * rank : (j + 1) * rank, :] = vectors(tile * (columns // rank) + j)

    def product(source, half):
        at = slice(half * columns, (half + 1) * columns)
        gram = lax.dot_general(own[...], source[...], NT, preferred_element_type=jnp.float32)
        if not first:
            gram = gram + before[:, at]
        if last:
            shape = (rows, columns)
            row = lax.broadcasted_iota(jnp.int32, shape, 0) + place[0] * rows
            column = lax.broadcasted_iota(jnp.int32, shape, 1) + (2 * step + half) * columns
            gram = gram * (1.0 / tokens) + jnp.where(row == column, DAMPING, 0.0)
        out[:, at] = gram

    @pl.when(step == 0)
    def _():
        for n in range(count * parts):
            piece = pieces[n // parts]
            at = slice(n * block, (n + 1) * block)
            x_s[:, at] = piece[n % parts, :rank, :].astype(jnp.float32)
            g_s[:, at] = piece[n % parts, rank:, :]
        for i in range(rows // rank):
            own[i * rank : (i + 1) * rank, :] = vectors(place[0] * (rows // rank) + i)
        form(even, 0)

    form(odd, 2 * step + 1)
    product(even, 0)
    form(even, lax.rem(2 * step + 2, 2 * steps))
    product(odd, 1)


def hessian_rows(place, pieces, tokens, rows, before, last):
    rank = pieces[0].shape[1] // 2
    count = len(pieces)
    width = rank * rank
    columns = 256
    here = count * pieces[0].shape[0] * pieces[0].shape[2]
    first = before is None
    tile = pl.BlockSpec((rows, 2 * columns), lambda step: (0, step))
    return pl.pallas_call(
        functools.partial(hessian_kernel, tokens, count, first, last),
        grid=(width // (2 * columns),),
        in_specs=[pl.BlockSpec(memory_space=pltpu.SMEM)]
        + [whole_spec(pieces[0].shape)] * count
        + ([] if first else [tile]),
        out_specs=tile,
        out_shape=jax.ShapeDtypeStruct((rows, width), jnp.float32),
        scratch_shapes=[
            pltpu.VMEM((rank, here), jnp.float32),
            pltpu.VMEM((rank, here), jnp.bfloat16),
            pltpu.VMEM((rows, here), jnp.bfloat16),
            pltpu.VMEM((columns, here), jnp.bfloat16),
            pltpu.VMEM((columns, here), jnp.bfloat16),
        ],
        input_output_aliases={} if first else {1 + count: 0},
        compiler_params=pltpu.CompilerParams(vmem_limit_bytes=VMEM_BYTES),
        cost_estimate=pl.CostEstimate(
            flops=2 * rows * width * here,
            bytes_accessed=(1 if first else 2) * 4 * rows * width,
            transcendentals=0,
        ),
        name="hessian_first" if first else "hessian_rest",
    )(place, *pieces, *([] if first else [before]))


def shards(layer_input, out_grads, proj_in, proj_out, queries):
    rank = proj_in.shape[2]
    parts, dp_size, pipe_size = (lax.axis_size(a) for a in ("tensor", "dp", "pipe"))
    owners = parts * dp_size
    tok_dev = layer_input.shape[0]
    owned = queries.shape[1]
    dp_pos = lax.axis_index("dp").astype(jnp.int32)
    owner = lax.axis_index("tensor").astype(jnp.int32) * dp_size + dp_pos
    tokens = tok_dev * dp_size

    def exchange(value, axes):
        return lax.all_to_all(value, axes, 0, 0, tiled=True)

    columns = exchange(split_queries(queries[0], owners, rank), ("tensor", "dp"))
    partial = project(layer_input, out_grads[0], proj_in[0].T, proj_out[0].T, parts)
    columns, partial = lax.optimization_barrier((columns, partial))
    summed = jnp.sum(decode(exchange(partial, "tensor")), axis=0).astype(jnp.bfloat16)
    near = exchange(jnp.broadcast_to(summed, (parts,) + summed.shape), "tensor")
    far = [swap(near, "dp", dp_size, k) for k in range(1, dp_size)]

    span = min(tok_dev, LEN)
    rows = [
        (dp_pos ^ k) * (tok_dev // LEN) + at * span // LEN
        for k in range(dp_size)
        for at in range(tok_dev // span)
    ]
    place = jnp.stack([owner] + rows)

    begun = hessian_rows(place, [near], tokens, owned, None, not far)
    if far:
        begun, *far = lax.optimization_barrier((begun, *far))
    shares = solve(place, [near, *far], columns, tokens, span, owners * pipe_size)
    scores = jnp.sum(exchange(shares, ("tensor", "dp", "pipe")), axis=0)
    if far:
        begun = hessian_rows(place, far, tokens, owned, begun, True)
    return (begun[None], scores)


def solution(mesh):
    in_specs = (
        P(("groups", "dp"), "tensor"),
        P("pipe", ("groups", "dp"), "tensor"),
        P("pipe", "tensor", None),
        P("pipe", "tensor", None),
        P("pipe", ("tensor", "dp"), None),
    )
    out_specs = (P("pipe", ("groups", "tensor", "dp"), None), P("groups", None))
    return jax.shard_map(shards, mesh=mesh, in_specs=in_specs, out_specs=out_specs, check_vma=False)
```

time: 149 us -> 124 us (0.83)
  waiting for transfers between devices: 28.1 us -> 12.9 us
  starting transfers between devices: 23 us -> 15.7 us
  local copies, waits for them, and re-layouts: 6.19 us -> 2.3 us
  Pallas kernels: 68.2 us -> 71.8 us
  blocking collectives: 20.6 us -> 19 us
    all_gather x1 -> x0, blocking collectives: 20.6 us -> none  [shards(): lax.all_gather(placed, ('tensor', 'dp', 'pipe'), axis=0)]
    all_to_all x0 -> x1, blocking collectives: none -> 19 us  [exchange(): return lax.all_to_all(value, axes, 0, 0, tiled=True)]
    all_to_all x5 -> x3, waiting for transfers between devices: 25.3 us -> 12.8 us  [exchange(): return lax.all_to_all(value, axes, 0, 0, tiled=True)]
    all_to_all x5 -> x3, starting transfers between devices: 20.9 us -> 14.2 us  [exchange(): return lax.all_to_all(value, axes, 0, 0, tiled=True)]
    pallas_call x4, Pallas kernels: 66.1 us -> 69.6 us  [the longest x1 29.6 us: solve(): pl.pallas_call(functools.partial(solve_kernel, tokens, span, count), in_s...]
    ppermute x2 -> x1, waiting for transfers between devices: 2.82 us -> 0.01 us  [swap(): return lax.ppermute(value, axes, [(i, i ^ offset) for i in range(size)])]
    reshape x1 -> x0, local copies, waits for them, and re-layouts: 1.91 us -> none  [shards(): flat = split.reshape(owners, split.shape[1] * split.shape[2], rank)]
  transfers between devices with their start and end apart: 7 -> 4, of which waited for: 6 -> 1; matrix products, arithmetic and copies ran while one was open for 2% -> 1% of each run, Pallas kernels for 6% -> 32%
where the time goes in v3:
time: 124 us; the launch traced here: 123 us
  Pallas kernels  71.8 us (58%)
  blocking collectives  19 us (15%)
  starting transfers between devices  15.7 us (13%)
  waiting for transfers between devices  12.9 us (10%)
  local copies, waits for them, and re-layouts  2.3 us (2%)
    pallas_call x1, Pallas kernels, solve(): pl.pallas_call(functools.partial(solve_kernel, tokens, span, count), in_s...  29.6 us
    pallas_call x2, Pallas kernels, hessian_rows(): pl.pallas_call(functools.partial(hessian_kernel, tokens, count, first, la...  27.6 us
    all_to_all x1, blocking collectives, exchange(): return lax.all_to_all(value, axes, 0, 0, tiled=True)  19 us
    all_to_all x3, starting transfers between devices, exchange(): return lax.all_to_all(value, axes, 0, 0, tiled=True)  14.2 us
    all_to_all x3, waiting for transfers between devices, exchange(): return lax.all_to_all(value, axes, 0, 0, tiled=True)  12.8 us
    pallas_call x1, Pallas kernels, project(): pl.pallas_call(functools.partial(project_kernel, ways), grid=(parts * spl...  12.4 us
  transfers between devices with their start and end apart: 4, of which 1 were waited for; matrix products, arithmetic and copies ran while one was open for 1% of the time, Pallas kernels for 32%

profile of v3, /device:TPU:0, one launch (start us, length us, event | category | flops | bytes accessed | tf_op | source)
XLA Modules:
  0.0 123.4 jit_solution(899057933015196398)
XLA Ops:
  0.6 2.2 %split_queries.1 = f32[8,64,128]{2,1,0:T(8,128)} custom-call(f32[512,128]{1,0:T(8,128)} %bitcast.17), custom_call_target="tpu_custom_call" | custom-call | tf_op jit(solution)/shard_map/split_queries/pallas_call | solution.py:91
  2.8 7.3 %all-to-all-start = ((f32[8,64,128]{2,1,0:T(8,128)}), f32[8,64,128]{2,1,0:T(8,128)S(1)}, u32[]{:S(2)}, u32[]{:S(2)}) async-start(f32[8,64,128]{2,1,0:T(8,128)} %split_queries.1), calls=%async_computation | async-start | bytes 524288 | tf_op jit(solution)/shard_map/all_to_all | solution.py:311
  10.1 12.4 %project.1 = bf16[4,128,512]{2,1,0:T(8,128)(2,1)} custom-call(bf16[2048,1024]{1,0:T(8,128)(2,1)} %refs_1_.1, bf16[2048,1024]{1,0:T(8,128)(2,1)} %refs_1_.1, bf16[2048,3584]{1,0:T(8,128)(2,1)} %bitcast.14, bf16[2048,3584]{1,0:T(8,128)(2,1)} %bitcast.15, bf16[64,1024]{1,0:T(8,128)(2,1)} %bitcast.18, bf16[64,3584]{1,0:T(8,128)(2,1)} %bitcast.16), custom_call_target="tpu_custom_call" | custom-call | flops 1207959552 | bytes 18874368 | tf_op jit(solution)/shard_map/project/pallas_call | solution.py:59
  22.4 0.0 all-to-all-done.refs_2_
  22.5 0.0 copy-start.1
  22.5 19.0 %all_to_all.20 = bf16[4,128,512]{2,1,0:T(8,128)(2,1)S(1)} all-to-all(bf16[4,128,512]{2,1,0:T(8,128)(2,1)} %project.1), channel_id=1, replica_groups=mesh['groups'=2,'tensor'=4,'dp'=2,'pipe'=2] {'tensor'}, dimensions={0} | all-to-all | bytes 1048576 | tf_op jit(solution)/shard_map/all_to_all | solution.py:311
  41.5 0.5 fusion.1
  42.0 0.8 broadcast_in_dim.6
  42.8 3.5 %all-to-all-start.2 = ((bf16[4,128,512]{2,1,0:T(8,128)(2,1)}), bf16[4,128,512]{2,1,0:T(8,128)(2,1)S(1)}, u32[]{:S(2)}, u32[]{:S(2)}) async-start(bf16[4,128,512]{2,1,0:T(8,128)(2,1)} %broadcast_in_dim.6), calls=%async_computation.2 | async-start | bytes 1048576 | tf_op jit(solution)/shard_map/all_to_all | solution.py:311
  46.3 0.7 stack.23.place
  46.9 12.8 %all-to-all-done.2.refs_0_ = bf16[4,128,512]{2,1,0:T(8,128)(2,1)S(1)} async-done(((bf16[4,128,512]{2,1,0:T(8,128)(2,1)}), bf16[4,128,512]{2,1,0:T(8,128)(2,1)S(1)}, u32[]{:S(2)}, u32[]{:S(2)}) %all-to-all-start.2) | async-done | bytes 524320 | tf_op jit(solution)/shard_map/all_to_all | solution.py:311
  59.8 0.0 copy-start
  59.8 1.5 %collective-permute-start = (bf16[4,128,512]{2,1,0:T(8,128)(2,1)S(1)}, bf16[4,128,512]{2,1,0:T(8,128)(2,1)S(1)}, u32[]{:S(2)}, u32[]{:S(2)}) collective-permute-start(bf16[4,128,512]{2,1,0:T(8,128)(2,1)S(1)} %all-to-all-done.2.refs_0_), channel_id=1, source_target_pairs={{0,2},{2,0},{1,3},{3,1},{4,6},{6,4},{5,7},{7,5},{8,10},{10,8},{9,1... | collective-permute-start | bytes 1572872 | tf_op jit(solution)/shard_map/ppermute | solution.py:23
  61.2 0.0 copy-done
  61.2 13.1 %hessian_first.1.refs_1_ = f32[512,4096]{1,0:T(8,128)} custom-call(s32[5]{0:T(128)} %stack.23.place, bf16[4,128,512]{2,1,0:T(8,128)(2,1)} %copy-done), custom_call_target="tpu_custom_call" | custom-call | flops 8589934592 | bytes 8388608 | tf_op jit(solution)/shard_map/hessian_first/pallas_call | solution.py:274
  74.4 0.0 copy-done.1
  74.4 0.0 collective-permute-done.refs_0_.refs_1_
  74.4 0.0 copy-start.2
  74.4 0.8 copy-done.2
  75.2 29.6 %solve.1 = f32[16,4,128]{2,1,0:T(4,128)} custom-call(s32[5]{0:T(128)} %stack.23.place, bf16[4,128,512]{2,1,0:T(8,128)(2,1)} %copy-done, bf16[4,128,512]{2,1,0:T(8,128)(2,1)} %copy-done.2, f32[8,64,128]{2,1,0:T(8,128)} %copy-done.1), custom_call_target="tpu_custom_call" | custom-call | flops 25769803776 | bytes 1048576 | tf_op jit(solution)/shard_map/solve/pallas_call | solution.py:193
  104.8 3.5 %all-to-all-start.3 = ((f32[16,4,128]{2,1,0:T(4,128)}), f32[16,4,128]{2,1,0:T(4,128)S(1)}, u32[]{:S(2)}, u32[]{:S(2)}) async-start(f32[16,4,128]{2,1,0:T(4,128)} %solve.1), calls=%async_computation.3 | async-start | bytes 65536 | tf_op jit(solution)/shard_map/all_to_all | solution.py:311
  108.3 14.5 %hessian_rest.1 = f32[512,4096]{1,0:T(8,128)} custom-call(s32[5]{0:T(128)} %stack.23.place, bf16[4,128,512]{2,1,0:T(8,128)(2,1)} %copy-done.2, f32[512,4096]{1,0:T(8,128)} %hessian_first.1.refs_1_), custom_call_target="tpu_custom_call", output_to_operand_aliasing={{}: (2, {})} | custom-call | flops 8589934592 | bytes 16777216 | tf_op jit(solution)/shard_map/hessian_rest/pallas_call | solution.py:274
  122.8 0.0 all-to-all-done.3
  122.8 0.6 reduce_sum.19
Async XLA Ops:
  2.8 19.6 %all-to-all-start = ((f32[8,64,128]{2,1,0:T(8,128)}), f32[8,64,128]{2,1,0:T(8,128)S(1)}, u32[]{:S(2)}, u32[]{:S(2)}) async-start(f32[8,64,128]{2,1,0:T(8,128)} %split_queries.1), calls=%async_computation | async-start | bytes 524288 | tf_op jit(solution)/shard_map/all_to_all | solution.py:311
  22.5 51.9 %copy-start.1 = (f32[8,64,128]{2,1,0:T(8,128)}, f32[8,64,128]{2,1,0:T(8,128)S(1)}, u32[]{:S(2)}) copy-start(f32[8,64,128]{2,1,0:T(8,128)S(1)} %all-to-all-done.refs_2_) | copy-start | bytes 786436
  42.8 17.0 %all-to-all-start.2 = ((bf16[4,128,512]{2,1,0:T(8,128)(2,1)}), bf16[4,128,512]{2,1,0:T(8,128)(2,1)S(1)}, u32[]{:S(2)}, u32[]{:S(2)}) async-start(bf16[4,128,512]{2,1,0:T(8,128)(2,1)} %broadcast_in_dim.6), calls=%async_computation.2 | async-start | bytes 1048576 | tf_op jit(solution)/shard_map/all_to_all | solution.py:311
  59.8 1.5 %copy-start = (bf16[4,128,512]{2,1,0:T(8,128)(2,1)}, bf16[4,128,512]{2,1,0:T(8,128)(2,1)S(1)}, u32[]{:S(2)}) copy-start(bf16[4,128,512]{2,1,0:T(8,128)(2,1)S(1)} %all-to-all-done.2.refs_0_) | copy-start | bytes 1572868
  59.8 14.6 %collective-permute-start = (bf16[4,128,512]{2,1,0:T(8,128)(2,1)S(1)}, bf16[4,128,512]{2,1,0:T(8,128)(2,1)S(1)}, u32[]{:S(2)}, u32[]{:S(2)}) collective-permute-start(bf16[4,128,512]{2,1,0:T(8,128)(2,1)S(1)} %all-to-all-done.2.refs_0_), channel_id=1, source_target_pairs={{0,2},{2,0},{1,3},{3,1},{4,6},{6,4},{5,7},{7,5},{8,10},{10,8},{9,1... | collective-permute-start | bytes 1572872 | tf_op jit(solution)/shard_map/ppermute | solution.py:23
  74.4 0.8 copy-start.2
  104.8 18.0 %all-to-all-start.3 = ((f32[16,4,128]{2,1,0:T(4,128)}), f32[16,4,128]{2,1,0:T(4,128)S(1)}, u32[]{:S(2)}, u32[]{:S(2)}) async-start(f32[16,4,128]{2,1,0:T(4,128)} %solve.1), calls=%async_computation.3 | async-start | bytes 65536 | tf_op jit(solution)/shard_map/all_to_all | solution.py:311

commit v4 on v3

v4 whole, which is shorter than its diff:
```python
import functools

import jax
import jax.numpy as jnp
from jax import lax
from jax.experimental import pallas as pl
from jax.experimental.pallas import tpu as pltpu
from jax.sharding import PartitionSpec as P

LEN = 1024
ITERS = 6
DAMPING = 0.1
NT = (((1,), (1,)), ((), ()))
VMEM_BYTES = 56 * 1024 * 1024


def whole_spec(shape):
    zeros = (0,) * len(shape)
    return pl.BlockSpec(shape, lambda *_: zeros)


def swap(value, axes, size, offset):
    return lax.ppermute(value, axes, [(i, i ^ offset) for i in range(size)])


def encode(value):
    return (value * jnp.abs(value)).astype(jnp.bfloat16)


def decode(code):
    wide = code.astype(jnp.float32)
    root = jnp.sqrt(jnp.abs(wide))
    return jnp.where(wide < 0, -root, root)


def order(position, count, first):
    bits = (count - 1).bit_length()
    offset = first
    for b in range(bits):
        bit = lax.shift_right_logical(position, jnp.int32(bits - 1 - b)) & 1
        offset = offset + bit * (2 << b)
    return offset


def project_kernel(sent, count, narrow, place, *refs):
    inputs, grads = refs[:count], refs[count : 2 * count]
    proj_in, proj_out = refs[2 * count : 2 * count + 2]
    rest = refs[2 * count + 2 :]
    queries, out, split, sums = (None, rest[0], None, rest[1]) if sent else rest
    step = pl.program_id(0)
    rank = proj_in.shape[0]

    def product(left, right):
        return lax.dot_general(left[...], right[...], NT, preferred_element_type=jnp.float32)

    @pl.when(step == 0)
    def _():
        sums[...] = jnp.zeros_like(sums)
        if not sent:
            split_queries(queries, split)

    for n in range(count):
        sums[n, rank:, :] += product(proj_out, grads[n])

    @pl.when(step < narrow)
    def _():
        for n in range(count):
            sums[n, :rank, :] += product(proj_in, inputs[n])

    @pl.when(step == pl.num_programs(0) - 1)
    def _():
        out[...] = encode(sums[...]) if sent else sums[...]


def split_queries(queries, out):
    owners, rank, width = out.shape
    cols = queries.shape[1] // owners
    for i in range(width // cols):
        rows = queries[i * rank : (i + 1) * rank, :]
        for k in range(owners):
            out[k, :, i * cols : (i + 1) * cols] = rows[:, k * cols : (k + 1) * cols]


def project(place, inputs, grads, proj_in, proj_out, parts, queries=None, owners=1):
    sent = queries is None
    rank, features = proj_in.shape
    hidden = proj_out.shape[1]
    block = inputs.shape[0] // parts
    count = parts // 2
    depth = next(d for d in (512, 256, 128) if features % d == 0 and hidden % d == 0)
    narrow = features // depth

    def part(n, place):
        return lax.bitwise_xor(place[0], order(jnp.int32(n), count, 1 if sent else 0))

    def chunk(n, last):
        return lambda step, place: (part(n, place), jnp.minimum(step, last))

    wide = [pl.BlockSpec((block, depth), chunk(n, hidden // depth - 1)) for n in range(count)]
    thin = [pl.BlockSpec((block, depth), chunk(n, narrow - 1)) for n in range(count)]
    shape = (count, 2 * rank, block)
    out_shape = [jax.ShapeDtypeStruct(shape, jnp.bfloat16 if sent else jnp.float32)]
    if not sent:
        cut = (owners, rank, queries.size // (rank * owners))
        out_shape.append(jax.ShapeDtypeStruct(cut, jnp.float32))
    return pl.pallas_call(
        functools.partial(project_kernel, sent, count, narrow),
        grid_spec=pltpu.PrefetchScalarGridSpec(
            num_scalar_prefetch=1,
            grid=(hidden // depth,),
            in_specs=thin
            + wide
            + [
                pl.BlockSpec((rank, depth), lambda step, place: (0, jnp.minimum(step, narrow - 1))),
                pl.BlockSpec((rank, depth), lambda step, place: (0, step)),
            ]
            + ([] if sent else [whole_spec(queries.shape)]),
            out_specs=[whole_spec(o.shape) for o in out_shape],
            scratch_shapes=[pltpu.VMEM(shape, jnp.float32)],
        ),
        out_shape=out_shape,
        compiler_params=pltpu.CompilerParams(vmem_limit_bytes=VMEM_BYTES),
        cost_estimate=pl.CostEstimate(
            flops=2 * count * block * (features + hidden) * rank,
            bytes_accessed=2 * count * block * (features + hidden),
            transcendentals=0,
        ),
        name="project_sent" if sent else "project_kept",
    )(
        place,
        *[inputs] * count,
        *[grads] * count,
        proj_in,
        proj_out,
        *([] if sent else [queries]),
    )


def solve_kernel(tokens, count, parts_at, place, apart, *refs):
    pieces = refs[:count]
    queries, scores, kept, x_s, g_s, pair, direction, residual, image, sums = refs[count:]
    side, cols, rank = direction.shape
    chunks, _, wide = x_s.shape
    each, _, block = pieces[0].shape
    owners, _, width = queries.shape
    mine = side // owners
    real = width // mine
    for c in range(chunks):
        n, at = divmod(c * wide, block)
        piece = pieces[n // each]
        x_s[c] = piece[n % each, :rank, at : at + wide].astype(jnp.float32)
        g = piece[n % each, rank:, at : at + wide]
        g_s[c, :rank, :] = g
        g_s[c, rank:, :] = g
    if real < cols:
        direction[...] = jnp.zeros_like(direction)
    for k in range(owners):
        turned = queries[k].T
        for i in range(mine):
            direction[k * mine + i, :real, :] = turned[i * real : (i + 1) * real, :]
    residual[...] = direction[...]
    together = 256 // cols
    groups = side // together
    lanes = [slice(k, k + min(256, wide)) for k in range(0, wide, 256)]

    def total(value):
        return jnp.sum(jnp.sum(value, axis=0), axis=1, keepdims=True)

    def rows(group):
        return slice(group * together * cols, (group + 1) * together * cols)

    def features(group):
        return range(group * together, (group + 1) * together)

    def collect(c, group, us):
        sums_of = []
        for at, u in zip(lanes, us):
            w = jnp.dot(pair[rows(group), :], g_s[c, :, at], preferred_element_type=jnp.float32)
            for n, i in enumerate(features(group)):
                u = u + w[n * cols : (n + 1) * cols, :] * x_s[c, i : i + 1, at]
            sums_of.append(u)
        return sums_of

    def spread(c, group, us):
        part = 0.0
        for at, u in zip(lanes, us):
            terms = [(u * x_s[c, i : i + 1, at]).astype(jnp.bfloat16) for i in features(group)]
            part = part + lax.dot_general(
                g_s[c, :rank, at],
                jnp.concatenate(terms, axis=0),
                NT,
                preferred_element_type=jnp.float32,
            )
        image[:, rows(group)] = part if c == 0 else image[:, rows(group)] + part

    def fold(value):
        width = value[0].shape[1]
        return functools.reduce(
            jnp.add, [v[:, k : k + 128] for v in value for k in range(0, width, 128)]
        )

    def apply(back):
        d = direction[...]
        high = d.astype(jnp.bfloat16)
        low = (d - high.astype(jnp.float32)).astype(jnp.bfloat16)
        pair[...] = jnp.concatenate([high, low], axis=2).reshape(side * cols, 2 * rank)
        energy = jnp.zeros((cols, 128), jnp.float32)
        zeros = [jnp.zeros((cols, at.stop - at.start), jnp.float32) for at in lanes]
        later = zeros
        for group in range(groups):
            later = collect(0, group, later)
        for c in range(chunks):
            us, later = later, zeros
            for group in range(groups):
                if c + 1 < chunks:
                    later = collect(c + 1, group, later)
                if back:
                    spread(c, group, us)
            sums[c] = fold(us)
            energy = energy + fold([u * u for u in us])
        return total(d * d), jnp.sum(energy, axis=1, keepdims=True)

    def advance(norm, length, energy):
        alpha = norm / (energy * (1.0 / tokens) + DAMPING * length)
        for c in range(chunks):
            kept[c] += alpha * sums[c]
        return alpha

    kept[...] = jnp.zeros_like(kept)

    def one_step(_, norm):
        alpha = advance(norm, *apply(True))
        d = direction[...]
        turned = image[...].T.reshape(side, cols, rank)
        r = residual[...] - alpha * (turned * (1.0 / tokens) + DAMPING * d)
        residual[...] = r
        later = total(r * r)
        direction[...] = r + later / norm * d
        return later

    norm = lax.fori_loop(0, ITERS - 1, one_step, total(residual[...] * residual[...]))
    advance(norm, *apply(False))

    scores[...] = jnp.zeros_like(scores)
    lane = lax.broadcasted_iota(jnp.int32, (cols, 128), 1)
    column = lax.broadcasted_iota(jnp.int32, (cols, 128), 0)
    owner = place[0] * (owners // parts_at[1]) + apart[0]
    here = (lane == column + owner * real) & (column < real)
    for c in range(chunks):
        n, at = divmod(c * wide, block)
        away, k = parts_at[0][n]
        example = lax.bitwise_xor(apart[0], away) * parts_at[2] + lax.div(
            lax.bitwise_xor(place[0], k) * block + at, LEN
        )
        value = jnp.sum(kept[c], axis=1, keepdims=True) * (1.0 / LEN)
        row = jnp.sum(jnp.where(here, value, 0.0), axis=0, keepdims=True)
        scores[0, pl.ds(example, 1), :] += row
    for k in range(1, scores.shape[0]):
        scores[k] = scores[0]


def solve(place, apart, pieces, where, queries, tokens, examples, parts, devices):
    owners, rank, width = queries.shape
    cols = max(owners * width // rank, 16)
    count, block = len(pieces), pieces[0].shape[2]
    wide = min(512, block)
    chunks = tokens // wide
    vectors = pltpu.VMEM((rank, cols, rank), jnp.float32)
    sums = pltpu.VMEM((chunks, cols, 128), jnp.float32)
    smem = pl.BlockSpec(memory_space=pltpu.SMEM)
    dp_size = owners // parts
    return pl.pallas_call(
        functools.partial(solve_kernel, tokens, count, (where, parts, examples // dp_size)),
        in_specs=[smem, smem] + [pl.BlockSpec(memory_space=pltpu.VMEM)] * (count + 1),
        out_specs=pl.BlockSpec(memory_space=pltpu.VMEM),
        out_shape=jax.ShapeDtypeStruct((devices, examples, 128), jnp.float32),
        scratch_shapes=[
            sums,
            pltpu.VMEM((chunks, rank, wide), jnp.float32),
            pltpu.VMEM((chunks, 2 * rank, wide), jnp.bfloat16),
            pltpu.VMEM((rank * cols, 2 * rank), jnp.bfloat16),
            vectors,
            vectors,
            pltpu.VMEM((rank, rank * cols), jnp.float32),
            sums,
        ],
        compiler_params=pltpu.CompilerParams(vmem_limit_bytes=VMEM_BYTES),
        cost_estimate=pl.CostEstimate(
            flops=2 * 2 * ITERS * 4 * tokens * cols * rank * rank,
            bytes_accessed=4 * tokens * rank,
            transcendentals=0,
        ),
        name="solve",
    )(place, apart, *pieces, queries)


def hessian_kernel(tokens, count, dp_size, first, last, place, apart, *refs):
    pieces = refs[:count]
    before = None if first else refs[count]
    out, x_s, g_s, own, even, odd = refs[-6:]
    step = pl.program_id(0)
    steps = pl.num_programs(0)
    rank = x_s.shape[0]
    each, _, block = pieces[0].shape
    rows = out.shape[0]
    columns = even.shape[0]
    first_row = (place[0] * dp_size + apart[0]) * rows

    def vectors(i):
        return x_s[pl.ds(i, 1), :].astype(jnp.bfloat16) * g_s[...]

    def form(target, tile):
        for j in range(columns // rank):
            target[j * rank : (j + 1) * rank, :] = vectors(tile * (columns // rank) + j)

    def product(source, half):
        at = slice(half * columns, (half + 1) * columns)
        gram = lax.dot_general(own[...], source[...], NT, preferred_element_type=jnp.float32)
        if not first:
            gram = gram + before[:, at]
        if last:
            shape = (rows, columns)
            row = lax.broadcasted_iota(jnp.int32, shape, 0) + first_row
            column = lax.broadcasted_iota(jnp.int32, shape, 1) + (2 * step + half) * columns
            gram = gram * (1.0 / tokens) + jnp.where(row == column, DAMPING, 0.0)
        out[:, at] = gram

    @pl.when(step == 0)
    def _():
        for n in range(count * each):
            at = slice(n * block, (n + 1) * block)
            x_s[:, at] = pieces[n // each][n % each, :rank, :].astype(jnp.float32)
            g_s[:, at] = pieces[n // each][n % each, rank:, :]
        for i in range(rows // rank):
            own[i * rank : (i + 1) * rank, :] = vectors(first_row // rank + i)
        form(even, 0)

    form(odd, 2 * step + 1)
    product(even, 0)
    form(even, lax.rem(2 * step + 2, 2 * steps))
    product(odd, 1)


def hessian_rows(place, apart, dp_size, pieces, tokens, rows, before, last):
    rank = pieces[0].shape[1] // 2
    count = len(pieces)
    width = rank * rank
    columns = 256
    here = count * pieces[0].shape[0] * pieces[0].shape[2]
    first = before is None
    tile = pl.BlockSpec((rows, 2 * columns), lambda step: (0, step))
    return pl.pallas_call(
        functools.partial(hessian_kernel, tokens, count, dp_size, first, last),
        grid=(width // (2 * columns),),
        in_specs=[pl.BlockSpec(memory_space=pltpu.SMEM)] * 2
        + [whole_spec(pieces[0].shape)] * count
        + ([] if first else [tile]),
        out_specs=tile,
        out_shape=jax.ShapeDtypeStruct((rows, width), jnp.float32),
        scratch_shapes=[
            pltpu.VMEM((rank, here), jnp.float32),
            pltpu.VMEM((rank, here), jnp.bfloat16),
            pltpu.VMEM((rows, here), jnp.bfloat16),
            pltpu.VMEM((columns, here), jnp.bfloat16),
            pltpu.VMEM((columns, here), jnp.bfloat16),
        ],
        input_output_aliases={} if first else {2 + count: 0},
        compiler_params=pltpu.CompilerParams(vmem_limit_bytes=VMEM_BYTES),
        cost_estimate=pl.CostEstimate(
            flops=2 * rows * width * here,
            bytes_accessed=(1 if first else 2) * 4 * rows * width,
            transcendentals=0,
        ),
        name="hessian_begin" if first else "hessian_end" if last else "hessian_more",
    )(place, apart, *pieces, *([] if first else [before]))


def shards(layer_input, out_grads, proj_in, proj_out, queries):
    rank = proj_in.shape[2]
    parts, dp_size, pipe_size = (lax.axis_size(a) for a in ("tensor", "dp", "pipe"))
    owners = parts * dp_size
    tok_dev = layer_input.shape[0]
    owned = queries.shape[1]
    place = lax.axis_index("tensor").astype(jnp.int32).reshape(1)
    apart = lax.axis_index("dp").astype(jnp.int32).reshape(1)
    tokens = tok_dev * dp_size

    operands = (place, layer_input, out_grads[0], proj_in[0].T, proj_out[0].T, parts)
    (sent,) = project(*operands)
    sent = swap(sent, "tensor", parts, 1)
    total, cut = project(*operands, queries[0], owners)
    total = total + decode(sent)
    offset = 2
    while 2 * offset < parts:
        half = total.shape[0] // 2
        total = total[:half] + decode(swap(encode(total[half:]), "tensor", parts, offset))
        offset *= 2
    other = decode(swap(encode(total), "tensor", parts, offset))
    near = [jnp.stack([total[0] + other[1], total[1] + other[0]]).astype(jnp.bfloat16)]
    at = [[0, offset]]
    cut, near[0] = lax.optimization_barrier((cut, near[0]))
    columns = lax.all_to_all(cut, ("tensor", "dp"), 0, 0, tiled=True)

    while offset > 1:
        offset //= 2
        if offset < parts // 2:
            near = near + [swap(piece, "tensor", parts, offset) for piece in near]
            at = at + [[k ^ offset for k in ks] for ks in at]
    far = [swap(piece, "dp", dp_size, k) for k in range(1, dp_size) for piece in near]
    where = [(k, part) for k in range(dp_size) for ks in at for part in ks]

    def rows(pieces, begun, last):
        return hessian_rows(place, apart, dp_size, pieces, tokens, owned, begun, last)

    begun = rows(near[:1], None, False)
    begun = rows(near[1:], begun, not far)
    begun, columns, *far = lax.optimization_barrier((begun, columns, *far))
    examples = tokens // LEN
    devices = owners * pipe_size
    shares = solve(
        place, apart, near + far, where, columns, tokens, examples, parts, devices
    )
    shares = lax.all_to_all(shares, ("tensor", "dp", "pipe"), 0, 0, tiled=True)
    scores = jnp.sum(shares, axis=0)
    if far:
        begun = rows(far, begun, True)
    return (begun[None], scores)


def solution(mesh):
    in_specs = (
        P(("groups", "dp"), "tensor"),
        P("pipe", ("groups", "dp"), "tensor"),
        P("pipe", "tensor", None),
        P("pipe", "tensor", None),
        P("pipe", ("tensor", "dp"), None),
    )
    out_specs = (P("pipe", ("groups", "tensor", "dp"), None), P("groups", None))
    return jax.shard_map(shards, mesh=mesh, in_specs=in_specs, out_specs=out_specs, check_vma=False)
```

time: 124 us -> 122 us (0.984)
  blocking collectives: 19 us -> 0 us
  Pallas kernels: 71.8 us -> 86.3 us
  starting transfers between devices: 15.7 us -> 18.5 us
  waiting for transfers between devices: 12.9 us -> 11.6 us
    all_to_all x1 -> x0, blocking collectives: 19 us -> none  [exchange(): return lax.all_to_all(value, axes, 0, 0, tiled=True)]
    pallas_call x5 -> x6, Pallas kernels: 71.8 us -> 86.3 us  [the longest x3 34.7 us: hessian_rows(): pl.pallas_call(functools.partial(hessian_kernel, tokens, count, dp_size,...]
    all_to_all x3 -> x2, waiting for transfers between devices: 12.8 us -> 0.01 us  [the longest x1 0.01 us: shards(): columns = lax.all_to_all(cut, ('tensor', 'dp'), 0, 0, tiled=True)]
    ppermute x1 -> x5, waiting for transfers between devices: 0.01 us -> 11.6 us  [swap(): return lax.ppermute(value, axes, [(i, i ^ offset) for i in range(size)])]
    ppermute x1 -> x5, starting transfers between devices: 1.46 us -> 9.34 us  [swap(): return lax.ppermute(value, axes, [(i, i ^ offset) for i in range(size)])]
    all_to_all x3 -> x2, starting transfers between devices: 14.2 us -> 9.15 us  [the longest x1 4.8 us: shards(): shares = lax.all_to_all(shares, ('tensor', 'dp', 'pipe'), 0, 0, tiled=True)]
    convert_element_type x0 -> x1, other arithmetic: none -> 1.31 us  [encode(): return (value * jnp.abs(value)).astype(jnp.bfloat16)]
  transfers between devices with their start and end apart: 4 -> 7, of which waited for: 1 -> 1; matrix products, arithmetic and copies ran while one was open for 1% -> 0% of each run, Pallas kernels for 32% -> 37%
where the time goes in v4:
time: 122 us; the launch traced here: 121 us
  Pallas kernels  86.3 us (71%)
  starting transfers between devices  18.5 us (15%)
  waiting for transfers between devices  11.6 us (10%)
  other arithmetic  2.25 us (2%)
  local copies, waits for them, and re-layouts  1.49 us (1%)
    pallas_call x3, Pallas kernels, hessian_rows(): pl.pallas_call(functools.partial(hessian_kernel, tokens, count, dp_size,...  34.7 us
    pallas_call x1, Pallas kernels, solve(): pl.pallas_call(functools.partial(solve_kernel, tokens, count, (where, par...  33.7 us
    pallas_call x2, Pallas kernels, project(): pl.pallas_call(functools.partial(project_kernel, sent, count, narrow), gr...  17.9 us
    ppermute x5, waiting for transfers between devices, swap(): return lax.ppermute(value, axes, [(i, i ^ offset) for i in range(size)])  11.6 us
    ppermute x5, starting transfers between devices, swap(): return lax.ppermute(value, axes, [(i, i ^ offset) for i in range(size)])  9.34 us
    all_to_all x1, starting transfers between devices, shards(): shares = lax.all_to_all(shares, ('tensor', 'dp', 'pipe'), 0, 0, tiled=True)  4.8 us
    all_to_all x1, starting transfers between devices, shards(): columns = lax.all_to_all(cut, ('tensor', 'dp'), 0, 0, tiled=True)  4.35 us
  transfers between devices with their start and end apart: 7, of which 1 were waited for; matrix products, arithmetic and copies ran while one was open for 0% of the time, Pallas kernels for 37%

profile of v4, /device:TPU:0, one launch (start us, length us, event | category | flops | bytes accessed | tf_op | source)
XLA Modules:
  0.0 120.8 jit_solution(8016561486128982629)
XLA Ops:
  0.6 8.4 %project_sent.1 = bf16[2,128,512]{2,1,0:T(8,128)(2,1)} custom-call(s32[1]{0:T(128)} %bitcast.place, bf16[2048,1024]{1,0:T(8,128)(2,1)} %refs_1_.3, bf16[2048,1024]{1,0:T(8,128)(2,1)} %refs_1_.3, bf16[2048,3584]{1,0:T(8,128)(2,1)} %bitcast.11, bf16[2048,3584]{1,0:T(8,128)(2,1)} %bitcast.12, bf16[64,1024]{1,0:T(8,128)(2,1)} %bitcast.18, bf16[64,3584]{1,0:T(8,128)(2,1)} %bitcast.16), custom_call_target="tpu_custom_call" | custom-call | flops 603979776 | bytes 9437184 | tf_op jit(solution)/shard_map/project_sent/pallas_call | solution.py:106
  9.1 3.0 %collective-permute-start = (bf16[2,128,512]{2,1,0:T(8,128)(2,1)}, bf16[2,128,512]{2,1,0:T(8,128)(2,1)S(1)}, u32[]{:S(2)}, u32[]{:S(2)}) collective-permute-start(bf16[2,128,512]{2,1,0:T(8,128)(2,1)} %project_sent.1), channel_id=1, source_target_pairs={{0,4},{4,0},{8,12},{12,8},{1,5},{5,1},{9,13},{13,9},{2,6},{6,2},{1... | collective-permute-start | bytes 786440 | tf_op jit(solution)/shard_map/ppermute | solution.py:23
  12.1 9.5 %project_kept.1 = (f32[2,128,512]{2,1,0:T(8,128)}, f32[8,64,128]{2,1,0:T(8,128)}) custom-call(s32[1]{0:T(128)} %bitcast.place, bf16[2048,1024]{1,0:T(8,128)(2,1)} %refs_1_.3, bf16[2048,1024]{1,0:T(8,128)(2,1)} %refs_1_.3, bf16[2048,3584]{1,0:T(8,128)(2,1)} %bitcast.13, bf16[2048,3584]{1,0:T(8,128)(2,1)} %bitcast.14, bf16[64,1024]{1,0:T(8,128)(2,1)} %bitcast.19, ...), custom_call_target="tpu_custom_call" | custom-call | flops 603979776 | bytes 9437184 | tf_op jit(solution)/shard_map/project_kept/pallas_call | solution.py:106
  21.6 0.0 collective-permute-done
  21.6 1.3 %fusion.3 = (bf16[2,128,512]{2,1,0:T(8,128)(2,1)S(1)}, f32[2,128,512]{2,1,0:T(8,128)S(1)}) fusion(f32[2,128,512]{2,1,0:T(8,128)} %get-tuple-element.11, bf16[2,128,512]{2,1,0:T(8,128)(2,1)S(1)} %collective-permute-done), kind=kLoop, calls=%fused_computation.10 | loop fusion | flops 1179648 | bytes 1572864 | tf_op jit(solution)/shard_map/convert_element_type | solution.py:27
  22.9 2.7 %collective-permute-start.1 = (bf16[2,128,512]{2,1,0:T(8,128)(2,1)S(1)}, bf16[2,128,512]{2,1,0:T(8,128)(2,1)S(1)}, u32[]{:S(2)}, u32[]{:S(2)}) collective-permute-start(bf16[2,128,512]{2,1,0:T(8,128)(2,1)S(1)} %get-tuple-element.18), channel_id=1, source_target_pairs={{0,8},{4,12},{8,0},{12,4},{1,9},{5,13},{9,1},{13,5},{2,10},{6,14},... | collective-permute-start | bytes 786440 | tf_op jit(solution)/shard_map/ppermute | solution.py:23
  25.5 11.5 %collective-permute-done.1 = bf16[2,128,512]{2,1,0:T(8,128)(2,1)S(1)} collective-permute-done((bf16[2,128,512]{2,1,0:T(8,128)(2,1)S(1)}, bf16[2,128,512]{2,1,0:T(8,128)(2,1)S(1)}, u32[]{:S(2)}, u32[]{:S(2)}) %collective-permute-start.1) | collective-permute-done | bytes 262176 | tf_op jit(solution)/shard_map/ppermute | solution.py:23
  37.1 0.2 negate_select_fusion
  37.3 0.1 fusion.5
  37.5 0.0 copy-start.1
  37.5 0.1 collective-permute-start.2
  37.5 1.6 %collective-permute-start.3 = (bf16[2,128,512]{2,1,0:T(8,128)(2,1)S(1)}, bf16[2,128,512]{2,1,0:T(8,128)(2,1)S(1)}, u32[]{:S(2)}, u32[]{:S(2)}) collective-permute-start(bf16[2,128,512]{2,1,0:T(8,128)(2,1)S(1)} %pad_maximum_fusion.refs_0_), channel_id=1, source_target_pairs={{0,2},{2,0},{1,3},{3,1},{4,6},{6,4},{5,7},{7,5},{8,10},{10,8},{9,1... | collective-permute-start | bytes 786440 | tf_op jit(solution)/shard_map/ppermute | solution.py:23
  39.1 4.3 %all-to-all-start = ((f32[8,64,128]{2,1,0:T(8,128)}), f32[8,64,128]{2,1,0:T(8,128)S(1)}, u32[]{:S(2)}, u32[]{:S(2)}) async-start(f32[8,64,128]{2,1,0:T(8,128)} %get-tuple-element.13), calls=%async_computation | async-start | bytes 524288 | tf_op jit(solution)/shard_map/all_to_all | solution.py:402
  43.5 0.0 copy-done.1
  43.5 8.9 %hessian_begin.1.refs_1_ = f32[512,4096]{1,0:T(8,128)} custom-call(s32[1]{0:T(128)} %bitcast.place, s32[1]{0:T(128)} %bitcast.1.apart, bf16[2,128,512]{2,1,0:T(8,128)(2,1)} %copy-done.1), custom_call_target="tpu_custom_call" | custom-call | flops 4294967296 | bytes 8388608 | tf_op jit(solution)/shard_map/hessian_begin/pallas_call | solution.py:352
  52.4 0.0 collective-permute-done.2.refs_0_.refs_1_
  52.4 0.0 copy-start
  52.4 2.0 %collective-permute-start.4 = (bf16[2,128,512]{2,1,0:T(8,128)(2,1)S(1)}, bf16[2,128,512]{2,1,0:T(8,128)(2,1)S(1)}, u32[]{:S(2)}, u32[]{:S(2)}) collective-permute-start(bf16[2,128,512]{2,1,0:T(8,128)(2,1)S(1)} %collective-permute-done.2.refs_0_.refs_1_), channel_id=1, source_target_pairs={{0,2},{2,0},{1,3},{3,1},{4,6},{6,4},{5,7},{7,5},{8,10},{10,8},{9,1... | collective-permute-start | bytes 786440 | tf_op jit(solution)/shard_map/ppermute | solution.py:23
  54.4 0.0 copy-done
  54.4 11.4 %hessian_more.1.refs_2_ = f32[512,4096]{1,0:T(8,128)} custom-call(s32[1]{0:T(128)} %bitcast.place, s32[1]{0:T(128)} %bitcast.1.apart, bf16[2,128,512]{2,1,0:T(8,128)(2,1)} %copy-done, f32[512,4096]{1,0:T(8,128)} %hessian_begin.1.refs_1_), custom_call_target="tpu_custom_call", output_to_operand_aliasing={{}: (3, {})} | custom-call | flops 4294967296 | bytes 16777216 | tf_op jit(solution)/shard_map/hessian_more/pallas_call | solution.py:352
  65.8 0.0 collective-permute-done.3.refs_0_.refs_2_
  65.8 0.0 copy-start.3
  65.8 0.0 all-to-all-done.refs_4_
  65.8 0.0 copy-start.2
  65.8 0.0 collective-permute-done.4.refs_1_.refs_3_
  65.8 0.7 copy-done.3
  66.5 0.1 copy-done.2
  66.6 0.0 copy-start.4
  66.6 0.7 copy-done.4
  67.3 33.7 %solve.1 = f32[16,4,128]{2,1,0:T(4,128)} custom-call(s32[1]{0:T(128)} %bitcast.place, s32[1]{0:T(128)} %bitcast.1.apart, bf16[2,128,512]{2,1,0:T(8,128)(2,1)} %copy-done.1, bf16[2,128,512]{2,1,0:T(8,128)(2,1)} %copy-done, bf16[2,128,512]{2,1,0:T(8,128)(2,1)} %copy-done.3, bf16[2,128,512]{2,1,0:T(8,128)(2,1)} %copy-done.4, f32[8,64,128]{2,1,0:T(8,128)} %copy-done.2), custom_call_target="tpu_custom_call" | custom-call | flops 25769803776 | bytes 1048576 | tf_op jit(solution)/shard_map/solve/pallas_call | solution.py:272
  100.9 4.8 %all-to-all-start.1 = ((f32[16,4,128]{2,1,0:T(4,128)}), f32[16,4,128]{2,1,0:T(4,128)S(1)}, u32[]{:S(2)}, u32[]{:S(2)}) async-start(f32[16,4,128]{2,1,0:T(4,128)} %solve.1), calls=%async_computation.1 | async-start | bytes 65536 | tf_op jit(solution)/shard_map/all_to_all | solution.py:423
  105.7 14.5 %hessian_end.1 = f32[512,4096]{1,0:T(8,128)} custom-call(s32[1]{0:T(128)} %bitcast.place, s32[1]{0:T(128)} %bitcast.1.apart, bf16[2,128,512]{2,1,0:T(8,128)(2,1)} %copy-done.3, bf16[2,128,512]{2,1,0:T(8,128)(2,1)} %copy-done.4, f32[512,4096]{1,0:T(8,128)} %hessian_more.1.refs_2_), custom_call_target="tpu_custom_call", output_to_operand_aliasing={{}: (4, {})} | custom-call | flops 8589934592 | bytes 16777216 | tf_op jit(solution)/shard_map/hessian_end/pallas_call | solution.py:352
  120.2 0.0 all-to-all-done.1
  120.2 0.6 reduce_sum.9
  (1 shorter events, 0.0 us)
Async XLA Ops:
  9.1 12.5 %collective-permute-start = (bf16[2,128,512]{2,1,0:T(8,128)(2,1)}, bf16[2,128,512]{2,1,0:T(8,128)(2,1)S(1)}, u32[]{:S(2)}, u32[]{:S(2)}) collective-permute-start(bf16[2,128,512]{2,1,0:T(8,128)(2,1)} %project_sent.1), channel_id=1, source_target_pairs={{0,4},{4,0},{8,12},{12,8},{1,5},{5,1},{9,13},{13,9},{2,6},{6,2},{1... | collective-permute-start | bytes 786440 | tf_op jit(solution)/shard_map/ppermute | solution.py:23
  22.9 14.2 %collective-permute-start.1 = (bf16[2,128,512]{2,1,0:T(8,128)(2,1)S(1)}, bf16[2,128,512]{2,1,0:T(8,128)(2,1)S(1)}, u32[]{:S(2)}, u32[]{:S(2)}) collective-permute-start(bf16[2,128,512]{2,1,0:T(8,128)(2,1)S(1)} %get-tuple-element.18), channel_id=1, source_target_pairs={{0,8},{4,12},{8,0},{12,4},{1,9},{5,13},{9,1},{13,5},{2,10},{6,14},... | collective-permute-start | bytes 786440 | tf_op jit(solution)/shard_map/ppermute | solution.py:23
  37.5 6.0 %copy-start.1 = (bf16[2,128,512]{2,1,0:T(8,128)(2,1)}, bf16[2,128,512]{2,1,0:T(8,128)(2,1)S(1)}, u32[]{:S(2)}) copy-start(bf16[2,128,512]{2,1,0:T(8,128)(2,1)S(1)} %pad_maximum_fusion.refs_0_) | copy-start | bytes 786436
  37.5 14.9 %collective-permute-start.2 = (bf16[2,128,512]{2,1,0:T(8,128)(2,1)S(1)}, bf16[2,128,512]{2,1,0:T(8,128)(2,1)S(1)}, u32[]{:S(2)}, u32[]{:S(2)}) collective-permute-start(bf16[2,128,512]{2,1,0:T(8,128)(2,1)S(1)} %pad_maximum_fusion.refs_0_), channel_id=1, source_target_pairs={{0,4},{4,0},{8,12},{12,8},{1,5},{5,1},{9,13},{13,9},{2,6},{6,2},{1... | collective-permute-start | bytes 786440 | tf_op jit(solution)/shard_map/ppermute | solution.py:23
  37.5 28.2 %collective-permute-start.3 = (bf16[2,128,512]{2,1,0:T(8,128)(2,1)S(1)}, bf16[2,128,512]{2,1,0:T(8,128)(2,1)S(1)}, u32[]{:S(2)}, u32[]{:S(2)}) collective-permute-start(bf16[2,128,512]{2,1,0:T(8,128)(2,1)S(1)} %pad_maximum_fusion.refs_0_), channel_id=1, source_target_pairs={{0,2},{2,0},{1,3},{3,1},{4,6},{6,4},{5,7},{7,5},{8,10},{10,8},{9,1... | collective-permute-start | bytes 786440 | tf_op jit(solution)/shard_map/ppermute | solution.py:23
  39.1 26.6 %all-to-all-start = ((f32[8,64,128]{2,1,0:T(8,128)}), f32[8,64,128]{2,1,0:T(8,128)S(1)}, u32[]{:S(2)}, u32[]{:S(2)}) async-start(f32[8,64,128]{2,1,0:T(8,128)} %get-tuple-element.13), calls=%async_computation | async-start | bytes 524288 | tf_op jit(solution)/shard_map/all_to_all | solution.py:402
  52.4 2.0 %copy-start = (bf16[2,128,512]{2,1,0:T(8,128)(2,1)}, bf16[2,128,512]{2,1,0:T(8,128)(2,1)S(1)}, u32[]{:S(2)}) copy-start(bf16[2,128,512]{2,1,0:T(8,128)(2,1)S(1)} %collective-permute-done.2.refs_0_.refs_1_) | copy-start | bytes 786436
  52.4 13.4 %collective-permute-start.4 = (bf16[2,128,512]{2,1,0:T(8,128)(2,1)S(1)}, bf16[2,128,512]{2,1,0:T(8,128)(2,1)S(1)}, u32[]{:S(2)}, u32[]{:S(2)}) collective-permute-start(bf16[2,128,512]{2,1,0:T(8,128)(2,1)S(1)} %collective-permute-done.2.refs_0_.refs_1_), channel_id=1, source_target_pairs={{0,2},{2,0},{1,3},{3,1},{4,6},{6,4},{5,7},{7,5},{8,10},{10,8},{9,1... | collective-permute-start | bytes 786440 | tf_op jit(solution)/shard_map/ppermute | solution.py:23
  65.8 0.7 copy-start.3
  65.8 0.8 copy-start.2
  66.6 0.7 copy-start.4
  100.9 19.3 %all-to-all-start.1 = ((f32[16,4,128]{2,1,0:T(4,128)}), f32[16,4,128]{2,1,0:T(4,128)S(1)}, u32[]{:S(2)}, u32[]{:S(2)}) async-start(f32[16,4,128]{2,1,0:T(4,128)} %solve.1), calls=%async_computation.1 | async-start | bytes 65536 | tf_op jit(solution)/shard_map/all_to_all | solution.py:423

commit v5 on v4

--- a/solution.py
+++ b/solution.py
@@ -42,37 +42,55 @@
     return offset
 
 
-def project_kernel(sent, count, narrow, place, *refs):
-    inputs, grads = refs[:count], refs[count : 2 * count]
-    proj_in, proj_out = refs[2 * count : 2 * count + 2]
-    rest = refs[2 * count + 2 :]
-    queries, out, split, sums = (None, rest[0], None, rest[1]) if sent else rest
-    step = pl.program_id(0)
-    rank = proj_in.shape[0]
-
-    def product(left, right):
-        return lax.dot_general(left[...], right[...], NT, preferred_element_type=jnp.float32)
-
-    @pl.when(step == 0)
-    def _():
-        sums[...] = jnp.zeros_like(sums)
-        if not sent:
-            split_queries(queries, split)
-
-    for n in range(count):
-        sums[n, rank:, :] += product(proj_out, grads[n])
-
-    @pl.when(step < narrow)
-    def _():
-        for n in range(count):
-            sums[n, :rank, :] += product(proj_in, inputs[n])
-
-    @pl.when(step == pl.num_programs(0) - 1)
-    def _():
-        out[...] = encode(sums[...]) if sent else sums[...]
-
-
-def split_queries(queries, out):
+def project_kernel(sent, place, inputs, grads, proj_in, proj_out, out):
+    x = lax.dot_general(proj_in[...], inputs[...], NT, preferred_element_type=jnp.float32)
+    g = lax.dot_general(proj_out[...], grads[...], NT, preferred_element_type=jnp.float32)
+    rank = x.shape[0]
+    out[0, :rank, :] = encode(x) if sent else x
+    out[0, rank:, :] = encode(g) if sent else g
+
+
+def project(place, inputs, grads, proj_in, proj_out, parts, sent):
+    rank, features = proj_in.shape
+    hidden = proj_out.shape[1]
+    block = inputs.shape[0] // parts
+    tile = min(block, 256)
+    split = block // tile
+    count = parts // 2
+
+    def rows(step, place):
+        part = lax.bitwise_xor(place[0], order(step // split, count, 1 if sent else 0))
+        return (part * split + lax.rem(step, split), 0)
+
+    return pl.pallas_call(
+        functools.partial(project_kernel, sent),
+        grid_spec=pltpu.PrefetchScalarGridSpec(
+            num_scalar_prefetch=1,
+            grid=(count * split,),
+            in_specs=[
+                pl.BlockSpec((tile, features), rows),
+                pl.BlockSpec((tile, hidden), rows),
+                whole_spec(proj_in.shape),
+                whole_spec(proj_out.shape),
+            ],
+            out_specs=pl.BlockSpec(
+                (1, 2 * rank, tile), lambda step, place: (step // split, 0, lax.rem(step, split))
+            ),
+        ),
+        out_shape=jax.ShapeDtypeStruct(
+            (count, 2 * rank, block), jnp.bfloat16 if sent else jnp.float32
+        ),
+        compiler_params=pltpu.CompilerParams(vmem_limit_bytes=VMEM_BYTES),
+        cost_estimate=pl.CostEstimate(
+            flops=2 * count * block * (features + hidden) * rank,
+            bytes_accessed=2 * count * block * (features + hidden),
+            transcendentals=0,
+        ),
+        name="project_sent" if sent else "project_kept",
+    )(place, inputs, grads, proj_in, proj_out)
+
+
+def split_queries_kernel(queries, out):
     owners, rank, width = out.shape
     cols = queries.shape[1] // owners
     for i in range(width // cols):
@@ -81,64 +99,22 @@
             out[k, :, i * cols : (i + 1) * cols] = rows[:, k * cols : (k + 1) * cols]
 
 
-def project(place, inputs, grads, proj_in, proj_out, parts, queries=None, owners=1):
-    sent = queries is None
-    rank, features = proj_in.shape
-    hidden = proj_out.shape[1]
-    block = inputs.shape[0] // parts
-    count = parts // 2
-    depth = next(d for d in (512, 256, 128) if features % d == 0 and hidden % d == 0)
-    narrow = features // depth
-
-    def part(n, place):
-        return lax.bitwise_xor(place[0], order(jnp.int32(n), count, 1 if sent else 0))
-
-    def chunk(n, last):
-        return lambda step, place: (part(n, place), jnp.minimum(step, last))
-
-    wide = [pl.BlockSpec((block, depth), chunk(n, hidden // depth - 1)) for n in range(count)]
-    thin = [pl.BlockSpec((block, depth), chunk(n, narrow - 1)) for n in range(count)]
-    shape = (count, 2 * rank, block)
-    out_shape = [jax.ShapeDtypeStruct(shape, jnp.bfloat16 if sent else jnp.float32)]
-    if not sent:
-        cut = (owners, rank, queries.size // (rank * owners))
-        out_shape.append(jax.ShapeDtypeStruct(cut, jnp.float32))
+def split_queries(queries, owners, rank):
+    rows, total = queries.shape
+    shape = (owners, rank, (rows // rank) * (total // owners))
     return pl.pallas_call(
-        functools.partial(project_kernel, sent, count, narrow),
-        grid_spec=pltpu.PrefetchScalarGridSpec(
-            num_scalar_prefetch=1,
-            grid=(hidden // depth,),
-            in_specs=thin
-            + wide
-            + [
-                pl.BlockSpec((rank, depth), lambda step, place: (0, jnp.minimum(step, narrow - 1))),
-                pl.BlockSpec((rank, depth), lambda step, place: (0, step)),
-            ]
-            + ([] if sent else [whole_spec(queries.shape)]),
-            out_specs=[whole_spec(o.shape) for o in out_shape],
-            scratch_shapes=[pltpu.VMEM(shape, jnp.float32)],
-        ),
-        out_shape=out_shape,
+        split_queries_kernel,
+        out_shape=jax.ShapeDtypeStruct(shape, jnp.float32),
         compiler_params=pltpu.CompilerParams(vmem_limit_bytes=VMEM_BYTES),
-        cost_estimate=pl.CostEstimate(
-            flops=2 * count * block * (features + hidden) * rank,
-            bytes_accessed=2 * count * block * (features + hidden),
-            transcendentals=0,
-        ),
-        name="project_sent" if sent else "project_kept",
-    )(
-        place,
-        *[inputs] * count,
-        *[grads] * count,
-        proj_in,
-        proj_out,
-        *([] if sent else [queries]),
-    )
+        name="split_queries",
+    )(queries)
 
 
 def solve_kernel(tokens, count, parts_at, place, apart, *refs):
     pieces = refs[:count]
-    queries, scores, kept, x_s, g_s, pair, direction, residual, image, sums = refs[count:]
+    queries, scores, kept, x_s, g_s, pair, direction, residual, image, sums, w_even, w_odd = refs[
+        count:
+    ]
     side, cols, rank = direction.shape
     chunks, _, wide = x_s.shape
     each, _, block = pieces[0].shape
@@ -159,45 +135,32 @@
         for i in range(mine):
             direction[k * mine + i, :real, :] = turned[i * real : (i + 1) * real, :]
     residual[...] = direction[...]
-    together = 256 // cols
-    groups = side // together
-    lanes = [slice(k, k + min(256, wide)) for k in range(0, wide, 256)]
+    bank = (w_even, w_odd)
 
     def total(value):
         return jnp.sum(jnp.sum(value, axis=0), axis=1, keepdims=True)
 
-    def rows(group):
-        return slice(group * together * cols, (group + 1) * together * cols)
-
-    def features(group):
-        return range(group * together, (group + 1) * together)
-
-    def collect(c, group, us):
-        sums_of = []
-        for at, u in zip(lanes, us):
-            w = jnp.dot(pair[rows(group), :], g_s[c, :, at], preferred_element_type=jnp.float32)
-            for n, i in enumerate(features(group)):
-                u = u + w[n * cols : (n + 1) * cols, :] * x_s[c, i : i + 1, at]
-            sums_of.append(u)
-        return sums_of
-
-    def spread(c, group, us):
-        part = 0.0
-        for at, u in zip(lanes, us):
-            terms = [(u * x_s[c, i : i + 1, at]).astype(jnp.bfloat16) for i in features(group)]
-            part = part + lax.dot_general(
-                g_s[c, :rank, at],
-                jnp.concatenate(terms, axis=0),
-                NT,
-                preferred_element_type=jnp.float32,
-            )
-        image[:, rows(group)] = part if c == 0 else image[:, rows(group)] + part
+    def expand(c):
+        bank[c % 2][...] = jnp.dot(pair[...], g_s[c], preferred_element_type=jnp.float32)
+
+    def collect(c):
+        u = jnp.zeros((cols, wide), jnp.float32)
+        for i in range(side):
+            u = u + bank[c % 2][i * cols : (i + 1) * cols, :] * x_s[c, i : i + 1, :]
+        return u
+
+    def spread(c, u):
+        terms = [(u * x_s[c, i : i + 1, :]).astype(jnp.bfloat16) for i in range(side)]
+        part = lax.dot_general(
+            jnp.concatenate(terms, axis=0),
+            g_s[c, :rank, :],
+            NT,
+            preferred_element_type=jnp.float32,
+        ).reshape(side, cols, rank)
+        image[...] = part if c == 0 else image[...] + part
 
     def fold(value):
-        width = value[0].shape[1]
-        return functools.reduce(
-            jnp.add, [v[:, k : k + 128] for v in value for k in range(0, width, 128)]
-        )
+        return functools.reduce(jnp.add, [value[:, k : k + 128] for k in range(0, wide, 128)])
 
     def apply(back):
         d = direction[...]
@@ -205,19 +168,15 @@
         low = (d - high.astype(jnp.float32)).astype(jnp.bfloat16)
         pair[...] = jnp.concatenate([high, low], axis=2).reshape(side * cols, 2 * rank)
         energy = jnp.zeros((cols, 128), jnp.float32)
-        zeros = [jnp.zeros((cols, at.stop - at.start), jnp.float32) for at in lanes]
-        later = zeros
-        for group in range(groups):
-            later = collect(0, group, later)
+        expand(0)
         for c in range(chunks):
-            us, later = later, zeros
-            for group in range(groups):
-                if c + 1 < chunks:
-                    later = collect(c + 1, group, later)
-                if back:
-                    spread(c, group, us)
-            sums[c] = fold(us)
-            energy = energy + fold([u * u for u in us])
+            if c + 1 < chunks:
+                expand(c + 1)
+            u = collect(c)
+            if back:
+                spread(c, u)
+            sums[c] = fold(u)
+            energy = energy + fold(u * u)
         return total(d * d), jnp.sum(energy, axis=1, keepdims=True)
 
     def advance(norm, length, energy):
@@ -231,8 +190,7 @@
     def one_step(_, norm):
         alpha = advance(norm, *apply(True))
         d = direction[...]
-        turned = image[...].T.reshape(side, cols, rank)
-        r = residual[...] - alpha * (turned * (1.0 / tokens) + DAMPING * d)
+        r = residual[...] - alpha * (image[...] * (1.0 / tokens) + DAMPING * d)
         residual[...] = r
         later = total(r * r)
         direction[...] = r + later / norm * d
@@ -267,6 +225,7 @@
     chunks = tokens // wide
     vectors = pltpu.VMEM((rank, cols, rank), jnp.float32)
     sums = pltpu.VMEM((chunks, cols, 128), jnp.float32)
+    product = pltpu.VMEM((rank * cols, wide), jnp.float32)
     smem = pl.BlockSpec(memory_space=pltpu.SMEM)
     dp_size = owners // parts
     return pl.pallas_call(
@@ -281,8 +240,10 @@
             pltpu.VMEM((rank * cols, 2 * rank), jnp.bfloat16),
             vectors,
             vectors,
-            pltpu.VMEM((rank, rank * cols), jnp.float32),
+            vectors,
             sums,
+            product,
+            product,
         ],
         compiler_params=pltpu.CompilerParams(vmem_limit_bytes=VMEM_BYTES),
         cost_estimate=pl.CostEstimate(
@@ -345,7 +306,7 @@
     rank = pieces[0].shape[1] // 2
     count = len(pieces)
     width = rank * rank
-    columns = 256
+    columns = 512
     here = count * pieces[0].shape[0] * pieces[0].shape[2]
     first = before is None
     tile = pl.BlockSpec((rows, 2 * columns), lambda step: (0, step))
@@ -371,7 +332,7 @@
             bytes_accessed=(1 if first else 2) * 4 * rows * width,
             transcendentals=0,
         ),
-        name="hessian_begin" if first else "hessian_end" if last else "hessian_more",
+        name="hessian_first" if first else "hessian_rest",
     )(place, apart, *pieces, *([] if first else [before]))
 
 
@@ -386,10 +347,10 @@
     tokens = tok_dev * dp_size
 
     operands = (place, layer_input, out_grads[0], proj_in[0].T, proj_out[0].T, parts)
-    (sent,) = project(*operands)
-    sent = swap(sent, "tensor", parts, 1)
-    total, cut = project(*operands, queries[0], owners)
-    total = total + decode(sent)
+    sent = swap(project(*operands, True), "tensor", parts, 1)
+    total = project(*operands, False) + decode(sent)
+    rows, total = lax.optimization_barrier((queries[0], total))
+    cut = split_queries(rows, owners, rank)
     offset = 2
     while 2 * offset < parts:
         half = total.shape[0] // 2
@@ -409,11 +370,7 @@
     far = [swap(piece, "dp", dp_size, k) for k in range(1, dp_size) for piece in near]
     where = [(k, part) for k in range(dp_size) for ks in at for part in ks]
 
-    def rows(pieces, begun, last):
-        return hessian_rows(place, apart, dp_size, pieces, tokens, owned, begun, last)
-
-    begun = rows(near[:1], None, False)
-    begun = rows(near[1:], begun, not far)
+    begun = hessian_rows(place, apart, dp_size, near, tokens, owned, None, not far)
     begun, columns, *far = lax.optimization_barrier((begun, columns, *far))
     examples = tokens // LEN
     devices = owners * pipe_size
@@ -423,7 +380,7 @@
     shares = lax.all_to_all(shares, ("tensor", "dp", "pipe"), 0, 0, tiled=True)
     scores = jnp.sum(shares, axis=0)
     if far:
-        begun = rows(far, begun, True)
+        begun = hessian_rows(place, apart, dp_size, far, tokens, owned, begun, True)
     return (begun[None], scores)
 
 

time: 122 us -> 107 us (0.88)
  Pallas kernels: 86.3 us -> 71.9 us
    pallas_call x3 -> x2, Pallas kernels: 34.7 us -> 26.3 us  [hessian_rows(): pl.pallas_call(functools.partial(hessian_kernel, tokens, count, dp_size,...]
    pallas_call x1, Pallas kernels: 33.7 us -> 29.7 us  [solve(): pl.pallas_call(functools.partial(solve_kernel, tokens, count, (where, par...]
    pallas_call x2 -> x3, Pallas kernels: 17.9 us -> 15.9 us  [the longest x2 13.7 us: project(): pl.pallas_call(functools.partial(project_kernel, sent), grid_spec=pltpu.P...]
    add x0 -> x1, other arithmetic: none -> 1.27 us  [shards(): total = project(*operands, False) + decode(sent)]
    convert_element_type x1, other arithmetic: 1.31 us -> 0.05 us  [encode(): return (value * jnp.abs(value)).astype(jnp.bfloat16)]
  transfers between devices with their start and end apart: 7 -> 7, of which waited for: 1 -> 2; matrix products, arithmetic and copies ran while one was open for 0% -> 0% of each run, Pallas kernels for 37% -> 33%
where the time goes in v5:
time: 107 us
  Pallas kernels  71.9 us (67%)
  starting transfers between devices  18.4 us (17%)
  waiting for transfers between devices  11.9 us (11%)
  other arithmetic  2.26 us (2%)
  local copies, waits for them, and re-layouts  1.47 us (1%)
    pallas_call x1, Pallas kernels, solve(): pl.pallas_call(functools.partial(solve_kernel, tokens, count, (where, par...  29.7 us
    pallas_call x2, Pallas kernels, hessian_rows(): pl.pallas_call(functools.partial(hessian_kernel, tokens, count, dp_size,...  26.3 us
    pallas_call x2, Pallas kernels, project(): pl.pallas_call(functools.partial(project_kernel, sent), grid_spec=pltpu.P...  13.7 us
    ppermute x5, waiting for transfers between devices, swap(): return lax.ppermute(value, axes, [(i, i ^ offset) for i in range(size)])  11.9 us
    ppermute x5, starting transfers between devices, swap(): return lax.ppermute(value, axes, [(i, i ^ offset) for i in range(size)])  9.16 us
    all_to_all x1, starting transfers between devices, shards(): shares = lax.all_to_all(shares, ('tensor', 'dp', 'pipe'), 0, 0, tiled=True)  4.68 us
    all_to_all x1, starting transfers between devices, shards(): columns = lax.all_to_all(cut, ('tensor', 'dp'), 0, 0, tiled=True)  4.58 us
    pallas_call x1, Pallas kernels, split_queries(): pl.pallas_call(split_queries_kernel, out_shape=jax.ShapeDtypeStruct(shape...  2.18 us
  transfers between devices with their start and end apart: 7, of which 2 were waited for; matrix products, arithmetic and copies ran while one was open for 0% of the time, Pallas kernels for 33%

profile of v5, /device:TPU:0, one launch (start us, length us, event | category | flops | bytes accessed | tf_op | source)
XLA Modules:
  0.0 106.7 jit_solution(6451082048156946541)
XLA Ops:
  0.6 6.9 %project_sent.1 = bf16[2,128,512]{2,1,0:T(8,128)(2,1)} custom-call(s32[1]{0:T(128)} %bitcast.place, bf16[2048,1024]{1,0:T(8,128)(2,1)} %inputs.3, bf16[2048,3584]{1,0:T(8,128)(2,1)} %bitcast.11, bf16[64,1024]{1,0:T(8,128)(2,1)} %bitcast.15, bf16[64,3584]{1,0:T(8,128)(2,1)} %bitcast.13), custom_call_target="tpu_custom_call" | custom-call | flops 603979776 | bytes 9437184 | tf_op jit(solution)/shard_map/project_sent/pallas_call | solution.py:65
  7.5 3.0 %collective-permute-start = (bf16[2,128,512]{2,1,0:T(8,128)(2,1)}, bf16[2,128,512]{2,1,0:T(8,128)(2,1)S(1)}, u32[]{:S(2)}, u32[]{:S(2)}) collective-permute-start(bf16[2,128,512]{2,1,0:T(8,128)(2,1)} %project_sent.1), channel_id=1, source_target_pairs={{0,4},{4,0},{8,12},{12,8},{1,5},{5,1},{9,13},{13,9},{2,6},{6,2},{1... | collective-permute-start | bytes 786440 | tf_op jit(solution)/shard_map/ppermute | solution.py:23
  10.5 6.9 %project_kept.1 = f32[2,128,512]{2,1,0:T(8,128)} custom-call(s32[1]{0:T(128)} %bitcast.place, bf16[2048,1024]{1,0:T(8,128)(2,1)} %inputs.3, bf16[2048,3584]{1,0:T(8,128)(2,1)} %bitcast.12, bf16[64,1024]{1,0:T(8,128)(2,1)} %bitcast.16, bf16[64,3584]{1,0:T(8,128)(2,1)} %bitcast.14), custom_call_target="tpu_custom_call" | custom-call | flops 603979776 | bytes 9437184 | tf_op jit(solution)/shard_map/project_kept/pallas_call | solution.py:65
  17.4 0.0 collective-permute-done
  17.4 1.3 %fusion.2 = f32[2,128,512]{2,1,0:T(8,128)S(1)} fusion(f32[2,128,512]{2,1,0:T(8,128)} %project_kept.1, bf16[2,128,512]{2,1,0:T(8,128)(2,1)S(1)} %collective-permute-done), kind=kLoop, calls=%fused_computation.9 | loop fusion | flops 786432 | bytes 1310720 | tf_op jit(solution)/shard_map/add | solution.py:351
  18.7 0.1 fusion.3
  18.7 2.6 %collective-permute-start.1 = (bf16[2,128,512]{2,1,0:T(8,128)(2,1)S(1)}, bf16[2,128,512]{2,1,0:T(8,128)(2,1)S(1)}, u32[]{:S(2)}, u32[]{:S(2)}) collective-permute-start(bf16[2,128,512]{2,1,0:T(8,128)(2,1)S(1)} %fusion.3), channel_id=1, source_target_pairs={{0,8},{4,12},{8,0},{12,4},{1,9},{5,13},{9,1},{13,5},{2,10},{6,14},... | collective-permute-start | bytes 786440 | tf_op jit(solution)/shard_map/ppermute | solution.py:23
  21.4 2.2 %split_queries.1 = f32[8,64,128]{2,1,0:T(8,128)} custom-call(f32[512,128]{1,0:T(8,128)} %bitcast.17), custom_call_target="tpu_custom_call" | custom-call | tf_op jit(solution)/shard_map/split_queries/pallas_call | solution.py:105
  23.6 9.5 %collective-permute-done.1 = bf16[2,128,512]{2,1,0:T(8,128)(2,1)S(1)} collective-permute-done((bf16[2,128,512]{2,1,0:T(8,128)(2,1)S(1)}, bf16[2,128,512]{2,1,0:T(8,128)(2,1)S(1)}, u32[]{:S(2)}, u32[]{:S(2)}) %collective-permute-start.1) | collective-permute-done | bytes 262176 | tf_op jit(solution)/shard_map/ppermute | solution.py:23
  33.1 0.2 negate_select_fusion
  33.3 0.1 fusion.5
  33.4 0.0 copy-start
  33.4 0.1 collective-permute-start.2
  33.5 1.6 %collective-permute-start.3 = (bf16[2,128,512]{2,1,0:T(8,128)(2,1)S(1)}, bf16[2,128,512]{2,1,0:T(8,128)(2,1)S(1)}, u32[]{:S(2)}, u32[]{:S(2)}) collective-permute-start(bf16[2,128,512]{2,1,0:T(8,128)(2,1)S(1)} %pad_maximum_fusion.refs_0_), channel_id=1, source_target_pairs={{0,2},{2,0},{1,3},{3,1},{4,6},{6,4},{5,7},{7,5},{8,10},{10,8},{9,1... | collective-permute-start | bytes 786440 | tf_op jit(solution)/shard_map/ppermute | solution.py:23
  35.1 4.6 %all-to-all-start = ((f32[8,64,128]{2,1,0:T(8,128)}), f32[8,64,128]{2,1,0:T(8,128)S(1)}, u32[]{:S(2)}, u32[]{:S(2)}) async-start(f32[8,64,128]{2,1,0:T(8,128)} %split_queries.1), calls=%async_computation | async-start | bytes 524288 | tf_op jit(solution)/shard_map/all_to_all | solution.py:363
  39.7 2.4 %collective-permute-done.2.refs_1_ = bf16[2,128,512]{2,1,0:T(8,128)(2,1)S(1)} collective-permute-done((bf16[2,128,512]{2,1,0:T(8,128)(2,1)S(1)}, bf16[2,128,512]{2,1,0:T(8,128)(2,1)S(1)}, u32[]{:S(2)}, u32[]{:S(2)}) %collective-permute-start.2) | collective-permute-done | bytes 262176 | tf_op jit(solution)/shard_map/ppermute | solution.py:23
  42.0 0.0 copy-start.2
  42.0 1.9 %collective-permute-start.4 = (bf16[2,128,512]{2,1,0:T(8,128)(2,1)S(1)}, bf16[2,128,512]{2,1,0:T(8,128)(2,1)S(1)}, u32[]{:S(2)}, u32[]{:S(2)}) collective-permute-start(bf16[2,128,512]{2,1,0:T(8,128)(2,1)S(1)} %collective-permute-done.2.refs_1_), channel_id=1, source_target_pairs={{0,2},{2,0},{1,3},{3,1},{4,6},{6,4},{5,7},{7,5},{8,10},{10,8},{9,1... | collective-permute-start | bytes 786440 | tf_op jit(solution)/shard_map/ppermute | solution.py:23
  43.9 0.0 copy-done
  43.9 0.0 copy-done.2
  43.9 12.7 %hessian_first.1.refs_2_ = f32[512,4096]{1,0:T(8,128)} custom-call(s32[1]{0:T(128)} %bitcast.place, s32[1]{0:T(128)} %bitcast.1.apart, bf16[2,128,512]{2,1,0:T(8,128)(2,1)} %copy-done, bf16[2,128,512]{2,1,0:T(8,128)(2,1)} %copy-done.2), custom_call_target="tpu_custom_call" | custom-call | flops 8589934592 | bytes 8388608 | tf_op jit(solution)/shard_map/hessian_first/pallas_call | solution.py:313
  56.6 0.0 collective-permute-done.3.refs_0_.refs_2_
  56.6 0.0 copy-start.3
  56.6 0.0 all-to-all-done.refs_4_
  56.6 0.0 copy-start.1
  56.6 0.0 collective-permute-done.4.refs_1_.refs_3_
  56.6 0.7 copy-done.3
  57.3 0.1 copy-done.1
  57.4 0.0 copy-start.4
  57.4 0.7 copy-done.4
  58.1 29.7 %solve.1 = f32[16,4,128]{2,1,0:T(4,128)} custom-call(s32[1]{0:T(128)} %bitcast.place, s32[1]{0:T(128)} %bitcast.1.apart, bf16[2,128,512]{2,1,0:T(8,128)(2,1)} %copy-done, bf16[2,128,512]{2,1,0:T(8,128)(2,1)} %copy-done.2, bf16[2,128,512]{2,1,0:T(8,128)(2,1)} %copy-done.3, bf16[2,128,512]{2,1,0:T(8,128)(2,1)} %copy-done.4, f32[8,64,128]{2,1,0:T(8,128)} %copy-done.1), custom_call_target="tpu_custom_call" | custom-call | flops 25769803776 | bytes 1048576 | tf_op jit(solution)/shard_map/solve/pallas_call | solution.py:231
  87.8 4.7 %all-to-all-start.1 = ((f32[16,4,128]{2,1,0:T(4,128)}), f32[16,4,128]{2,1,0:T(4,128)S(1)}, u32[]{:S(2)}, u32[]{:S(2)}) async-start(f32[16,4,128]{2,1,0:T(4,128)} %solve.1), calls=%async_computation.1 | async-start | bytes 65536 | tf_op jit(solution)/shard_map/all_to_all | solution.py:380
  92.5 13.6 %hessian_rest.1 = f32[512,4096]{1,0:T(8,128)} custom-call(s32[1]{0:T(128)} %bitcast.place, s32[1]{0:T(128)} %bitcast.1.apart, bf16[2,128,512]{2,1,0:T(8,128)(2,1)} %copy-done.3, bf16[2,128,512]{2,1,0:T(8,128)(2,1)} %copy-done.4, f32[512,4096]{1,0:T(8,128)} %hessian_first.1.refs_2_), custom_call_target="tpu_custom_call", output_to_operand_aliasing={{}: (4, {})} | custom-call | flops 8589934592 | bytes 16777216 | tf_op jit(solution)/shard_map/hessian_rest/pallas_call | solution.py:313
  106.1 0.0 all-to-all-done.1
  106.1 0.6 reduce_sum.9
  (1 shorter events, 0.0 us)
Async XLA Ops:
  7.5 9.9 %collective-permute-start = (bf16[2,128,512]{2,1,0:T(8,128)(2,1)}, bf16[2,128,512]{2,1,0:T(8,128)(2,1)S(1)}, u32[]{:S(2)}, u32[]{:S(2)}) collective-permute-start(bf16[2,128,512]{2,1,0:T(8,128)(2,1)} %project_sent.1), channel_id=1, source_target_pairs={{0,4},{4,0},{8,12},{12,8},{1,5},{5,1},{9,13},{13,9},{2,6},{6,2},{1... | collective-permute-start | bytes 786440 | tf_op jit(solution)/shard_map/ppermute | solution.py:23
  18.7 14.4 %collective-permute-start.1 = (bf16[2,128,512]{2,1,0:T(8,128)(2,1)S(1)}, bf16[2,128,512]{2,1,0:T(8,128)(2,1)S(1)}, u32[]{:S(2)}, u32[]{:S(2)}) collective-permute-start(bf16[2,128,512]{2,1,0:T(8,128)(2,1)S(1)} %fusion.3), channel_id=1, source_target_pairs={{0,8},{4,12},{8,0},{12,4},{1,9},{5,13},{9,1},{13,5},{2,10},{6,14},... | collective-permute-start | bytes 786440 | tf_op jit(solution)/shard_map/ppermute | solution.py:23
  33.4 10.5 %copy-start = (bf16[2,128,512]{2,1,0:T(8,128)(2,1)}, bf16[2,128,512]{2,1,0:T(8,128)(2,1)S(1)}, u32[]{:S(2)}) copy-start(bf16[2,128,512]{2,1,0:T(8,128)(2,1)S(1)} %pad_maximum_fusion.refs_0_) | copy-start | bytes 786436
  33.4 8.6 %collective-permute-start.2 = (bf16[2,128,512]{2,1,0:T(8,128)(2,1)S(1)}, bf16[2,128,512]{2,1,0:T(8,128)(2,1)S(1)}, u32[]{:S(2)}, u32[]{:S(2)}) collective-permute-start(bf16[2,128,512]{2,1,0:T(8,128)(2,1)S(1)} %pad_maximum_fusion.refs_0_), channel_id=1, source_target_pairs={{0,4},{4,0},{8,12},{12,8},{1,5},{5,1},{9,13},{13,9},{2,6},{6,2},{1... | collective-permute-start | bytes 786440 | tf_op jit(solution)/shard_map/ppermute | solution.py:23
  33.5 23.1 %collective-permute-start.3 = (bf16[2,128,512]{2,1,0:T(8,128)(2,1)S(1)}, bf16[2,128,512]{2,1,0:T(8,128)(2,1)S(1)}, u32[]{:S(2)}, u32[]{:S(2)}) collective-permute-start(bf16[2,128,512]{2,1,0:T(8,128)(2,1)S(1)} %pad_maximum_fusion.refs_0_), channel_id=1, source_target_pairs={{0,2},{2,0},{1,3},{3,1},{4,6},{6,4},{5,7},{7,5},{8,10},{10,8},{9,1... | collective-permute-start | bytes 786440 | tf_op jit(solution)/shard_map/ppermute | solution.py:23
  35.1 21.5 %all-to-all-start = ((f32[8,64,128]{2,1,0:T(8,128)}), f32[8,64,128]{2,1,0:T(8,128)S(1)}, u32[]{:S(2)}, u32[]{:S(2)}) async-start(f32[8,64,128]{2,1,0:T(8,128)} %split_queries.1), calls=%async_computation | async-start | bytes 524288 | tf_op jit(solution)/shard_map/all_to_all | solution.py:363
  42.0 1.9 %copy-start.2 = (bf16[2,128,512]{2,1,0:T(8,128)(2,1)}, bf16[2,128,512]{2,1,0:T(8,128)(2,1)S(1)}, u32[]{:S(2)}) copy-start(bf16[2,128,512]{2,1,0:T(8,128)(2,1)S(1)} %collective-permute-done.2.refs_1_) | copy-start | bytes 786436
  42.0 14.6 %collective-permute-start.4 = (bf16[2,128,512]{2,1,0:T(8,128)(2,1)S(1)}, bf16[2,128,512]{2,1,0:T(8,128)(2,1)S(1)}, u32[]{:S(2)}, u32[]{:S(2)}) collective-permute-start(bf16[2,128,512]{2,1,0:T(8,128)(2,1)S(1)} %collective-permute-done.2.refs_1_), channel_id=1, source_target_pairs={{0,2},{2,0},{1,3},{3,1},{4,6},{6,4},{5,7},{7,5},{8,10},{10,8},{9,1... | collective-permute-start | bytes 786440 | tf_op jit(solution)/shard_map/ppermute | solution.py:23
  56.6 0.7 copy-start.3
  56.6 0.8 copy-start.1
  57.4 0.7 copy-start.4
  87.8 18.3 %all-to-all-start.1 = ((f32[16,4,128]{2,1,0:T(4,128)}), f32[16,4,128]{2,1,0:T(4,128)S(1)}, u32[]{:S(2)}, u32[]{:S(2)}) async-start(f32[16,4,128]{2,1,0:T(4,128)} %solve.1), calls=%async_computation.1 | async-start | bytes 65536 | tf_op jit(solution)/shard_map/all_to_all | solution.py:380
